TPU v7x, 256 devices: a whole 4x4x8 slice. The times are simulated.
256 devices in a mesh: dp: 32 (over z_hi, y, core), tensor: 8 (over x, z_lo).
Axes of the slice: x: 4, y: 4, z: 8 (z_hi: 4, z_lo: 2; z = z_hi * 2 + z_lo), core: 2. Of those that a mesh axis runs over, the one named last changes fastest.
Arguments:
- tokens: bfloat16 [8192, 3072], P('dp'), may hold values from -6 to 6
- weights: bfloat16 [6, 512, 12288], P(None, 'dp', 'tensor'), may hold values from -0.109375 to 0.109375
- cotangent: bfloat16 [8192, 12288], P('dp', 'tensor'), may hold values from -6 to 6
Outputs:
- activated: bfloat16 [8192, 12288], P('dp', 'tensor')
- input_grad: bfloat16 [8192, 3072], P('dp', 'tensor')
- update: float32 [6, 512, 12288], P(None, 'dp', 'tensor')
All inputs are finite; a program needn't handle non-finite values.
Results may differ from a plain program's by a relative error of at most 0.02.
Values may be sent and summed in bfloat16 or wider, within the bound.
No kernel may reach another device: no remote copies, remote signals or barrier semaphores. Data moves between devices by JAX's collectives and lax.ppermute only.
A program may use at most 128 MiB of HBM per device.

v0:
```python
import jax
import jax.numpy as jnp
from jax import lax
from jax.experimental import pallas as pl
from jax.experimental.pallas import tpu as pltpu
from jax.sharding import PartitionSpec as P

S = 512
HALF = 256
NZ, NY, NC = 4, 4, 2
CHIPS = NZ * NY
LIMIT = 56 * 1024 * 1024


def params():
    return pltpu.CompilerParams(vmem_limit_bytes=LIMIT)


def dev(z, y, c):
    return ((z % NZ) * NY + y % NY) * NC + c % NC


def moved(array, pairs):
    return lax.ppermute(array, "dp", pairs)


def swap_cores(array):
    return moved(
        array,
        [(dev(z, y, c), dev(z, y, 1 - c)) for z in range(NZ) for y in range(NY) for c in range(NC)],
    )


def turn(place, core, step):
    return (1 if (place + core) % 2 == 0 else -1) * (1 if step == 1 else -1)


def exchange(array, axis, step):
    pairs = []
    for z in range(NZ):
        for y in range(NY):
            for c in range(NC):
                if axis == "y":
                    to = dev(z, y + turn(y, c, step), c)
                else:
                    to = dev(z + turn(z, c, step), y, c)
                pairs.append((dev(z, y, c), to))
    return moved(array, pairs)


def chips_of(pos_ref, large):
    y, z, core = pos_ref[0], pos_ref[1], pos_ref[2]
    sy = 1 - 2 * lax.rem(y + core, 2)
    sz = 1 - 2 * lax.rem(z + core, 2)
    ys = [lax.rem(y + step + NY, NY) for step in (0, sy, -sy, 2)]
    zs = [lax.rem(z + step + NZ, NZ) for step in (0, sz, -sz, 2)]
    if large == "y":
        return [[zz * NY + yy for zz in zs] for yy in ys]
    return [[zz * NY + yy for yy in ys] for zz in zs]


def chunk_kernel(large, scale, pos, tok, tok_t, cot0, cot1, near, far, *refs):
    w_ref, act0, act1, slope_ref = refs[:4]
    grads, stage = refs[4:-1], refs[-1]
    rows, wide = w_ref.shape[0], w_ref.shape[3]
    half = tok.shape[0] // 2
    chips = chips_of(pos, large)
    for i in range(4):
        for k in range(4):
            w_ref[:, chips[i][k]] = (near if i < 2 else far)[i % 2, k]
    w = w_ref[...].reshape(rows * S, wide)
    v = jnp.dot(tok[...], w, preferred_element_type=jnp.float32)
    coeff = 0.7978845608
    square = v * v
    t = jnp.tanh(coeff * (v + 0.044715 * square * v))
    value = 0.5 * v * (1.0 + t)
    deriv = 0.5 * (1.0 + t) + 0.5 * v * (1.0 - t * t) * coeff * (1.0 + 3.0 * 0.044715 * square)
    act0[...] = value[:half].astype(jnp.bfloat16)
    act1[...] = value[half:].astype(jnp.bfloat16)
    slope_ref[:half] = (cot0[...].astype(jnp.float32) * deriv[:half]).astype(jnp.bfloat16)
    slope_ref[half:] = (cot1[...].astype(jnp.float32) * deriv[half:]).astype(jnp.bfloat16)
    for b in range(rows):
        g = jnp.dot(tok_t[b * S : (b + 1) * S], slope_ref[...], preferred_element_type=jnp.float32)
        g = (g * scale).astype(jnp.bfloat16)
        for j in range(wide // HALF):
            stage[j * rows + b] = g[:, j * HALF : (j + 1) * HALF]
    y, z, core = pos[0], pos[1], pos[2]
    if large == "y":
        sy = 1 - 2 * lax.rem(y + core, 2)
        keep0, keep1, send = grads
        for ref, lo, step in ((keep0, 0, 0), (keep1, 0, sy), (send, 0, -sy), (send, 3, 2)):
            place = lax.rem(y + step + NY, NY)
            for m in range(3):
                ref[lo + m] = stage[3 * place + m]
    else:
        sz = 1 - 2 * lax.rem(z + core, 2)
        keep, send = grads
        other = lax.rem(z + sz + NZ, NZ)
        odd = lax.rem(z, 2)
        even_place = jnp.where(odd == 0, z, other)
        odd_place = jnp.where(odd == 0, other, z)
        for ref, step in ((keep, 0), (send, 2)):
            e = lax.div(lax.rem(even_place + step, NZ), 2) * 3
            o = lax.div(lax.rem(odd_place + step, NZ), 2) * 3 + 2
            ref[0] = stage[e]
            ref[1] = stage[e + 1]
            ref[2] = stage[o]


def chunk(large, scale, pos, tok, tok_t, cot0, cot1, near, far):
    tokens = tok.shape[0]
    rows, wide = near.shape[2], near.shape[4]
    blocks = rows * wide // HALF
    shape = lambda *dims: jax.ShapeDtypeStruct(dims, jnp.bfloat16)
    vmem = pl.BlockSpec(memory_space=pltpu.VMEM)
    outs = [
        shape(rows, CHIPS, S // CHIPS, wide),
        shape(tokens // 2, wide),
        shape(tokens // 2, wide),
        shape(tokens, wide),
    ] + [shape(n, S, HALF) for n in ((3, 3, 6) if large == "y" else (3, 3))]
    return pl.pallas_call(
        lambda *refs: chunk_kernel(large, scale, *refs),
        out_shape=outs,
        in_specs=[pl.BlockSpec(memory_space=pltpu.SMEM)] + [vmem] * 6,
        out_specs=[vmem] * len(outs),
        scratch_shapes=[pltpu.VMEM((blocks, S, HALF), jnp.bfloat16)],
        compiler_params=params(),
        cost_estimate=pl.CostEstimate(
            flops=4 * tokens * rows * S * wide,
            bytes_accessed=4 * tokens * rows * S,
            transcendentals=tokens * wide,
        ),
    )(pos, tok, tok_t, cot0, cot1, near, far)


def fold_kernel(pos, keep, got, got2, zkeep, zsend):
    z, core = pos[1], pos[2]
    sz = 1 - 2 * lax.rem(z + core, 2)
    for ref, index, step in ((zsend, 0, -sz), (zsend, 1, 2), (zkeep, 0, 0), (zkeep, 1, sz)):
        m = jnp.minimum(lax.rem(z + step + NZ, NZ), 2)
        total = (
            keep[m].astype(jnp.float32)
            + got[m].astype(jnp.float32)
            + got2[m].astype(jnp.float32)
        )
        ref[index] = total.astype(ref.dtype)


def fold(pos, keep, got, got2):
    vmem = pl.BlockSpec(memory_space=pltpu.VMEM)
    return pl.pallas_call(
        fold_kernel,
        out_shape=[
            jax.ShapeDtypeStruct((2, S, HALF), jnp.float32),
            jax.ShapeDtypeStruct((2, S, HALF), jnp.bfloat16),
        ],
        grid=(1,),
        in_specs=[
            pl.BlockSpec(memory_space=pltpu.SMEM),
            pl.BlockSpec((3, S, HALF), lambda i: (0, 0, 0)),
            pl.BlockSpec((3, S, HALF), lambda i: (0, 0, 0)),
            pl.BlockSpec((3, S, HALF), lambda i: (0, 0, 0)),
        ],
        out_specs=[vmem, vmem],
        compiler_params=params(),
        cost_estimate=pl.CostEstimate(flops=S * S * 8, bytes_accessed=8 * S * S, transcendentals=0),
    )(pos, keep, got, got2)


def input_kernel(*refs):
    count = (len(refs) - 2) // 2
    slopes, weights, own, other = refs[:count], refs[count : 2 * count], refs[-2], refs[-1]
    half, width = own.shape[1], own.shape[2]
    rows = weights[0].shape[0]
    for b in range(rows):
        term = 0.0
        for slope, weight in zip(slopes, weights):
            term = term + lax.dot_general(
                slope[...],
                weight[b].reshape(S, weight.shape[3]),
                (((1,), (1,)), ((), ())),
                preferred_element_type=jnp.float32,
            )
        term = term.astype(jnp.bfloat16)
        at = b * S
        while at < (b + 1) * S:
            part, inside = at // width, at % width
            take = min(width - inside, (b + 1) * S - at)
            lo = at - b * S
            own[part, :, inside : inside + take] = term[:half, lo : lo + take]
            other[part, :, inside : inside + take] = term[half:, lo : lo + take]
            at += take


def input_partials(parts, slopes, weights):
    tokens = slopes[0].shape[0]
    rows = weights[0].shape[0]
    wide = sum(slope.shape[1] for slope in slopes)
    vmem = pl.BlockSpec(memory_space=pltpu.VMEM)
    out = jax.ShapeDtypeStruct((parts, tokens // 2, rows * S // parts), jnp.bfloat16)
    return pl.pallas_call(
        input_kernel,
        out_shape=[out, out],
        in_specs=[vmem] * (2 * len(slopes)),
        out_specs=[vmem] * 2,
        compiler_params=params(),
        cost_estimate=pl.CostEstimate(
            flops=2 * tokens * rows * S * wide,
            bytes_accessed=2 * tokens * rows * S + 2 * rows * S * wide,
            transcendentals=0,
        ),
    )(*slopes, *weights)


def owners():
    table = {}
    for y in range(NY):
        for m in range(3):
            table[3 * (y % 2) + m, y // 2] = dev(m, y, 0)
    for z in range(NZ):
        for index, y in enumerate((0, 2) if z % 2 == 0 else (0,)):
            table[3 * (z // 2) + index + 2 * (z % 2), 2] = dev(z, y, 1)
    return table


def newton_kernel(g0_ref, g1_ref, out_ref):
    def mm(a, b):
        return jnp.dot(
            a.astype(jnp.bfloat16), b.astype(jnp.bfloat16), preferred_element_type=jnp.float32
        )

    g = jnp.concatenate([g0_ref[...], g1_ref[...]], axis=1)
    gf = g.astype(jnp.float32)
    left = lax.dot_general(g, g, (((1,), (1,)), ((), ())), preferred_element_type=jnp.float32)
    trace = jnp.sum(gf * gf, axis=(0, 1), keepdims=True)
    diagonal = lax.broadcasted_iota(jnp.int32, (S, S), 0) == lax.broadcasted_iota(
        jnp.int32, (S, S), 1
    )
    damped = left + jnp.where(diagonal, 0.1 * trace / S + 1e-06, 0.0)
    norm = jnp.sum(damped * damped, axis=(0, 1), keepdims=True)
    scale = 5.0 / (2.0 * jnp.sqrt(norm))
    m = damped * scale
    sq = mm(m, m)
    n = (10.0 * m - sq) * 0.0625
    km = (5.0 * m - sq) * 0.25
    u = 2.44140625 * km - mm(3.125 * n - mm(n, n), km)
    v = (1.25 * m + u) * 0.25
    h = 3.125 * v - mm(v, v)
    factor = (float(S) ** 0.5) * jnp.sqrt(scale)
    result = (2.44140625 * gf - mm(h, g)) * factor
    out_ref[...] = result.astype(jnp.bfloat16).reshape(out_ref.shape)


def newton(g0, g1):
    vmem = pl.BlockSpec(memory_space=pltpu.VMEM)
    count = CHIPS * NC
    return pl.pallas_call(
        newton_kernel,
        out_shape=jax.ShapeDtypeStruct((count, S // count, S), jnp.bfloat16),
        in_specs=[vmem, vmem],
        out_specs=vmem,
        compiler_params=params(),
    )(g0, g1)


def place_kernel(in_ref, out_ref):
    for (b, j), owner in owners().items():
        out_ref[b, :, j * S : (j + 1) * S] = in_ref[owner].astype(jnp.float32)


def place(rows, cols, arrived):
    vmem = pl.BlockSpec(memory_space=pltpu.VMEM)
    return pl.pallas_call(
        place_kernel,
        out_shape=jax.ShapeDtypeStruct((rows, arrived.shape[1], cols * S), jnp.float32),
        in_specs=[vmem],
        out_specs=vmem,
        compiler_params=params(),
    )(arrived)


def local(tokens, weights, cotangent):
    rows, local_rows, width = weights.shape
    cols = width // S
    tok_local = tokens.shape[0]
    scale = 1.0 / (tok_local * lax.axis_size("dp"))
    parts = lax.axis_size("tensor")
    here = lax.axis_index("dp")
    core = here % NC
    first = core == 0
    pos = jnp.stack([(here // NC) % NY, here // (NC * NY), core]).astype(jnp.int32)
    wide32 = lambda array: array.astype(jnp.float32)

    def split(array):
        pairs = [
            (array[..., j * S : j * S + HALF], array[..., j * S + HALF : (j + 1) * S])
            for j in range(cols)
        ]
        mine = jnp.concatenate([jnp.where(first, a, b) for a, b in pairs], axis=-1)
        theirs = jnp.concatenate([jnp.where(first, b, a) for a, b in pairs], axis=-1)
        return mine, theirs

    w_mine, w_theirs = split(weights)
    w_recv = swap_cores(w_theirs)
    shard = jnp.concatenate(
        [jnp.where(first, w_mine, w_recv), jnp.where(first, w_recv, w_mine)], axis=1
    )

    tok = jnp.concatenate([tokens, swap_cores(tokens)], axis=0)
    c_mine, c_theirs = split(cotangent)
    c_recv = swap_cores(c_theirs)
    tok_t = tok.T

    plan = [("z", "y", 0, (cols - 1) * HALF), ("y", "z", (cols - 1) * HALF, cols * HALF)]

    together = lax.optimization_barrier
    ones = [shard[..., lo:hi] for small, large, lo, hi in plan]
    twos = together(
        tuple(
            jnp.stack([one, got])
            for one, got in zip(
                ones, together(tuple(exchange(x, p[0], 1) for x, p in zip(ones, plan)))
            )
        )
    )
    fours = together(
        tuple(
            jnp.concatenate([two, got])
            for two, got in zip(
                twos, together(tuple(exchange(x, p[0], 2) for x, p in zip(twos, plan)))
            )
        )
    )
    nears = together(
        tuple(
            jnp.stack([four, got])
            for four, got in zip(
                fours, together(tuple(exchange(x, p[1], 1) for x, p in zip(fours, plan)))
            )
        )
    )
    fars = together(tuple(exchange(x, p[1], 2) for x, p in zip(nears, plan)))

    w_full, acts, slopes, grads = [], [], [], []
    after = None
    for (small, large, lo, hi), near, far in zip(plan, nears, fars):
        if after is not None:
            far, after = together((far, after))
        w, act0, act1, slope, *grad = chunk(
            large, scale, pos, tok, tok_t, c_mine[:, lo:hi], c_recv[:, lo:hi], near, far
        )
        after = slope
        w_full.append(w)
        acts.append((act0, act1))
        slopes.append(slope)
        grads.append(grad)

    cast = lambda array: array.astype(jnp.bfloat16)
    (keep0, keep1, send), (q_keep, q_send) = grads
    got = exchange(send, "y", 2)
    got2 = exchange(cast(wide32(keep1) + wide32(got[3:])), "y", 1)
    z_keep, z_send = fold(pos, keep0, got, got2)
    got3 = exchange(z_send, "z", 2)
    got4 = exchange(cast(z_keep[1] + wide32(got3[1])), "z", 1)
    p_block = cast(z_keep[0] + wide32(got3[0]) + wide32(got4))

    z_even = pos[1] % 2 == 0
    q_got = exchange(q_send, "z", 2)
    q_sum = wide32(q_keep) + wide32(q_got)
    q_pair, q_last = q_sum[:2], jnp.stack([q_sum[2], q_sum[2]])
    q_got2 = exchange(cast(jnp.where(z_even, q_last, q_pair)), "z", 1)
    q_two = jnp.where(z_even, q_pair, q_last) + wide32(q_got2)
    y, turned = pos[0], 1 - 2 * ((pos[0] + core) % 2)
    y_even = jnp.where(y % 2 == 0, y, (y + turned + NY) % NY)
    q_mine = jnp.where(y_even == 0, q_two[0], q_two[1])
    q_got3 = exchange(cast(jnp.where(y_even == 0, q_two[1], q_two[0])), "y", 2)
    q_half = cast(q_mine + wide32(q_got3))
    q_block = cast(wide32(q_half) + wide32(exchange(q_half, "y", 1)))

    act_mine = jnp.concatenate([a[0] for a in acts], axis=1)
    act_recv = swap_cores(jnp.concatenate([a[1] for a in acts], axis=1))
    columns = []
    for j in range(cols):
        at = slice(j * HALF, (j + 1) * HALF)
        columns.append(jnp.where(first, act_mine[:, at], act_recv[:, at]))
        columns.append(jnp.where(first, act_recv[:, at], act_mine[:, at]))
    activated = jnp.concatenate(columns, axis=1)

    ig_own, ig_other = input_partials(parts, slopes, w_full)
    ig_sum = (wide32(ig_own) + wide32(swap_cores(ig_other))).astype(jnp.bfloat16)
    input_grad = lax.psum_scatter(ig_sum, "tensor", scatter_dimension=0, tiled=False)

    recv = swap_cores(jnp.where(first, q_block, p_block))
    result = newton(jnp.where(first, p_block, recv), jnp.where(first, recv, q_block))
    arrived = lax.all_to_all(result, "dp", 0, 0, tiled=True)
    update = place(rows, cols, arrived)
    return (activated, input_grad, update)


def solution(mesh):
    return jax.shard_map(
        local,
        mesh=mesh,
        in_specs=(P("dp", None), P(None, "dp", "tensor"), P("dp", "tensor")),
        out_specs=(P("dp", "tensor"), P("dp", "tensor"), P(None, "dp", "tensor")),
        check_vma=False,
    )
```

profile of v0, /device:TPU:1, one launch (start us, length us, event | category | flops | bytes accessed | tf_op | source)
XLA Modules:
  0.0 228.4 jit_solution(13158227785377750359)
XLA Ops:
  8.2 3.3 %collective-permute-start.2 = (bf16[6,16,768]{2,1,0:T(8,128)(2,1)S(1)}, bf16[6,16,768]{2,1,0:T(8,128)(2,1)S(1)}, u32[]{:S(2)}, u32[]{:S(2)}) collective-permute-start(bf16[6,16,768]{2,1,0:T(8,128)(2,1)S(1)} %pad_maximum_fusion.12), channel_id=1, source_target_pairs={{0,8},{8,0},{16,24},{24,16},{32,40},{40,32},{48,56},{56,48},{64,72... | collective-permute-start | bytes 442376 | tf_op jit(solution)/shard_map/ppermute | solution.py:24
  12.6 4.4 %collective-permute-start.3 = (bf16[6,32,512]{2,1,0:T(8,128)(2,1)S(1)}, bf16[6,32,512]{2,1,0:T(8,128)(2,1)S(1)}, u32[]{:S(2)}, u32[]{:S(2)}) collective-permute-start(bf16[6,32,512]{2,1,0:T(8,128)(2,1)S(1)} %fusion.8), channel_id=1, source_target_pairs={{0,64},{8,200},{16,80},{24,216},{32,96},{40,232},{48,112},{56,248}... | collective-permute-start | bytes 589832 | tf_op jit(solution)/shard_map/ppermute | solution.py:24
  24.8 3.5 %collective-permute-done.6 = bf16[2,6,32,256]{3,2,1,0:T(8,128)(2,1)S(1)} collective-permute-done((bf16[2,6,32,256]{3,2,1,0:T(8,128)(2,1)S(1)}, bf16[2,6,32,256]{3,2,1,0:T(8,128)(2,1)S(1)}, u32[]{:S(2)}, u32[]{:S(2)}) %collective-permute-start.6) | collective-permute-done | bytes 196640 | tf_op jit(solution)/shard_map/ppermute | solution.py:24
  28.3 5.5 %collective-permute-done.5 = bf16[2,6,32,512]{3,2,1,0:T(8,128)(2,1)S(1)} collective-permute-done((bf16[2,6,32,512]{3,2,1,0:T(8,128)(2,1)S(1)}, bf16[2,6,32,512]{3,2,1,0:T(8,128)(2,1)S(1)}, u32[]{:S(2)}, u32[]{:S(2)}) %collective-permute-start.5) | collective-permute-done | bytes 393248 | tf_op jit(solution)/shard_map/ppermute | solution.py:24
  33.9 3.0 %collective-permute-start.7 = (bf16[4,6,32,512]{3,2,1,0:T(8,128)(2,1)S(1)}, bf16[4,6,32,512]{3,2,1,0:T(8,128)(2,1)S(1)}, u32[]{:S(2)}, u32[]{:S(2)}) collective-permute-start(bf16[4,6,32,512]{3,2,1,0:T(8,128)(2,1)S(1)} %pad_maximum_fusion.3), channel_id=1, source_target_pairs={{0,16},{8,56},{16,0},{24,40},{32,48},{40,24},{48,32},{56,8},{64,80... | collective-permute-start | bytes 2359304 | tf_op jit(solution)/shard_map/ppermute | solution.py:24
  36.9 4.0 %collective-permute-start.8 = (bf16[4,6,32,256]{3,2,1,0:T(8,128)(2,1)S(1)}, bf16[4,6,32,256]{3,2,1,0:T(8,128)(2,1)}, u32[]{:S(2)}, u32[]{:S(2)}) collective-permute-start(bf16[4,6,32,256]{3,2,1,0:T(8,128)(2,1)S(1)} %pad_maximum_fusion.7), channel_id=1, source_target_pairs={{0,64},{8,200},{16,80},{24,216},{32,96},{40,232},{48,112},{56,248}... | collective-permute-start | bytes 1179656 | tf_op jit(solution)/shard_map/ppermute | solution.py:24
  42.7 5.3 %collective-permute-done.8 = bf16[4,6,32,256]{3,2,1,0:T(8,128)(2,1)} collective-permute-done((bf16[4,6,32,256]{3,2,1,0:T(8,128)(2,1)S(1)}, bf16[4,6,32,256]{3,2,1,0:T(8,128)(2,1)}, u32[]{:S(2)}, u32[]{:S(2)}) %collective-permute-start.8) | collective-permute-done | bytes 393248 | tf_op jit(solution)/shard_map/ppermute | solution.py:24
  52.0 6.3 %collective-permute-start.1 = (bf16[256,768]{1,0:T(8,128)(2,1)S(1)}, bf16[256,768]{1,0:T(8,128)(2,1)S(1)}, u32[]{:S(2)}, u32[]{:S(2)}) collective-permute-start(bf16[256,768]{1,0:T(8,128)(2,1)S(1)} %pad_maximum_fusion.5), channel_id=1, source_target_pairs={{0,8},{8,0},{16,24},{24,16},{32,40},{40,32},{48,56},{56,48},{64,72... | collective-permute-start | bytes 1179656 | tf_op jit(solution)/shard_map/ppermute | solution.py:24
  62.3 3.9 %fusion.9 = (bf16[3072,512]{1,0:T(8,128)(2,1)}, bf16[512,3072]{0,1:T(8,128)(2,1)S(1)}) fusion(bf16[256,3072]{0,1:T(8,128)(2,1)} %collective-permute-done, bf16[256,3072]{0,1:T(8,128)(2,1)} %copy-done), kind=kLoop, calls=%fused_computation.57 | loop fusion | flops 6291456 | bytes 9437184 | tf_op jit(solution)/shard_map/transpose | solution.py:313
  66.2 3.1 %copy.8.refs_1_ = bf16[512,3072]{1,0:T(8,128)(2,1)} copy(bf16[512,3072]{0,1:T(8,128)(2,1)S(1)} %get-tuple-element.70) | data formatting | bytes 6291456 | tf_op jit(solution)/shard_map/concatenate | solution.py:310
  69.3 6.7 %collective-permute-done.10.refs_6_ = bf16[2,4,6,32,256]{4,3,2,1,0:T(8,128)(2,1)} collective-permute-done((bf16[2,4,6,32,256]{4,3,2,1,0:T(8,128)(2,1)}, bf16[2,4,6,32,256]{4,3,2,1,0:T(8,128)(2,1)}, u32[]{:S(2)}, u32[]{:S(2)}) %collective-permute-start.10) | collective-permute-done | bytes 786464 | tf_op jit(solution)/shard_map/ppermute | solution.py:24
  76.0 10.3 %shard_map.58 = (bf16[6,16,32,512]{3,2,1,0:T(8,128)(2,1)}, bf16[256,512]{1,0:T(8,128)(2,1)}, bf16[256,512]{1,0:T(8,128)(2,1)}, bf16[512,512]{1,0:T(8,128)(2,1)},...) custom-call(s32[3]{0:T(128)} %pad_add_fusion.refs_0_.pos, ...), custom_call_target="tpu_custom_call" | custom-call | flops 3221225472 | bytes 6291456 | tf_op jit(solution)/shard_map/pallas_call | solution.py:122
  87.7 8.3 %shard_map.59 = (bf16[6,16,32,256]{3,2,1,0:T(8,128)(2,1)}, bf16[256,256]{1,0:T(8,128)(2,1)}, bf16[256,256]{1,0:T(8,128)(2,1)}, bf16[512,256]{1,0:T(8,128)(2,1)},...) custom-call(s32[3]{0:T(128)} %pad_add_fusion.refs_0_.pos, bf16[512,3072]{1,0:T(8,128)(2,1)} %copy.8.refs_1_, ...), custom_call_target="tpu_custom_call" | custom-call | flops 1610612736 | bytes 6291456 | tf_op jit(solution)/shard_map/pallas_call | solution.py:122
  98.9 6.9 %shard_map.60 = (bf16[8,256,384]{2,1,0:T(8,128)(2,1)}, bf16[8,256,384]{2,1,0:T(8,128)(2,1)}) custom-call(bf16[512,512]{1,0:T(8,128)(2,1)} %get-tuple-element.51.refs_0_, bf16[512,256]{1,0:T(8,128)(2,1)} %get-tuple-element.55.refs_1_, bf16[6,16,32,512]{3,2,1,0:T(8,128)(2,1)} %get-tuple-element.56.refs_2_, bf16[6,16,32,256]{3,2,1,0:T(8,128)(2,1)} %get-tuple-element.57.refs_3_), custom_call_target="tpu_custom_call" | custom-call | flops 2415919104 | bytes 7864320 | tf_op jit(solution)/shard_map/pallas_call | solution.py:202
  105.7 4.6 %collective-permute-start.12 = (bf16[8,256,384]{2,1,0:T(8,128)(2,1)}, bf16[8,256,384]{2,1,0:T(8,128)(2,1)}, u32[]{:S(2)}, u32[]{:S(2)}) collective-permute-start(bf16[8,256,384]{2,1,0:T(8,128)(2,1)} %get-tuple-element.59), channel_id=1, source_target_pairs={{0,8},{8,0},{16,24},{24,16},{32,40},{40,32},{48,56},{56,48},{64,72... | collective-permute-start | bytes 4718600 | tf_op jit(solution)/shard_map/ppermute | solution.py:24
  110.7 8.7 %collective-permute-start.18 = (bf16[2,512,256]{2,1,0:T(8,128)(2,1)S(1)}, bf16[2,512,256]{2,1,0:T(8,128)(2,1)}, u32[]{:S(2)}, u32[]{:S(2)}) collective-permute-start(bf16[2,512,256]{2,1,0:T(8,128)(2,1)S(1)} %fusion.3), channel_id=1, source_target_pairs={{0,64},{8,200},{16,80},{24,216},{32,96},{40,232},{48,112},{56,248}... | collective-permute-start | bytes 1572872 | tf_op jit(solution)/shard_map/ppermute | solution.py:24
  122.3 10.2 %collective-permute-done.18 = bf16[2,512,256]{2,1,0:T(8,128)(2,1)} collective-permute-done((bf16[2,512,256]{2,1,0:T(8,128)(2,1)S(1)}, bf16[2,512,256]{2,1,0:T(8,128)(2,1)}, u32[]{:S(2)}, u32[]{:S(2)}) %collective-permute-start.18) | collective-permute-done | bytes 524320 | tf_op jit(solution)/shard_map/ppermute | solution.py:24
  141.8 5.2 %collective-permute-done.19 = bf16[512,256]{1,0:T(8,128)(2,1)S(1)} collective-permute-done((bf16[512,256]{1,0:T(8,128)(2,1)S(1)}, bf16[512,256]{1,0:T(8,128)(2,1)S(1)}, u32[]{:S(2)}, u32[]{:S(2)}) %collective-permute-start.19) | collective-permute-done | bytes 262176 | tf_op jit(solution)/shard_map/ppermute | solution.py:24
  149.5 5.2 %collective-permute-done.15 = bf16[2,512,256]{2,1,0:T(8,128)(2,1)S(1)} collective-permute-done((bf16[2,512,256]{2,1,0:T(8,128)(2,1)}, bf16[2,512,256]{2,1,0:T(8,128)(2,1)S(1)}, u32[]{:S(2)}, u32[]{:S(2)}) %collective-permute-start.15) | collective-permute-done | bytes 524320 | tf_op jit(solution)/shard_map/ppermute | solution.py:24
  155.6 20.4 %collective-permute-start.11 = (bf16[256,768]{1,0:T(8,128)(2,1)S(1)}, bf16[256,768]{1,0:T(8,128)(2,1)S(1)}, u32[]{:S(2)}, u32[]{:S(2)}) collective-permute-start(bf16[256,768]{1,0:T(8,128)(2,1)S(1)} %pad_maximum_fusion.8), channel_id=1, source_target_pairs={{0,8},{8,0},{16,24},{24,16},{32,40},{40,32},{48,56},{56,48},{64,72... | collective-permute-start | bytes 1179656 | tf_op jit(solution)/shard_map/ppermute | solution.py:24
  176.1 8.8 %collective-permute-start.21 = (bf16[512,256]{1,0:T(8,128)(2,1)S(1)}, bf16[512,256]{1,0:T(8,128)(2,1)S(1)}, u32[]{:S(2)}, u32[]{:S(2)}) collective-permute-start(bf16[512,256]{1,0:T(8,128)(2,1)S(1)} %get-tuple-element.67), channel_id=1, source_target_pairs={{0,8},{8,0},{16,24},{24,16},{32,40},{40,32},{48,56},{56,48},{64,72... | collective-permute-start | bytes 786440 | tf_op jit(solution)/shard_map/ppermute | solution.py:24
  187.0 4.6 %shard_map.62 = bf16[32,16,512]{2,1,0:T(8,128)(2,1)} custom-call(bf16[512,256]{1,0:T(8,128)(2,1)} %get-tuple-element.86.g0_ref, bf16[512,256]{1,0:T(8,128)(2,1)} %get-tuple-element.85.g1_ref), custom_call_target="tpu_custom_call" | custom-call | tf_op jit(solution)/shard_map/pallas_call | solution.py:258
  191.6 5.2 %all-to-all-start = ((bf16[32,16,512]{2,1,0:T(8,128)(2,1)}), bf16[32,16,512]{2,1,0:T(8,128)(2,1)S(1)}, u32[]{:S(2)}, u32[]{:S(2)}) async-start(bf16[32,16,512]{2,1,0:T(8,128)(2,1)} %shard_map.62), calls=%async_computation.1 | async-start | bytes 1048576 | tf_op jit(solution)/shard_map/all_to_all | solution.py:396
  197.1 21.8 %all-to-all-done.in_ref = bf16[32,16,512]{2,1,0:T(8,128)(2,1)S(1)} async-done(((bf16[32,16,512]{2,1,0:T(8,128)(2,1)}), bf16[32,16,512]{2,1,0:T(8,128)(2,1)S(1)}, u32[]{:S(2)}, u32[]{:S(2)}) %all-to-all-start) | async-done | bytes 524320 | tf_op jit(solution)/shard_map/all_to_all | solution.py:396
  (93 shorter events, 44.9 us)
Async XLA Ops:
  7.2 214.4 %reduce-scatter.2.cloned.1.call-start = ((), (), s32[]{:S(2)}) async-start(), calls=%async_computation.2 | async-start | bytes 1769472 | tf_op jit(solution)/shard_map/reduce_scatter | solution.py:392
  8.2 4.3 %collective-permute-start.2 = (bf16[6,16,768]{2,1,0:T(8,128)(2,1)S(1)}, bf16[6,16,768]{2,1,0:T(8,128)(2,1)S(1)}, u32[]{:S(2)}, u32[]{:S(2)}) collective-permute-start(bf16[6,16,768]{2,1,0:T(8,128)(2,1)S(1)} %pad_maximum_fusion.12), channel_id=1, source_target_pairs={{0,8},{8,0},{16,24},{24,16},{32,40},{40,32},{48,56},{56,48},{64,72... | collective-permute-start | bytes 442376 | tf_op jit(solution)/shard_map/ppermute | solution.py:24
  12.6 9.2 %collective-permute-start.3 = (bf16[6,32,512]{2,1,0:T(8,128)(2,1)S(1)}, bf16[6,32,512]{2,1,0:T(8,128)(2,1)S(1)}, u32[]{:S(2)}, u32[]{:S(2)}) collective-permute-start(bf16[6,32,512]{2,1,0:T(8,128)(2,1)S(1)} %fusion.8), channel_id=1, source_target_pairs={{0,64},{8,200},{16,80},{24,216},{32,96},{40,232},{48,112},{56,248}... | collective-permute-start | bytes 589832 | tf_op jit(solution)/shard_map/ppermute | solution.py:24
  17.0 4.8 %collective-permute-start.4 = (bf16[6,32,256]{2,1,0:T(8,128)(2,1)S(1)}, bf16[6,32,256]{2,1,0:T(8,128)(2,1)S(1)}, u32[]{:S(2)}, u32[]{:S(2)}) collective-permute-start(bf16[6,32,256]{2,1,0:T(8,128)(2,1)S(1)} %pad_maximum_fusion.13), channel_id=1, source_target_pairs={{0,16},{8,56},{16,0},{24,40},{32,48},{40,24},{48,32},{56,8},{64,80... | collective-permute-start | bytes 294920 | tf_op jit(solution)/shard_map/ppermute | solution.py:24
  21.9 11.9 %collective-permute-start.5 = (bf16[2,6,32,512]{3,2,1,0:T(8,128)(2,1)S(1)}, bf16[2,6,32,512]{3,2,1,0:T(8,128)(2,1)S(1)}, u32[]{:S(2)}, u32[]{:S(2)}) collective-permute-start(bf16[2,6,32,512]{3,2,1,0:T(8,128)(2,1)S(1)} %pad_maximum_fusion.6), channel_id=1, source_target_pairs={{0,192},{8,72},{16,208},{24,88},{32,224},{40,104},{48,240},{56,120... | collective-permute-start | bytes 1179656 | tf_op jit(solution)/shard_map/ppermute | solution.py:24
  23.5 4.8 %collective-permute-start.6 = (bf16[2,6,32,256]{3,2,1,0:T(8,128)(2,1)S(1)}, bf16[2,6,32,256]{3,2,1,0:T(8,128)(2,1)S(1)}, u32[]{:S(2)}, u32[]{:S(2)}) collective-permute-start(bf16[2,6,32,256]{3,2,1,0:T(8,128)(2,1)S(1)} %pad_maximum_fusion.10), channel_id=1, source_target_pairs={{0,48},{8,24},{16,32},{24,8},{32,16},{40,56},{48,0},{56,40},{64,11... | collective-permute-start | bytes 589832 | tf_op jit(solution)/shard_map/ppermute | solution.py:24
  33.9 14.1 %collective-permute-start.7 = (bf16[4,6,32,512]{3,2,1,0:T(8,128)(2,1)S(1)}, bf16[4,6,32,512]{3,2,1,0:T(8,128)(2,1)S(1)}, u32[]{:S(2)}, u32[]{:S(2)}) collective-permute-start(bf16[4,6,32,512]{3,2,1,0:T(8,128)(2,1)S(1)} %pad_maximum_fusion.3), channel_id=1, source_target_pairs={{0,16},{8,56},{16,0},{24,40},{32,48},{40,24},{48,32},{56,8},{64,80... | collective-permute-start | bytes 2359304 | tf_op jit(solution)/shard_map/ppermute | solution.py:24
  36.9 11.1 %collective-permute-start.8 = (bf16[4,6,32,256]{3,2,1,0:T(8,128)(2,1)S(1)}, bf16[4,6,32,256]{3,2,1,0:T(8,128)(2,1)}, u32[]{:S(2)}, u32[]{:S(2)}) collective-permute-start(bf16[4,6,32,256]{3,2,1,0:T(8,128)(2,1)S(1)} %pad_maximum_fusion.7), channel_id=1, source_target_pairs={{0,64},{8,200},{16,80},{24,216},{32,96},{40,232},{48,112},{56,248}... | collective-permute-start | bytes 1179656 | tf_op jit(solution)/shard_map/ppermute | solution.py:24
  42.6 19.7 %collective-permute-start = (bf16[256,3072]{0,1:T(8,128)(2,1)S(1)}, bf16[256,3072]{0,1:T(8,128)(2,1)}, u32[]{:S(2)}, u32[]{:S(2)}) collective-permute-start(bf16[256,3072]{0,1:T(8,128)(2,1)S(1)} %copy.7), channel_id=1, source_target_pairs={{0,8},{8,0},{16,24},{24,16},{32,40},{40,32},{48,56},{56,48},{64,72... | collective-permute-start | bytes 4718600 | tf_op jit(solution)/shard_map/ppermute | solution.py:24
  51.2 24.8 %collective-permute-start.9 = (bf16[2,4,6,32,512]{4,3,2,1,0:T(8,128)(2,1)}, bf16[2,4,6,32,512]{4,3,2,1,0:T(8,128)(2,1)}, u32[]{:S(2)}, u32[]{:S(2)}) collective-permute-start(bf16[2,4,6,32,512]{4,3,2,1,0:T(8,128)(2,1)} %pad_maximum_fusion.1.refs_5_), channel_id=1, source_target_pairs={{0,48},{8,24},{16,32},{24,8},{32,16},{40,56},{48,0},{56,40},{64,11... | collective-permute-start | bytes 4718600 | tf_op jit(solution)/shard_map/ppermute | solution.py:24
  52.0 8.8 %collective-permute-start.1 = (bf16[256,768]{1,0:T(8,128)(2,1)S(1)}, bf16[256,768]{1,0:T(8,128)(2,1)S(1)}, u32[]{:S(2)}, u32[]{:S(2)}) collective-permute-start(bf16[256,768]{1,0:T(8,128)(2,1)S(1)} %pad_maximum_fusion.5), channel_id=1, source_target_pairs={{0,8},{8,0},{16,24},{24,16},{32,40},{40,32},{48,56},{56,48},{64,72... | collective-permute-start | bytes 1179656 | tf_op jit(solution)/shard_map/ppermute | solution.py:24
  58.3 17.7 %collective-permute-start.10 = (bf16[2,4,6,32,256]{4,3,2,1,0:T(8,128)(2,1)}, bf16[2,4,6,32,256]{4,3,2,1,0:T(8,128)(2,1)}, u32[]{:S(2)}, u32[]{:S(2)}) collective-permute-start(bf16[2,4,6,32,256]{4,3,2,1,0:T(8,128)(2,1)} %pad_maximum_fusion.4.refs_5_), channel_id=1, source_target_pairs={{0,192},{8,72},{16,208},{24,88},{32,224},{40,104},{48,240},{56,120... | collective-permute-start | bytes 2359304 | tf_op jit(solution)/shard_map/ppermute | solution.py:24
  86.2 33.2 %collective-permute-start.13 = (bf16[6,512,256]{2,1,0:T(8,128)(2,1)}, bf16[6,512,256]{2,1,0:T(8,128)(2,1)}, u32[]{:S(2)}, u32[]{:S(2)}) collective-permute-start(bf16[6,512,256]{2,1,0:T(8,128)(2,1)} %get-tuple-element.61), channel_id=1, source_target_pairs={{0,48},{8,24},{16,32},{24,8},{32,16},{40,56},{48,0},{56,40},{64,11... | collective-permute-start | bytes 4718600 | tf_op jit(solution)/shard_map/ppermute | solution.py:24
  96.1 14.3 %collective-permute-start.17 = (bf16[3,512,256]{2,1,0:T(8,128)(2,1)}, bf16[3,512,256]{2,1,0:T(8,128)(2,1)S(1)}, u32[]{:S(2)}, u32[]{:S(2)}) collective-permute-start(bf16[3,512,256]{2,1,0:T(8,128)(2,1)} %get-tuple-element.66), channel_id=1, source_target_pairs={{0,192},{8,72},{16,208},{24,88},{32,224},{40,104},{48,240},{56,120... | collective-permute-start | bytes 2359304 | tf_op jit(solution)/shard_map/ppermute | solution.py:24
  105.7 28.0 %collective-permute-start.12 = (bf16[8,256,384]{2,1,0:T(8,128)(2,1)}, bf16[8,256,384]{2,1,0:T(8,128)(2,1)}, u32[]{:S(2)}, u32[]{:S(2)}) collective-permute-start(bf16[8,256,384]{2,1,0:T(8,128)(2,1)} %get-tuple-element.59), channel_id=1, source_target_pairs={{0,8},{8,0},{16,24},{24,16},{32,40},{40,32},{48,56},{56,48},{64,72... | collective-permute-start | bytes 4718600 | tf_op jit(solution)/shard_map/ppermute | solution.py:24
  110.7 21.8 %collective-permute-start.18 = (bf16[2,512,256]{2,1,0:T(8,128)(2,1)S(1)}, bf16[2,512,256]{2,1,0:T(8,128)(2,1)}, u32[]{:S(2)}, u32[]{:S(2)}) collective-permute-start(bf16[2,512,256]{2,1,0:T(8,128)(2,1)S(1)} %fusion.3), channel_id=1, source_target_pairs={{0,64},{8,200},{16,80},{24,216},{32,96},{40,232},{48,112},{56,248}... | collective-permute-start | bytes 1572872 | tf_op jit(solution)/shard_map/ppermute | solution.py:24
  121.6 15.1 %collective-permute-start.14 = (bf16[3,512,256]{2,1,0:T(8,128)(2,1)}, bf16[3,512,256]{2,1,0:T(8,128)(2,1)}, u32[]{:S(2)}, u32[]{:S(2)}) collective-permute-start(bf16[3,512,256]{2,1,0:T(8,128)(2,1)} %add_convert_fusion.1), channel_id=1, source_target_pairs={{0,16},{8,56},{16,0},{24,40},{32,48},{40,24},{48,32},{56,8},{64,80... | collective-permute-start | bytes 2359304 | tf_op jit(solution)/shard_map/ppermute | solution.py:24
  139.7 14.9 %collective-permute-start.15 = (bf16[2,512,256]{2,1,0:T(8,128)(2,1)}, bf16[2,512,256]{2,1,0:T(8,128)(2,1)S(1)}, u32[]{:S(2)}, u32[]{:S(2)}) collective-permute-start(bf16[2,512,256]{2,1,0:T(8,128)(2,1)} %get-tuple-element.64), channel_id=1, source_target_pairs={{0,192},{8,72},{16,208},{24,88},{32,224},{40,104},{48,240},{56,120... | collective-permute-start | bytes 1572872 | tf_op jit(solution)/shard_map/ppermute | solution.py:24
  141.7 5.3 %collective-permute-start.19 = (bf16[512,256]{1,0:T(8,128)(2,1)S(1)}, bf16[512,256]{1,0:T(8,128)(2,1)S(1)}, u32[]{:S(2)}, u32[]{:S(2)}) collective-permute-start(bf16[512,256]{1,0:T(8,128)(2,1)S(1)} %fusion.7), channel_id=1, source_target_pairs={{0,48},{8,24},{16,32},{24,8},{32,16},{40,56},{48,0},{56,40},{64,11... | collective-permute-start | bytes 786440 | tf_op jit(solution)/shard_map/ppermute | solution.py:24
  147.1 28.9 %collective-permute-start.20 = (bf16[512,256]{1,0:T(8,128)(2,1)S(1)}, bf16[512,256]{1,0:T(8,128)(2,1)S(1)}, u32[]{:S(2)}, u32[]{:S(2)}) collective-permute-start(bf16[512,256]{1,0:T(8,128)(2,1)S(1)} %fusion.4), channel_id=1, source_target_pairs={{0,16},{8,56},{16,0},{24,40},{32,48},{40,24},{48,32},{56,8},{64,80... | collective-permute-start | bytes 786440 | tf_op jit(solution)/shard_map/ppermute | solution.py:24
  154.7 21.2 %collective-permute-start.16 = (bf16[512,256]{1,0:T(8,128)(2,1)S(1)}, bf16[512,256]{1,0:T(8,128)(2,1)S(1)}, u32[]{:S(2)}, u32[]{:S(2)}) collective-permute-start(bf16[512,256]{1,0:T(8,128)(2,1)S(1)} %fusion.6), channel_id=1, source_target_pairs={{0,64},{8,200},{16,80},{24,216},{32,96},{40,232},{48,112},{56,248}... | collective-permute-start | bytes 786440 | tf_op jit(solution)/shard_map/ppermute | solution.py:24
  155.6 29.3 %collective-permute-start.11 = (bf16[256,768]{1,0:T(8,128)(2,1)S(1)}, bf16[256,768]{1,0:T(8,128)(2,1)S(1)}, u32[]{:S(2)}, u32[]{:S(2)}) collective-permute-start(bf16[256,768]{1,0:T(8,128)(2,1)S(1)} %pad_maximum_fusion.8), channel_id=1, source_target_pairs={{0,8},{8,0},{16,24},{24,16},{32,40},{40,32},{48,56},{56,48},{64,72... | collective-permute-start | bytes 1179656 | tf_op jit(solution)/shard_map/ppermute | solution.py:24
  176.1 9.9 %collective-permute-start.21 = (bf16[512,256]{1,0:T(8,128)(2,1)S(1)}, bf16[512,256]{1,0:T(8,128)(2,1)S(1)}, u32[]{:S(2)}, u32[]{:S(2)}) collective-permute-start(bf16[512,256]{1,0:T(8,128)(2,1)S(1)} %get-tuple-element.67), channel_id=1, source_target_pairs={{0,8},{8,0},{16,24},{24,16},{32,40},{40,32},{48,56},{56,48},{64,72... | collective-permute-start | bytes 786440 | tf_op jit(solution)/shard_map/ppermute | solution.py:24
  191.6 27.3 %all-to-all-start = ((bf16[32,16,512]{2,1,0:T(8,128)(2,1)}), bf16[32,16,512]{2,1,0:T(8,128)(2,1)S(1)}, u32[]{:S(2)}, u32[]{:S(2)}) async-start(bf16[32,16,512]{2,1,0:T(8,128)(2,1)} %shard_map.62), calls=%async_computation.1 | async-start | bytes 1048576 | tf_op jit(solution)/shard_map/all_to_all | solution.py:396
  (12 other events, 153.9 us)
Sparse Core Ops, SparseCore 0:
  136.9 71.3 reduce-scatter.1
where the time goes:
time: 231 us; the launch traced here: 228 us
  starting transfers between devices  85.8 us (37%)
  waiting for transfers between devices  67.7 us (29%)
  Pallas kernels  35 us (15%)
  other arithmetic  18.6 us (8%)
  between operations  14.3 us (6%)
  local copies, waits for them, and re-layouts  7.13 us (3%)
    ppermute x22, starting transfers between devices, moved(): return lax.ppermute(array, 'dp', pairs)  80.6 us
    ppermute x22, waiting for transfers between devices, moved(): return lax.ppermute(array, 'dp', pairs)  45.8 us
    all_to_all x1, waiting for transfers between devices, local(): arrived = lax.all_to_all(result, 'dp', 0, 0, tiled=True)  21.8 us
    pallas_call x2, Pallas kernels, chunk(): pl.pallas_call(lambda *refs: chunk_kernel(large, scale, *refs), out_shape...  18.6 us
    pallas_call x1, Pallas kernels, input_partials(): pl.pallas_call(input_kernel, out_shape=[out, out], in_specs=[vmem] * (2 *...  6.89 us
    all_to_all x1, starting transfers between devices, local(): arrived = lax.all_to_all(result, 'dp', 0, 0, tiled=True)  5.18 us
  transfers between devices with their start and end apart: 24, of which 11 were waited for; matrix products, arithmetic and copies ran while one was open for 10% of the time, Pallas kernels for 11%

commit v1 on v0

v1 whole, which is shorter than its diff:
```python
import jax
import jax.numpy as jnp
from jax import lax
from jax.experimental import pallas as pl
from jax.experimental.pallas import tpu as pltpu
from jax.sharding import PartitionSpec as P

S = 512
HALF = 256
NZ, NY, NC = 4, 4, 2
NX = 4
CHIPS = NZ * NY


def params(size=58):
    return pltpu.CompilerParams(vmem_limit_bytes=size * 1024 * 1024)


def dev(z, y, c):
    return ((z % NZ) * NY + y % NY) * NC + c % NC


def moved(array, pairs):
    return lax.ppermute(array, "dp", pairs)


def swap_cores(array):
    return moved(
        array,
        [(dev(z, y, c), dev(z, y, 1 - c)) for z in range(NZ) for y in range(NY) for c in range(NC)],
    )


def turn(place, core, step):
    return (1 if (place + core) % 2 == 0 else -1) * (1 if step == 1 else -1)


def exchange(array, axis, step):
    pairs = []
    for z in range(NZ):
        for y in range(NY):
            for c in range(NC):
                if axis == "y":
                    to = dev(z, y + turn(y, c, step), c)
                else:
                    to = dev(z + turn(z, c, step), y, c)
                pairs.append((dev(z, y, c), to))
    return moved(array, pairs)


def chips_of(pos_ref, large):
    y, z, core = pos_ref[0], pos_ref[1], pos_ref[2]
    sy = 1 - 2 * lax.rem(y + core, 2)
    sz = 1 - 2 * lax.rem(z + core, 2)
    ys = [lax.rem(y + step + NY, NY) for step in (0, sy, -sy, 2)]
    zs = [lax.rem(z + step + NZ, NZ) for step in (0, sz, -sz, 2)]
    if large == "y":
        return [[zz * NY + yy for zz in zs] for yy in ys]
    return [[zz * NY + yy for yy in ys] for zz in zs]


def main_kernel(scale, pos, tok_h, tok_t_h, cot0_h, cot1_h, *refs):
    pieces, refs = refs[:8], refs[8:]
    act0, act1, keep0, keep1, send, q_keep, q_send, ig_own, ig_other = refs[:9]
    tok, tok_t, w, cot, v, slope_ref, stage, ig, sem_w, sem_in, sem_out, sem_ig = refs[9:]
    rows, wide = w.shape[0], w.shape[3]
    tokens = tok.shape[0]
    half, mid = tokens // 2, rows * S // 2
    y, z, core = pos[0], pos[1], pos[2]
    copy = pltpu.make_async_copy
    w_copies = []
    for part, large, lo in ((0, "y", 0), (1, "z", wide - HALF)):
        chips = chips_of(pos, large)
        for i in range(4):
            piece = pieces[4 * part + i]
            for k in range(4):
                to = w.at[:, chips[i][k], :, pl.ds(lo, piece.shape[3])]
                w_copies.append(copy(piece.at[k], to, sem_w.at[16 * part + 4 * i + k]))
    in_copies = [
        copy(tok_h.at[:, pl.ds(n * mid, mid)], tok.at[:, pl.ds(n * mid, mid)], sem_in.at[n])
        for n in (0, 1)
    ]
    in_copies.append(copy(cot0_h, cot.at[pl.ds(0, half)], sem_in.at[2]))
    in_copies.append(copy(cot1_h, cot.at[pl.ds(half, half)], sem_in.at[3]))
    for b in range(rows):
        here = pl.ds(b * S, S)
        in_copies.append(copy(tok_t_h.at[here], tok_t.at[here], sem_in.at[4 + b]))
    for item in w_copies + in_copies:
        item.start()
    for item in w_copies:
        item.wait()
    in_copies[0].wait()
    first = jnp.dot(
        tok[:, :mid], w[: rows // 2].reshape(mid, wide), preferred_element_type=jnp.float32
    )
    in_copies[1].wait()
    v[...] = first + jnp.dot(
        tok[:, mid:], w[rows // 2 :].reshape(mid, wide), preferred_element_type=jnp.float32
    )
    in_copies[2].wait()
    in_copies[3].wait()
    coeff = 0.7978845608
    tile = min(16, half)

    def gelu(act, start):
        def body(n, carry):
            at = pl.multiple_of(n * tile, tile)
            here = pl.ds(start + at, tile)
            x = v[here]
            square = x * x
            t = jnp.tanh(coeff * (x + 0.044715 * square * x))
            act[pl.ds(at, tile)] = (0.5 * x * (1.0 + t)).astype(jnp.bfloat16)
            deriv = 0.5 * (1.0 + t) + 0.5 * x * (1.0 - t * t) * coeff * (
                1.0 + 3.0 * 0.044715 * square
            )
            slope_ref[here] = (cot[here].astype(jnp.float32) * deriv).astype(jnp.bfloat16)
            return carry

        lax.fori_loop(0, half // tile, body, 0)

    gelu(act0, 0)
    gelu(act1, half)

    def send_off(block, ref, slot, when):
        @pl.when(when)
        def _():
            copy(stage.at[block], ref.at[slot], sem_out.at[block]).start()

    sy = 1 - 2 * lax.rem(y + core, 2)
    sz = 1 - 2 * lax.rem(z + core, 2)
    other = lax.rem(z + sz + NZ, NZ)
    for b in range(rows):
        in_copies[4 + b].wait()
        g = jnp.dot(tok_t[b * S : (b + 1) * S], slope_ref[...], preferred_element_type=jnp.float32)
        g = (g * scale).astype(jnp.bfloat16)
        for j in range(wide // HALF):
            block = j * rows + b
            stage[block] = g[:, j * HALF : (j + 1) * HALF]
            place, m = block // 3, block % 3
            if j < 2:
                step = lax.rem(place - y + NY, NY)
                send_off(block, keep0, m, step == 0)
                send_off(block, keep1, m, step == lax.rem(sy + NY, NY))
                send_off(block, send, m, step == lax.rem(NY - sy, NY))
                send_off(block, send, 3 + m, step == 2)
            else:
                to = 2 * (b // 3) + m // 2
                mine = jnp.logical_or(to == z, to == other)
                send_off(block, q_keep, m, mine)
                send_off(block, q_send, m, jnp.logical_not(mine))
    parts, width = ig.shape[1], ig.shape[3]
    ig_copies = []
    for b in range(rows):
        term = lax.dot_general(
            slope_ref[...],
            w[b].reshape(S, wide),
            (((1,), (1,)), ((), ())),
            preferred_element_type=jnp.float32,
        ).astype(jnp.bfloat16)
        at = b * S
        while at < (b + 1) * S:
            part, inside = at // width, at % width
            take = min(width - inside, (b + 1) * S - at)
            lo = at - b * S
            for side in (0, 1):
                ig[side, part, :, inside : inside + take] = term[
                    side * half : (side + 1) * half, lo : lo + take
                ]
            at += take
        if b % (rows // 2) == rows // 2 - 1:
            span = pl.ds(b // (rows // 2) * (parts // 2), parts // 2)
            for side, ref in ((1, ig_other), (0, ig_own)):
                ig_copies.append(
                    copy(ig.at[side, span], ref.at[span], sem_ig.at[len(ig_copies)])
                )
                ig_copies[-1].start()
    for block in range(rows * wide // HALF):
        copy(stage.at[block], keep0.at[0], sem_out.at[block]).wait()
    for item in ig_copies:
        item.wait()


def main_part(parts, scale, pos, tok, tok_t, cot0, cot1, pieces):
    tokens = tok.shape[0]
    rows, wide = pieces[0].shape[1], cot0.shape[1]
    blocks = rows * wide // HALF
    shape = lambda *dims: jax.ShapeDtypeStruct(dims, jnp.bfloat16)
    vmem = pl.BlockSpec(memory_space=pltpu.VMEM)
    hbm = pl.BlockSpec(memory_space=pltpu.HBM)
    share = (rows, CHIPS, S // CHIPS, wide)
    sums = [shape(n, S, HALF) for n in (3, 3, 6, 3, 3)]
    cut = (parts, tokens // 2, rows * S // parts)
    outs = [shape(tokens // 2, wide), shape(tokens // 2, wide)] + sums + [shape(*cut)] * 2
    held = lambda dims, dtype=jnp.bfloat16: pltpu.VMEM(dims, dtype)
    return pl.pallas_call(
        lambda *refs: main_kernel(scale, *refs),
        out_shape=outs,
        in_specs=[pl.BlockSpec(memory_space=pltpu.SMEM)] + [hbm] * 12,
        out_specs=[vmem] * 2 + [hbm] * (len(sums) + 2),
        scratch_shapes=[
            held(tok.shape),
            held(tok_t.shape),
            held(share),
            held((tokens, wide)),
            held((tokens, wide), jnp.float32),
            held((tokens, wide)),
            held((blocks, S, HALF)),
            held((2, *cut)),
            pltpu.SemaphoreType.DMA((32,)),
            pltpu.SemaphoreType.DMA((4 + rows,)),
            pltpu.SemaphoreType.DMA((blocks,)),
            pltpu.SemaphoreType.DMA((4,)),
        ],
        compiler_params=params(),
        cost_estimate=pl.CostEstimate(
            flops=6 * tokens * rows * S * wide,
            bytes_accessed=8 * tokens * rows * S,
            transcendentals=tokens * wide,
        ),
    )(pos, tok, tok_t, cot0, cot1, *pieces)


def owners():
    table = {}
    for y in range(NY):
        for m in range(3):
            table[3 * (y % 2) + m, y // 2] = dev(m, y, 0)
    for z in range(NZ):
        for index, y in enumerate((0, 2) if z % 2 == 0 else (0,)):
            table[3 * (z // 2) + index + 2 * (z % 2), 2] = dev(z, y, 1)
    return table


def newton_kernel(g0_ref, g1_ref, out_ref):
    def mm(a, b):
        return jnp.dot(
            a.astype(jnp.bfloat16), b.astype(jnp.bfloat16), preferred_element_type=jnp.float32
        )

    g = jnp.concatenate([g0_ref[...], g1_ref[...]], axis=1)
    gf = g.astype(jnp.float32)
    left = lax.dot_general(g, g, (((1,), (1,)), ((), ())), preferred_element_type=jnp.float32)
    trace = jnp.sum(gf * gf, axis=(0, 1), keepdims=True)
    diagonal = lax.broadcasted_iota(jnp.int32, (S, S), 0) == lax.broadcasted_iota(
        jnp.int32, (S, S), 1
    )
    damped = left + jnp.where(diagonal, 0.1 * trace / S + 1e-06, 0.0)
    norm = jnp.sum(damped * damped, axis=(0, 1), keepdims=True)
    scale = 5.0 / (2.0 * jnp.sqrt(norm))
    m = damped * scale
    sq = mm(m, m)
    n = (10.0 * m - sq) * 0.0625
    km = (5.0 * m - sq) * 0.25
    u = 2.44140625 * km - mm(3.125 * n - mm(n, n), km)
    v = (1.25 * m + u) * 0.25
    h = 3.125 * v - mm(v, v)
    factor = (float(S) ** 0.5) * jnp.sqrt(scale)
    result = (2.44140625 * gf - mm(h, g)) * factor
    out_ref[...] = result.astype(jnp.bfloat16).reshape(out_ref.shape)


def newton(g0, g1):
    vmem = pl.BlockSpec(memory_space=pltpu.VMEM)
    count = CHIPS * NC
    return pl.pallas_call(
        newton_kernel,
        out_shape=jax.ShapeDtypeStruct((count, S // count, S), jnp.bfloat16),
        in_specs=[vmem, vmem],
        out_specs=vmem,
        compiler_params=params(24),
    )(g0, g1)


def place_kernel(in_ref, out_ref):
    for (b, j), owner in owners().items():
        out_ref[b, :, j * S : (j + 1) * S] = in_ref[owner].astype(jnp.float32)


def place(rows, cols, arrived):
    vmem = pl.BlockSpec(memory_space=pltpu.VMEM)
    return pl.pallas_call(
        place_kernel,
        out_shape=jax.ShapeDtypeStruct((rows, arrived.shape[1], cols * S), jnp.float32),
        in_specs=[vmem],
        out_specs=vmem,
        compiler_params=params(16),
    )(arrived)


def local(tokens, weights, cotangent):
    rows, local_rows, width = weights.shape
    cols = width // S
    tok_local = tokens.shape[0]
    scale = 1.0 / (tok_local * lax.axis_size("dp"))
    parts = lax.axis_size("tensor")
    here = lax.axis_index("dp")
    core = here % NC
    first = core == 0
    pos = jnp.stack([(here // NC) % NY, here // (NC * NY), core]).astype(jnp.int32)
    wide32 = lambda array: array.astype(jnp.float32)
    cast = lambda array: array.astype(jnp.bfloat16)

    def split(array):
        pairs = [
            (array[..., j * S : j * S + HALF], array[..., j * S + HALF : (j + 1) * S])
            for j in range(cols)
        ]
        mine = jnp.concatenate([jnp.where(first, a, b) for a, b in pairs], axis=-1)
        theirs = jnp.concatenate([jnp.where(first, b, a) for a, b in pairs], axis=-1)
        return mine, theirs

    w_mine, w_theirs = split(weights)
    w_recv = swap_cores(w_theirs)
    shard = jnp.concatenate(
        [jnp.where(first, w_mine, w_recv), jnp.where(first, w_recv, w_mine)], axis=1
    )

    tok = jnp.concatenate([tokens, swap_cores(tokens)], axis=0)
    c_mine, c_theirs = split(cotangent)
    c_recv = swap_cores(c_theirs)
    tok_t = tok.T

    plan = [("z", "y", 0, (cols - 1) * HALF), ("y", "z", (cols - 1) * HALF, cols * HALF)]

    together = lax.optimization_barrier
    ones = [shard[..., lo:hi] for small, large, lo, hi in plan]
    twos = together(
        tuple(
            jnp.stack([one, got])
            for one, got in zip(
                ones, together(tuple(exchange(x, p[0], 1) for x, p in zip(ones, plan)))
            )
        )
    )
    fours = together(
        tuple(
            jnp.concatenate([two, got])
            for two, got in zip(
                twos, together(tuple(exchange(x, p[0], 2) for x, p in zip(twos, plan)))
            )
        )
    )
    got1 = together(
        tuple(exchange(x, p[1], step) for step in (1, 2) for x, p in zip(fours, plan))
    )
    pieces = []
    for n, (small, large, lo, hi) in enumerate(plan):
        pieces += [fours[n], got1[n], got1[2 + n], exchange(got1[n], large, 2)]

    act0, act1, *grads, ig_own, ig_other = main_part(
        parts, scale, pos, tok, tok_t, c_mine, c_recv, pieces
    )
    keep0, keep1, send, q_keep, q_send = grads
    y, z = pos[0], pos[1]
    z_even = z % 2 == 0
    ig_sum = cast(wide32(ig_own) + wide32(swap_cores(ig_other)))
    got, q_got, ig_sum = together((exchange(send, "y", 2), exchange(q_send, "z", 2), ig_sum))

    def q_pick(keep, got, pair):
        both = lambda array: jnp.where(pair, array[:2], jnp.stack([array[2], array[2]]))
        return wide32(both(keep)) + wide32(both(got))

    got2, q_got2 = together(
        (
            exchange(cast(wide32(keep1) + wide32(got[3:])), "y", 1),
            exchange(cast(q_pick(q_keep, q_got, jnp.logical_not(z_even))), "z", 1),
        )
    )

    def p_slot(step):
        m = jnp.minimum((z + step + NZ) % NZ, 2)
        one = lambda array: lax.dynamic_index_in_dim(array, m, 0, keepdims=False)
        return wide32(one(keep0)) + wide32(one(got)) + wide32(one(got2))

    sz = 1 - 2 * ((z + core) % 2)
    y_pair = jnp.where(y % 2 == 0, y, (y + 1 - 2 * ((y + core) % 2) + NY) % NY)
    q_two = q_pick(q_keep, q_got, z_even) + wide32(q_got2)
    got3, q_got3 = together(
        (
            exchange(jnp.stack([cast(p_slot(-sz)), cast(p_slot(2))]), "z", 2),
            exchange(cast(jnp.where(y_pair == 0, q_two[1], q_two[0])), "y", 2),
        )
    )
    q_half = cast(jnp.where(y_pair == 0, q_two[0], q_two[1]) + wide32(q_got3))

    low = parts // NX
    pairs_x = [[x * low + l for x in range(NX)] for l in range(low)]
    ig_x = lax.psum_scatter(
        ig_sum, "tensor", scatter_dimension=0, axis_index_groups=pairs_x, tiled=True
    )
    odd = lax.axis_index("tensor") % low == 1
    ig_there = lax.ppermute(
        jnp.where(odd, ig_x[0], ig_x[1]), "tensor", [(t, t + 1 - 2 * (t % 2)) for t in range(parts)]
    )
    got4, q_got4, ig_there = together(
        (
            exchange(cast(p_slot(sz) + wide32(got3[1])), "z", 1),
            exchange(q_half, "y", 1),
            ig_there,
        )
    )
    p_block = cast(p_slot(0) + wide32(got3[0]) + wide32(got4))
    q_block = cast(wide32(q_half) + wide32(q_got4))
    input_grad = cast(wide32(jnp.where(odd, ig_x[1], ig_x[0])) + wide32(ig_there))

    act_recv = swap_cores(act1)
    columns = []
    for j in range(cols):
        at = slice(j * HALF, (j + 1) * HALF)
        columns.append(jnp.where(first, act0[:, at], act_recv[:, at]))
        columns.append(jnp.where(first, act_recv[:, at], act0[:, at]))
    activated = jnp.concatenate(columns, axis=1)

    recv = swap_cores(jnp.where(first, q_block, p_block))
    result = newton(jnp.where(first, p_block, recv), jnp.where(first, recv, q_block))
    arrived = lax.all_to_all(result, "dp", 0, 0, tiled=True)
    update = place(rows, cols, arrived)
    return (activated, input_grad, update)


def solution(mesh):
    return jax.shard_map(
        local,
        mesh=mesh,
        in_specs=(P("dp", None), P(None, "dp", "tensor"), P("dp", "tensor")),
        out_specs=(P("dp", "tensor"), P("dp", "tensor"), P(None, "dp", "tensor")),
        check_vma=False,
    )
```

time: 231 us -> 214 us (0.926)
  starting transfers between devices: 85.8 us -> 56 us
  waiting for transfers between devices: 67.7 us -> 87.4 us
  Pallas kernels: 35 us -> 23 us
  other arithmetic: 18.6 us -> 26.6 us
    ppermute x22 -> x24, starting transfers between devices: 80.6 us -> 48.8 us  [moved(): return lax.ppermute(array, 'dp', pairs)]
    ppermute x22 -> x24, waiting for transfers between devices: 45.8 us -> 71.6 us  [moved(): return lax.ppermute(array, 'dp', pairs)]
    pallas_call x4 -> x1, Pallas kernels: 28.5 us -> 18.6 us  [main_part(): pl.pallas_call(lambda *refs: main_kernel(scale, *refs), out_shape=outs, i...]
    all_to_all x1, waiting for transfers between devices: 21.8 us -> 14.5 us  [local(): arrived = lax.all_to_all(result, 'dp', 0, 0, tiled=True)]
    convert_element_type x5 -> x7, other arithmetic: 2.46 us -> 7.65 us  [local(): cast = lambda array: array.astype(jnp.bfloat16)]
    convert_element_type x1 -> x0, other arithmetic: 2.98 us -> none  [local(): (wide32(ig_own) + wide32(swap_cores(ig_other))).astype(jnp.bfloat16)]
    another operation x2 -> x1, other arithmetic: 3.23 us -> 0.84 us  [local(): jnp.stack([cast(p_slot(-sz)), cast(p_slot(2))])]
  transfers between devices with their start and end apart: 24 -> 27, of which waited for: 11 -> 16; matrix products, arithmetic and copies ran while one was open for 10% -> 13% of each run, Pallas kernels for 11% -> 0%
where the time goes in v1:
time: 214 us; the launch traced here: 213 us
  waiting for transfers between devices  87.4 us (41%)
  starting transfers between devices  56 us (26%)
  other arithmetic  26.6 us (12%)
  Pallas kernels  23 us (11%)
  between operations  14.4 us (7%)
  local copies, waits for them, and re-layouts  6 us (3%)
    ppermute x24, waiting for transfers between devices, moved(): return lax.ppermute(array, 'dp', pairs)  71.6 us
    ppermute x24, starting transfers between devices, moved(): return lax.ppermute(array, 'dp', pairs)  48.8 us
    pallas_call x1, Pallas kernels, main_part(): pl.pallas_call(lambda *refs: main_kernel(scale, *refs), out_shape=outs, i...  18.6 us
    all_to_all x1, waiting for transfers between devices, local(): arrived = lax.all_to_all(result, 'dp', 0, 0, tiled=True)  14.5 us
    convert_element_type x7, other arithmetic, local(): cast = lambda array: array.astype(jnp.bfloat16)  7.65 us
    all_to_all x1, starting transfers between devices, local(): arrived = lax.all_to_all(result, 'dp', 0, 0, tiled=True)  7.05 us
  transfers between devices with their start and end apart: 27, of which 16 were waited for; matrix products, arithmetic and copies ran while one was open for 13% of the time, Pallas kernels for 0%

profile of v1, /device:TPU:1, one launch (start us, length us, event | category | flops | bytes accessed | tf_op | source)
XLA Modules:
  0.0 213.5 jit_solution(11794320734819162892)
XLA Ops:
  8.2 3.3 %collective-permute-start.2 = (bf16[6,16,768]{2,1,0:T(8,128)(2,1)S(1)}, bf16[6,16,768]{2,1,0:T(8,128)(2,1)S(1)}, u32[]{:S(2)}, u32[]{:S(2)}) collective-permute-start(bf16[6,16,768]{2,1,0:T(8,128)(2,1)S(1)} %pad_maximum_fusion.11), channel_id=1, source_target_pairs={{0,8},{8,0},{16,24},{24,16},{32,40},{40,32},{48,56},{56,48},{64,72... | collective-permute-start | bytes 442376 | tf_op jit(solution)/shard_map/ppermute | solution.py:24
  12.6 4.4 %collective-permute-start.3 = (bf16[6,32,512]{2,1,0:T(8,128)(2,1)S(1)}, bf16[6,32,512]{2,1,0:T(8,128)(2,1)S(1)}, u32[]{:S(2)}, u32[]{:S(2)}) collective-permute-start(bf16[6,32,512]{2,1,0:T(8,128)(2,1)S(1)} %fusion.5), channel_id=1, source_target_pairs={{0,64},{8,200},{16,80},{24,216},{32,96},{40,232},{48,112},{56,248}... | collective-permute-start | bytes 589832 | tf_op jit(solution)/shard_map/ppermute | solution.py:24
  17.0 2.8 %collective-permute-start.4 = (bf16[6,32,256]{2,1,0:T(8,128)(2,1)S(1)}, bf16[6,32,256]{2,1,0:T(8,128)(2,1)S(1)}, u32[]{:S(2)}, u32[]{:S(2)}) collective-permute-start(bf16[6,32,256]{2,1,0:T(8,128)(2,1)S(1)} %pad_maximum_fusion.12), channel_id=1, source_target_pairs={{0,16},{8,56},{16,0},{24,40},{32,48},{40,24},{48,32},{56,8},{64,80... | collective-permute-start | bytes 294920 | tf_op jit(solution)/shard_map/ppermute | solution.py:24
  26.1 4.8 %collective-permute-start = (bf16[256,3072]{0,1:T(8,128)(2,1)S(1)}, bf16[256,3072]{0,1:T(8,128)(2,1)}, u32[]{:S(2)}, u32[]{:S(2)}) collective-permute-start(bf16[256,3072]{0,1:T(8,128)(2,1)S(1)} %copy.7), channel_id=1, source_target_pairs={{0,8},{8,0},{16,24},{24,16},{32,40},{40,32},{48,56},{56,48},{64,72... | collective-permute-start | bytes 4718600 | tf_op jit(solution)/shard_map/ppermute | solution.py:24
  30.9 3.6 %collective-permute-done.5 = bf16[2,6,32,512]{3,2,1,0:T(8,128)(2,1)} collective-permute-done((bf16[2,6,32,512]{3,2,1,0:T(8,128)(2,1)S(1)}, bf16[2,6,32,512]{3,2,1,0:T(8,128)(2,1)}, u32[]{:S(2)}, u32[]{:S(2)}) %collective-permute-start.5) | collective-permute-done | bytes 393248 | tf_op jit(solution)/shard_map/ppermute | solution.py:24
  36.8 3.0 %collective-permute-start.7 = (bf16[4,6,32,512]{3,2,1,0:T(8,128)(2,1)S(1)}, bf16[4,6,32,512]{3,2,1,0:T(8,128)(2,1)}, u32[]{:S(2)}, u32[]{:S(2)}) collective-permute-start(bf16[4,6,32,512]{3,2,1,0:T(8,128)(2,1)S(1)} %pad_maximum_fusion.1.refs_5_), channel_id=1, source_target_pairs={{0,16},{8,56},{16,0},{24,40},{32,48},{40,24},{48,32},{56,8},{64,80... | collective-permute-start | bytes 2359304 | tf_op jit(solution)/shard_map/ppermute | solution.py:24
  41.4 2.8 %collective-permute-start.8 = (bf16[4,6,32,256]{3,2,1,0:T(8,128)(2,1)S(1)}, bf16[4,6,32,256]{3,2,1,0:T(8,128)(2,1)S(1)}, u32[]{:S(2)}, u32[]{:S(2)}) collective-permute-start(bf16[4,6,32,256]{3,2,1,0:T(8,128)(2,1)S(1)} %pad_maximum_fusion.8.refs_9_), channel_id=1, source_target_pairs={{0,64},{8,200},{16,80},{24,216},{32,96},{40,232},{48,112},{56,248}... | collective-permute-start | bytes 1179656 | tf_op jit(solution)/shard_map/ppermute | solution.py:24
  44.2 8.0 %collective-permute-done.10.refs_11_ = bf16[4,6,32,256]{3,2,1,0:T(8,128)(2,1)S(1)} collective-permute-done((bf16[4,6,32,256]{3,2,1,0:T(8,128)(2,1)S(1)}, bf16[4,6,32,256]{3,2,1,0:T(8,128)(2,1)S(1)}, u32[]{:S(2)}, u32[]{:S(2)}) %collective-permute-start.10) | collective-permute-done | bytes 393248 | tf_op jit(solution)/shard_map/ppermute | solution.py:24
  52.2 6.4 %collective-permute-done.8.refs_10_ = bf16[4,6,32,256]{3,2,1,0:T(8,128)(2,1)S(1)} collective-permute-done((bf16[4,6,32,256]{3,2,1,0:T(8,128)(2,1)S(1)}, bf16[4,6,32,256]{3,2,1,0:T(8,128)(2,1)S(1)}, u32[]{:S(2)}, u32[]{:S(2)}) %collective-permute-start.8) | collective-permute-done | bytes 393248 | tf_op jit(solution)/shard_map/ppermute | solution.py:24
  65.6 3.9 %fusion.6 = (bf16[3072,512]{1,0:T(8,128)(2,1)}, bf16[512,3072]{0,1:T(8,128)(2,1)S(1)}) fusion(bf16[256,3072]{0,1:T(8,128)(2,1)} %collective-permute-done, bf16[256,3072]{0,1:T(8,128)(2,1)} %copy-done), kind=kLoop, calls=%fused_computation.58 | loop fusion | flops 6291456 | bytes 9437184 | tf_op jit(solution)/shard_map/transpose | solution.py:321
  69.6 3.0 %copy.8.refs_1_ = bf16[512,3072]{1,0:T(8,128)(2,1)} copy(bf16[512,3072]{0,1:T(8,128)(2,1)S(1)} %get-tuple-element.70) | data formatting | bytes 6291456 | tf_op jit(solution)/shard_map/concatenate | solution.py:318
  72.6 4.1 %collective-permute-done.12.refs_12_ = bf16[4,6,32,256]{3,2,1,0:T(8,128)(2,1)} collective-permute-done((bf16[4,6,32,256]{3,2,1,0:T(8,128)(2,1)S(1)}, bf16[4,6,32,256]{3,2,1,0:T(8,128)(2,1)}, u32[]{:S(2)}, u32[]{:S(2)}) %collective-permute-start.12) | collective-permute-done | bytes 393248 | tf_op jit(solution)/shard_map/ppermute | solution.py:24
  76.7 18.6 %shard_map.58 = (bf16[256,768]{1,0:T(8,128)(2,1)}, bf16[256,768]{1,0:T(8,128)(2,1)}, bf16[3,512,256]{2,1,0:T(8,128)(2,1)}, bf16[3,512,256]{2,1,0:T(8,128)(2,1)},...) custom-call(s32[3]{0:T(128)} %pad_add_fusion.refs_0_, ...), custom_call_target="tpu_custom_call" | custom-call | flops 7247757312 | bytes 12582912 | tf_op jit(solution)/shard_map/pallas_call | solution.py:195
  99.8 3.0 %add_convert_fusion = bf16[8,256,384]{2,1,0:T(8,128)(2,1)} fusion(bf16[8,256,384]{2,1,0:T(8,128)(2,1)S(1)} %collective-permute-done.16, bf16[8,256,384]{2,1,0:T(8,128)(2,1)} %get-tuple-element.50), kind=kLoop, calls=%fused_computation.1 | loop fusion | flops 3145728 | bytes 4718592 | tf_op jit(solution)/shard_map/convert_element_type | solution.py:301
  102.8 16.7 %collective-permute-done.15 = bf16[3,512,256]{2,1,0:T(8,128)(2,1)S(1)} collective-permute-done((bf16[3,512,256]{2,1,0:T(8,128)(2,1)}, bf16[3,512,256]{2,1,0:T(8,128)(2,1)S(1)}, u32[]{:S(2)}, u32[]{:S(2)}) %collective-permute-start.15) | collective-permute-done | bytes 786464 | tf_op jit(solution)/shard_map/ppermute | solution.py:24
  124.2 4.3 %collective-permute-start.18 = (bf16[2,512,256]{2,1,0:T(8,128)(2,1)S(1)}, bf16[2,512,256]{2,1,0:T(8,128)(2,1)}, u32[]{:S(2)}, u32[]{:S(2)}) collective-permute-start(bf16[2,512,256]{2,1,0:T(8,128)(2,1)S(1)} %add_convert_fusion.2), channel_id=1, source_target_pairs={{0,64},{8,200},{16,80},{24,216},{32,96},{40,232},{48,112},{56,248}... | collective-permute-start | bytes 1572872 | tf_op jit(solution)/shard_map/ppermute | solution.py:24
  128.5 12.4 %collective-permute-done.18 = bf16[2,512,256]{2,1,0:T(8,128)(2,1)} collective-permute-done((bf16[2,512,256]{2,1,0:T(8,128)(2,1)S(1)}, bf16[2,512,256]{2,1,0:T(8,128)(2,1)}, u32[]{:S(2)}, u32[]{:S(2)}) %collective-permute-start.18) | collective-permute-done | bytes 524320 | tf_op jit(solution)/shard_map/ppermute | solution.py:24
  145.0 5.6 %collective-permute-done.20 = bf16[512,256]{1,0:T(8,128)(2,1)S(1)} collective-permute-done((bf16[512,256]{1,0:T(8,128)(2,1)S(1)}, bf16[512,256]{1,0:T(8,128)(2,1)S(1)}, u32[]{:S(2)}, u32[]{:S(2)}) %collective-permute-start.20) | collective-permute-done | bytes 262176 | tf_op jit(solution)/shard_map/ppermute | solution.py:24
  150.6 7.8 %collective-permute-done.19 = bf16[2,512,256]{2,1,0:T(8,128)(2,1)} collective-permute-done((bf16[2,512,256]{2,1,0:T(8,128)(2,1)}, bf16[2,512,256]{2,1,0:T(8,128)(2,1)}, u32[]{:S(2)}, u32[]{:S(2)}) %collective-permute-start.19) | collective-permute-done | bytes 524320 | tf_op jit(solution)/shard_map/ppermute | solution.py:24
  163.4 4.0 %collective-permute-start.13 = (bf16[256,768]{1,0:T(8,128)(2,1)S(1)}, bf16[256,768]{1,0:T(8,128)(2,1)S(1)}, u32[]{:S(2)}, u32[]{:S(2)}) collective-permute-start(bf16[256,768]{1,0:T(8,128)(2,1)S(1)} %copy-done.14), channel_id=1, source_target_pairs={{0,8},{8,0},{16,24},{24,16},{32,40},{40,32},{48,56},{56,48},{64,72... | collective-permute-start | bytes 1179656 | tf_op jit(solution)/shard_map/ppermute | solution.py:24
  172.4 3.4 %collective-permute-start.24 = (bf16[512,256]{1,0:T(8,128)(2,1)S(1)}, bf16[512,256]{1,0:T(8,128)(2,1)S(1)}, u32[]{:S(2)}, u32[]{:S(2)}) collective-permute-start(bf16[512,256]{1,0:T(8,128)(2,1)S(1)} %get-tuple-element.65), channel_id=1, source_target_pairs={{0,8},{8,0},{16,24},{24,16},{32,40},{40,32},{48,56},{56,48},{64,72... | collective-permute-start | bytes 786440 | tf_op jit(solution)/shard_map/ppermute | solution.py:24
  177.2 3.5 %shard_map.59 = bf16[32,16,512]{2,1,0:T(8,128)(2,1)} custom-call(bf16[512,256]{1,0:T(8,128)(2,1)S(1)} %get-tuple-element.86.g0_ref, bf16[512,256]{1,0:T(8,128)(2,1)S(1)} %get-tuple-element.85.g1_ref), custom_call_target="tpu_custom_call" | custom-call | tf_op jit(solution)/shard_map/pallas_call | solution.py:265
  180.7 7.1 %all-to-all-start = ((bf16[32,16,512]{2,1,0:T(8,128)(2,1)}), bf16[32,16,512]{2,1,0:T(8,128)(2,1)S(1)}, u32[]{:S(2)}, u32[]{:S(2)}) async-start(bf16[32,16,512]{2,1,0:T(8,128)(2,1)} %shard_map.59), calls=%async_computation.1 | async-start | bytes 1048576 | tf_op jit(solution)/shard_map/all_to_all | solution.py:416
  191.3 14.5 %all-to-all-done.in_ref = bf16[32,16,512]{2,1,0:T(8,128)(2,1)S(1)} async-done(((bf16[32,16,512]{2,1,0:T(8,128)(2,1)}), bf16[32,16,512]{2,1,0:T(8,128)(2,1)S(1)}, u32[]{:S(2)}, u32[]{:S(2)}) %all-to-all-start) | async-done | bytes 524320 | tf_op jit(solution)/shard_map/all_to_all | solution.py:416
  (105 shorter events, 48.0 us)
Async XLA Ops:
  7.2 155.0 %reduce-scatter.2.cloned.1.call-start = ((), (), s32[]{:S(2)}) async-start(), calls=%async_computation.2 | async-start | bytes 1966080 | tf_op jit(solution)/shard_map/reduce_scatter | solution.py:388
  12.6 9.2 %collective-permute-start.3 = (bf16[6,32,512]{2,1,0:T(8,128)(2,1)S(1)}, bf16[6,32,512]{2,1,0:T(8,128)(2,1)S(1)}, u32[]{:S(2)}, u32[]{:S(2)}) collective-permute-start(bf16[6,32,512]{2,1,0:T(8,128)(2,1)S(1)} %fusion.5), channel_id=1, source_target_pairs={{0,64},{8,200},{16,80},{24,216},{32,96},{40,232},{48,112},{56,248}... | collective-permute-start | bytes 589832 | tf_op jit(solution)/shard_map/ppermute | solution.py:24
  17.0 4.8 %collective-permute-start.4 = (bf16[6,32,256]{2,1,0:T(8,128)(2,1)S(1)}, bf16[6,32,256]{2,1,0:T(8,128)(2,1)S(1)}, u32[]{:S(2)}, u32[]{:S(2)}) collective-permute-start(bf16[6,32,256]{2,1,0:T(8,128)(2,1)S(1)} %pad_maximum_fusion.12), channel_id=1, source_target_pairs={{0,16},{8,56},{16,0},{24,40},{32,48},{40,24},{48,32},{56,8},{64,80... | collective-permute-start | bytes 294920 | tf_op jit(solution)/shard_map/ppermute | solution.py:24
  22.6 11.9 %collective-permute-start.5 = (bf16[2,6,32,512]{3,2,1,0:T(8,128)(2,1)S(1)}, bf16[2,6,32,512]{3,2,1,0:T(8,128)(2,1)}, u32[]{:S(2)}, u32[]{:S(2)}) collective-permute-start(bf16[2,6,32,512]{3,2,1,0:T(8,128)(2,1)S(1)} %pad_maximum_fusion.7), channel_id=1, source_target_pairs={{0,192},{8,72},{16,208},{24,88},{32,224},{40,104},{48,240},{56,120... | collective-permute-start | bytes 1179656 | tf_op jit(solution)/shard_map/ppermute | solution.py:24
  24.1 6.8 %collective-permute-start.6 = (bf16[2,6,32,256]{3,2,1,0:T(8,128)(2,1)}, bf16[2,6,32,256]{3,2,1,0:T(8,128)(2,1)}, u32[]{:S(2)}, u32[]{:S(2)}) collective-permute-start(bf16[2,6,32,256]{3,2,1,0:T(8,128)(2,1)} %pad_maximum_fusion.9), channel_id=1, source_target_pairs={{0,48},{8,24},{16,32},{24,8},{32,16},{40,56},{48,0},{56,40},{64,11... | collective-permute-start | bytes 589832 | tf_op jit(solution)/shard_map/ppermute | solution.py:24
  26.1 39.5 %collective-permute-start = (bf16[256,3072]{0,1:T(8,128)(2,1)S(1)}, bf16[256,3072]{0,1:T(8,128)(2,1)}, u32[]{:S(2)}, u32[]{:S(2)}) collective-permute-start(bf16[256,3072]{0,1:T(8,128)(2,1)S(1)} %copy.7), channel_id=1, source_target_pairs={{0,8},{8,0},{16,24},{24,16},{32,40},{40,32},{48,56},{56,48},{64,72... | collective-permute-start | bytes 4718600 | tf_op jit(solution)/shard_map/ppermute | solution.py:24
  36.8 21.9 %collective-permute-start.7 = (bf16[4,6,32,512]{3,2,1,0:T(8,128)(2,1)S(1)}, bf16[4,6,32,512]{3,2,1,0:T(8,128)(2,1)}, u32[]{:S(2)}, u32[]{:S(2)}) collective-permute-start(bf16[4,6,32,512]{3,2,1,0:T(8,128)(2,1)S(1)} %pad_maximum_fusion.1.refs_5_), channel_id=1, source_target_pairs={{0,16},{8,56},{16,0},{24,40},{32,48},{40,24},{48,32},{56,8},{64,80... | collective-permute-start | bytes 2359304 | tf_op jit(solution)/shard_map/ppermute | solution.py:24
  39.8 19.2 %collective-permute-start.9 = (bf16[4,6,32,512]{3,2,1,0:T(8,128)(2,1)S(1)}, bf16[4,6,32,512]{3,2,1,0:T(8,128)(2,1)S(1)}, u32[]{:S(2)}, u32[]{:S(2)}) collective-permute-start(bf16[4,6,32,512]{3,2,1,0:T(8,128)(2,1)S(1)} %pad_maximum_fusion.1.refs_5_), channel_id=1, source_target_pairs={{0,48},{8,24},{16,32},{24,8},{32,16},{40,56},{48,0},{56,40},{64,11... | collective-permute-start | bytes 2359304 | tf_op jit(solution)/shard_map/ppermute | solution.py:24
  39.8 12.4 %collective-permute-start.10 = (bf16[4,6,32,256]{3,2,1,0:T(8,128)(2,1)S(1)}, bf16[4,6,32,256]{3,2,1,0:T(8,128)(2,1)S(1)}, u32[]{:S(2)}, u32[]{:S(2)}) collective-permute-start(bf16[4,6,32,256]{3,2,1,0:T(8,128)(2,1)S(1)} %pad_maximum_fusion.8.refs_9_), channel_id=1, source_target_pairs={{0,192},{8,72},{16,208},{24,88},{32,224},{40,104},{48,240},{56,120... | collective-permute-start | bytes 1179656 | tf_op jit(solution)/shard_map/ppermute | solution.py:24
  41.4 17.3 %collective-permute-start.8 = (bf16[4,6,32,256]{3,2,1,0:T(8,128)(2,1)S(1)}, bf16[4,6,32,256]{3,2,1,0:T(8,128)(2,1)S(1)}, u32[]{:S(2)}, u32[]{:S(2)}) collective-permute-start(bf16[4,6,32,256]{3,2,1,0:T(8,128)(2,1)S(1)} %pad_maximum_fusion.8.refs_9_), channel_id=1, source_target_pairs={{0,64},{8,200},{16,80},{24,216},{32,96},{40,232},{48,112},{56,248}... | collective-permute-start | bytes 1179656 | tf_op jit(solution)/shard_map/ppermute | solution.py:24
  59.0 17.7 %collective-permute-start.11 = (bf16[4,6,32,512]{3,2,1,0:T(8,128)(2,1)}, bf16[4,6,32,512]{3,2,1,0:T(8,128)(2,1)}, u32[]{:S(2)}, u32[]{:S(2)}) collective-permute-start(bf16[4,6,32,512]{3,2,1,0:T(8,128)(2,1)} %collective-permute-done.7.refs_6_), channel_id=1, source_target_pairs={{0,48},{8,24},{16,32},{24,8},{32,16},{40,56},{48,0},{56,40},{64,11... | collective-permute-start | bytes 2359304 | tf_op jit(solution)/shard_map/ppermute | solution.py:24
  62.3 10.3 %collective-permute-start.1 = (bf16[256,768]{1,0:T(8,128)(2,1)}, bf16[256,768]{1,0:T(8,128)(2,1)}, u32[]{:S(2)}, u32[]{:S(2)}) collective-permute-start(bf16[256,768]{1,0:T(8,128)(2,1)} %pad_maximum_fusion.6), channel_id=1, source_target_pairs={{0,8},{8,0},{16,24},{24,16},{32,40},{40,32},{48,56},{56,48},{64,72... | collective-permute-start | bytes 1179656 | tf_op jit(solution)/shard_map/ppermute | solution.py:24
  65.6 11.1 %collective-permute-start.12 = (bf16[4,6,32,256]{3,2,1,0:T(8,128)(2,1)S(1)}, bf16[4,6,32,256]{3,2,1,0:T(8,128)(2,1)}, u32[]{:S(2)}, u32[]{:S(2)}) collective-permute-start(bf16[4,6,32,256]{3,2,1,0:T(8,128)(2,1)S(1)} %collective-permute-done.8.refs_10_), channel_id=1, source_target_pairs={{0,192},{8,72},{16,208},{24,88},{32,224},{40,104},{48,240},{56,120... | collective-permute-start | bytes 1179656 | tf_op jit(solution)/shard_map/ppermute | solution.py:24
  96.6 23.0 %collective-permute-start.14 = (bf16[6,512,256]{2,1,0:T(8,128)(2,1)}, bf16[6,512,256]{2,1,0:T(8,128)(2,1)S(1)}, u32[]{:S(2)}, u32[]{:S(2)}) collective-permute-start(bf16[6,512,256]{2,1,0:T(8,128)(2,1)} %get-tuple-element.48), channel_id=1, source_target_pairs={{0,48},{8,24},{16,32},{24,8},{32,16},{40,56},{48,0},{56,40},{64,11... | collective-permute-start | bytes 4718600 | tf_op jit(solution)/shard_map/ppermute | solution.py:24
  98.9 20.7 %collective-permute-start.15 = (bf16[3,512,256]{2,1,0:T(8,128)(2,1)}, bf16[3,512,256]{2,1,0:T(8,128)(2,1)S(1)}, u32[]{:S(2)}, u32[]{:S(2)}) collective-permute-start(bf16[3,512,256]{2,1,0:T(8,128)(2,1)} %get-tuple-element.49), channel_id=1, source_target_pairs={{0,192},{8,72},{16,208},{24,88},{32,224},{40,104},{48,240},{56,120... | collective-permute-start | bytes 2359304 | tf_op jit(solution)/shard_map/ppermute | solution.py:24
  124.0 16.9 %collective-permute-start.17 = (bf16[3,512,256]{2,1,0:T(8,128)(2,1)}, bf16[3,512,256]{2,1,0:T(8,128)(2,1)}, u32[]{:S(2)}, u32[]{:S(2)}) collective-permute-start(bf16[3,512,256]{2,1,0:T(8,128)(2,1)} %add_convert_fusion.1), channel_id=1, source_target_pairs={{0,16},{8,56},{16,0},{24,40},{32,48},{40,24},{48,32},{56,8},{64,80... | collective-permute-start | bytes 2359304 | tf_op jit(solution)/shard_map/ppermute | solution.py:24
  124.2 16.7 %collective-permute-start.18 = (bf16[2,512,256]{2,1,0:T(8,128)(2,1)S(1)}, bf16[2,512,256]{2,1,0:T(8,128)(2,1)}, u32[]{:S(2)}, u32[]{:S(2)}) collective-permute-start(bf16[2,512,256]{2,1,0:T(8,128)(2,1)S(1)} %add_convert_fusion.2), channel_id=1, source_target_pairs={{0,64},{8,200},{16,80},{24,216},{32,96},{40,232},{48,112},{56,248}... | collective-permute-start | bytes 1572872 | tf_op jit(solution)/shard_map/ppermute | solution.py:24
  143.2 15.1 %collective-permute-start.19 = (bf16[2,512,256]{2,1,0:T(8,128)(2,1)}, bf16[2,512,256]{2,1,0:T(8,128)(2,1)}, u32[]{:S(2)}, u32[]{:S(2)}) collective-permute-start(bf16[2,512,256]{2,1,0:T(8,128)(2,1)} %pad_maximum_fusion.4), channel_id=1, source_target_pairs={{0,192},{8,72},{16,208},{24,88},{32,224},{40,104},{48,240},{56,120... | collective-permute-start | bytes 1572872 | tf_op jit(solution)/shard_map/ppermute | solution.py:24
  144.9 5.7 %collective-permute-start.20 = (bf16[512,256]{1,0:T(8,128)(2,1)S(1)}, bf16[512,256]{1,0:T(8,128)(2,1)S(1)}, u32[]{:S(2)}, u32[]{:S(2)}) collective-permute-start(bf16[512,256]{1,0:T(8,128)(2,1)S(1)} %fusion.3), channel_id=1, source_target_pairs={{0,48},{8,24},{16,32},{24,8},{32,16},{40,56},{48,0},{56,40},{64,11... | collective-permute-start | bytes 786440 | tf_op jit(solution)/shard_map/ppermute | solution.py:24
  158.4 8.9 %collective-permute-start.22 = (bf16[512,256]{1,0:T(8,128)(2,1)S(1)}, bf16[512,256]{1,0:T(8,128)(2,1)S(1)}, u32[]{:S(2)}, u32[]{:S(2)}) collective-permute-start(bf16[512,256]{1,0:T(8,128)(2,1)S(1)} %fusion.1), channel_id=1, source_target_pairs={{0,16},{8,56},{16,0},{24,40},{32,48},{40,24},{48,32},{56,8},{64,80... | collective-permute-start | bytes 786440 | tf_op jit(solution)/shard_map/ppermute | solution.py:24
  159.8 10.0 %collective-permute-start.21 = (bf16[512,256]{1,0:T(8,128)(2,1)S(1)}, bf16[512,256]{1,0:T(8,128)(2,1)S(1)}, u32[]{:S(2)}, u32[]{:S(2)}) collective-permute-start(bf16[512,256]{1,0:T(8,128)(2,1)S(1)} %fusion.4), channel_id=1, source_target_pairs={{0,64},{8,200},{16,80},{24,216},{32,96},{40,232},{48,112},{56,248}... | collective-permute-start | bytes 786440 | tf_op jit(solution)/shard_map/ppermute | solution.py:24
  163.2 7.8 %collective-permute-start.23 = (bf16[256,384]{1,0:T(8,128)(2,1)S(1)}, bf16[256,384]{1,0:T(8,128)(2,1)S(1)}, u32[]{:S(2)}, u32[]{:S(2)}) collective-permute-start(bf16[256,384]{1,0:T(8,128)(2,1)S(1)} %select_bitcast_fusion), channel_id=1, source_target_pairs={{0,1},{1,0},{2,3},{3,2},{4,5},{5,4},{6,7},{7,6},{8,9},{9,8},{10,11... | collective-permute-start | bytes 589832 | tf_op jit(solution)/shard_map/ppermute | solution.py:392
  163.4 12.5 %collective-permute-start.13 = (bf16[256,768]{1,0:T(8,128)(2,1)S(1)}, bf16[256,768]{1,0:T(8,128)(2,1)S(1)}, u32[]{:S(2)}, u32[]{:S(2)}) collective-permute-start(bf16[256,768]{1,0:T(8,128)(2,1)S(1)} %copy-done.14), channel_id=1, source_target_pairs={{0,8},{8,0},{16,24},{24,16},{32,40},{40,32},{48,56},{56,48},{64,72... | collective-permute-start | bytes 1179656 | tf_op jit(solution)/shard_map/ppermute | solution.py:24
  180.7 25.0 %all-to-all-start = ((bf16[32,16,512]{2,1,0:T(8,128)(2,1)}), bf16[32,16,512]{2,1,0:T(8,128)(2,1)S(1)}, u32[]{:S(2)}, u32[]{:S(2)}) async-start(bf16[32,16,512]{2,1,0:T(8,128)(2,1)} %shard_map.59), calls=%async_computation.1 | async-start | bytes 1048576 | tf_op jit(solution)/shard_map/all_to_all | solution.py:416
  (20 other events, 224.6 us)
Sparse Core Ops, SparseCore 0:
  119.7 27.2 reduce-scatter.1

commit v2 on v1

--- a/solution.py
+++ b/solution.py
@@ -61,21 +61,24 @@
 
 def main_kernel(scale, pos, tok_h, tok_t_h, cot0_h, cot1_h, *refs):
     pieces, refs = refs[:8], refs[8:]
-    act0, act1, keep0, keep1, send, q_keep, q_send, ig_own, ig_other = refs[:9]
-    tok, tok_t, w, cot, v, slope_ref, stage, ig, sem_w, sem_in, sem_out, sem_ig = refs[9:]
+    act0, act1, keep0, keep1, send0, send1, q_keep, q_send, ig_own, ig_other = refs[:10]
+    tok, tok_t, w, cot, v, slope_ref, stage, ig, sem_w, sem_in, sem_out, sem_ig = refs[10:]
     rows, wide = w.shape[0], w.shape[3]
     tokens = tok.shape[0]
     half, mid = tokens // 2, rows * S // 2
     y, z, core = pos[0], pos[1], pos[2]
     copy = pltpu.make_async_copy
+    split = rows // 2
     w_copies = []
-    for part, large, lo in ((0, "y", 0), (1, "z", wide - HALF)):
-        chips = chips_of(pos, large)
-        for i in range(4):
-            piece = pieces[4 * part + i]
-            for k in range(4):
-                to = w.at[:, chips[i][k], :, pl.ds(lo, piece.shape[3])]
-                w_copies.append(copy(piece.at[k], to, sem_w.at[16 * part + 4 * i + k]))
+    for side in (0, 1):
+        some = pl.ds(side * split, split)
+        for part, large, lo in ((0, "y", 0), (1, "z", wide - HALF)):
+            chips = chips_of(pos, large)
+            for i in range(4):
+                piece = pieces[4 * part + i]
+                for k in range(4):
+                    to = w.at[some, chips[i][k], :, pl.ds(lo, piece.shape[3])]
+                    w_copies.append(copy(piece.at[k, some], to, sem_w.at[len(w_copies)]))
     in_copies = [
         copy(tok_h.at[:, pl.ds(n * mid, mid)], tok.at[:, pl.ds(n * mid, mid)], sem_in.at[n])
         for n in (0, 1)
@@ -85,15 +88,15 @@
     for b in range(rows):
         here = pl.ds(b * S, S)
         in_copies.append(copy(tok_t_h.at[here], tok_t.at[here], sem_in.at[4 + b]))
-    for item in w_copies + in_copies:
+    for item in w_copies[:32] + in_copies[:1] + w_copies[32:] + in_copies[1:]:
         item.start()
-    for item in w_copies:
+    for item in w_copies[:32] + in_copies[:1]:
         item.wait()
-    in_copies[0].wait()
     first = jnp.dot(
         tok[:, :mid], w[: rows // 2].reshape(mid, wide), preferred_element_type=jnp.float32
     )
-    in_copies[1].wait()
+    for item in w_copies[32:] + in_copies[1:2]:
+        item.wait()
     v[...] = first + jnp.dot(
         tok[:, mid:], w[rows // 2 :].reshape(mid, wide), preferred_element_type=jnp.float32
     )
@@ -121,33 +124,6 @@
     gelu(act0, 0)
     gelu(act1, half)
 
-    def send_off(block, ref, slot, when):
-        @pl.when(when)
-        def _():
-            copy(stage.at[block], ref.at[slot], sem_out.at[block]).start()
-
-    sy = 1 - 2 * lax.rem(y + core, 2)
-    sz = 1 - 2 * lax.rem(z + core, 2)
-    other = lax.rem(z + sz + NZ, NZ)
-    for b in range(rows):
-        in_copies[4 + b].wait()
-        g = jnp.dot(tok_t[b * S : (b + 1) * S], slope_ref[...], preferred_element_type=jnp.float32)
-        g = (g * scale).astype(jnp.bfloat16)
-        for j in range(wide // HALF):
-            block = j * rows + b
-            stage[block] = g[:, j * HALF : (j + 1) * HALF]
-            place, m = block // 3, block % 3
-            if j < 2:
-                step = lax.rem(place - y + NY, NY)
-                send_off(block, keep0, m, step == 0)
-                send_off(block, keep1, m, step == lax.rem(sy + NY, NY))
-                send_off(block, send, m, step == lax.rem(NY - sy, NY))
-                send_off(block, send, 3 + m, step == 2)
-            else:
-                to = 2 * (b // 3) + m // 2
-                mine = jnp.logical_or(to == z, to == other)
-                send_off(block, q_keep, m, mine)
-                send_off(block, q_send, m, jnp.logical_not(mine))
     parts, width = ig.shape[1], ig.shape[3]
     ig_copies = []
     for b in range(rows):
@@ -174,6 +150,34 @@
                     copy(ig.at[side, span], ref.at[span], sem_ig.at[len(ig_copies)])
                 )
                 ig_copies[-1].start()
+
+    def send_off(block, ref, slot, when):
+        @pl.when(when)
+        def _():
+            copy(stage.at[block], ref.at[slot], sem_out.at[block]).start()
+
+    sy = 1 - 2 * lax.rem(y + core, 2)
+    sz = 1 - 2 * lax.rem(z + core, 2)
+    other = lax.rem(z + sz + NZ, NZ)
+    for b in range(rows):
+        in_copies[4 + b].wait()
+        g = jnp.dot(tok_t[b * S : (b + 1) * S], slope_ref[...], preferred_element_type=jnp.float32)
+        g = (g * scale).astype(jnp.bfloat16)
+        for j in range(wide // HALF):
+            block = j * rows + b
+            stage[block] = g[:, j * HALF : (j + 1) * HALF]
+            place, m = block // 3, block % 3
+            if j < 2:
+                step = lax.rem(place - y + NY, NY)
+                send_off(block, keep0, m, step == 0)
+                send_off(block, keep1, m, step == lax.rem(sy + NY, NY))
+                send_off(block, send0, m, step == lax.rem(NY - sy, NY))
+                send_off(block, send1, m, step == 2)
+            else:
+                to = 2 * (b // 3) + m // 2
+                mine = jnp.logical_or(to == z, to == other)
+                send_off(block, q_keep, m, mine)
+                send_off(block, q_send, m, jnp.logical_not(mine))
     for block in range(rows * wide // HALF):
         copy(stage.at[block], keep0.at[0], sem_out.at[block]).wait()
     for item in ig_copies:
@@ -188,7 +192,7 @@
     vmem = pl.BlockSpec(memory_space=pltpu.VMEM)
     hbm = pl.BlockSpec(memory_space=pltpu.HBM)
     share = (rows, CHIPS, S // CHIPS, wide)
-    sums = [shape(n, S, HALF) for n in (3, 3, 6, 3, 3)]
+    sums = [shape(n, S, HALF) for n in (3,) * 6]
     cut = (parts, tokens // 2, rows * S // parts)
     outs = [shape(tokens // 2, wide), shape(tokens // 2, wide)] + sums + [shape(*cut)] * 2
     held = lambda dims, dtype=jnp.bfloat16: pltpu.VMEM(dims, dtype)
@@ -206,7 +210,7 @@
             held((tokens, wide)),
             held((blocks, S, HALF)),
             held((2, *cut)),
-            pltpu.SemaphoreType.DMA((32,)),
+            pltpu.SemaphoreType.DMA((64,)),
             pltpu.SemaphoreType.DMA((4 + rows,)),
             pltpu.SemaphoreType.DMA((blocks,)),
             pltpu.SemaphoreType.DMA((4,)),
@@ -332,14 +336,10 @@
             )
         )
     )
-    fours = together(
-        tuple(
-            jnp.concatenate([two, got])
-            for two, got in zip(
-                twos, together(tuple(exchange(x, p[0], 2) for x, p in zip(twos, plan)))
-            )
-        )
-    )
+    *got, c_mine, c_recv = together(
+        tuple(exchange(x, p[0], 2) for x, p in zip(twos, plan)) + (c_mine, c_recv)
+    )
+    fours = together(tuple(jnp.concatenate([two, x]) for two, x in zip(twos, got)))
     got1 = together(
         tuple(exchange(x, p[1], step) for step in (1, 2) for x, p in zip(fours, plan))
     )
@@ -350,11 +350,13 @@
     act0, act1, *grads, ig_own, ig_other = main_part(
         parts, scale, pos, tok, tok_t, c_mine, c_recv, pieces
     )
-    keep0, keep1, send, q_keep, q_send = grads
+    keep0, keep1, send0, send1, q_keep, q_send = grads
     y, z = pos[0], pos[1]
     z_even = z % 2 == 0
     ig_sum = cast(wide32(ig_own) + wide32(swap_cores(ig_other)))
-    got, q_got, ig_sum = together((exchange(send, "y", 2), exchange(q_send, "z", 2), ig_sum))
+    got1, got, q_got, ig_sum = together(
+        (exchange(send1, "y", 2), exchange(send0, "y", 2), exchange(q_send, "z", 2), ig_sum)
+    )
 
     def q_pick(keep, got, pair):
         both = lambda array: jnp.where(pair, array[:2], jnp.stack([array[2], array[2]]))
@@ -362,7 +364,7 @@
 
     got2, q_got2 = together(
         (
-            exchange(cast(wide32(keep1) + wide32(got[3:])), "y", 1),
+            exchange(cast(wide32(keep1) + wide32(got1)), "y", 1),
             exchange(cast(q_pick(q_keep, q_got, jnp.logical_not(z_even))), "z", 1),
         )
     )
@@ -375,12 +377,8 @@
     sz = 1 - 2 * ((z + core) % 2)
     y_pair = jnp.where(y % 2 == 0, y, (y + 1 - 2 * ((y + core) % 2) + NY) % NY)
     q_two = q_pick(q_keep, q_got, z_even) + wide32(q_got2)
-    got3, q_got3 = together(
-        (
-            exchange(jnp.stack([cast(p_slot(-sz)), cast(p_slot(2))]), "z", 2),
-            exchange(cast(jnp.where(y_pair == 0, q_two[1], q_two[0])), "y", 2),
-        )
-    )
+    got3 = exchange(jnp.stack([cast(p_slot(-sz)), cast(p_slot(2))]), "z", 2)
+    q_got3 = exchange(cast(jnp.where(y_pair == 0, q_two[1], q_two[0])), "y", 2)
     q_half = cast(jnp.where(y_pair == 0, q_two[0], q_two[1]) + wide32(q_got3))
 
     low = parts // NX

time: 214 us -> 211 us (0.986)
  waiting for transfers between devices: 87.4 us -> 75.5 us
  starting transfers between devices: 56 us -> 62.7 us
  other arithmetic: 26.6 us -> 29.5 us
    ppermute x24 -> x25, waiting for transfers between devices: 71.6 us -> 62.1 us  [moved(): return lax.ppermute(array, 'dp', pairs)]
    ppermute x24 -> x25, starting transfers between devices: 48.8 us -> 56.5 us  [moved(): return lax.ppermute(array, 'dp', pairs)]
    all_to_all x1, starting transfers between devices: 7.05 us -> 4.73 us  [local(): arrived = lax.all_to_all(result, 'dp', 0, 0, tiled=True)]
  transfers between devices with their start and end apart: 27 -> 28, of which waited for: 16 -> 15; matrix products, arithmetic and copies ran while one was open for 13% -> 15% of each run, Pallas kernels for 0% -> 0%
where the time goes in v2:
time: 211 us; the launch traced here: 210 us
  waiting for transfers between devices  75.5 us (36%)
  starting transfers between devices  62.7 us (30%)
  other arithmetic  29.5 us (14%)
  Pallas kernels  23.4 us (11%)
  between operations  14.4 us (7%)
  local copies, waits for them, and re-layouts  4.69 us (2%)
    ppermute x25, waiting for transfers between devices, moved(): return lax.ppermute(array, 'dp', pairs)  62.1 us
    ppermute x25, starting transfers between devices, moved(): return lax.ppermute(array, 'dp', pairs)  56.5 us
    pallas_call x1, Pallas kernels, main_part(): pl.pallas_call(lambda *refs: main_kernel(scale, *refs), out_shape=outs, i...  19 us
    all_to_all x1, waiting for transfers between devices, local(): arrived = lax.all_to_all(result, 'dp', 0, 0, tiled=True)  13.3 us
    convert_element_type x7, other arithmetic, local(): cast = lambda array: array.astype(jnp.bfloat16)  7.66 us
    all_to_all x1, starting transfers between devices, local(): arrived = lax.all_to_all(result, 'dp', 0, 0, tiled=True)  4.73 us
  transfers between devices with their start and end apart: 28, of which 15 were waited for; matrix products, arithmetic and copies ran while one was open for 15% of the time, Pallas kernels for 0%

profile of v2, /device:TPU:1, one launch (start us, length us, event | category | flops | bytes accessed | tf_op | source)
XLA Modules:
  0.0 210.1 jit_solution(8577697974951703721)
XLA Ops:
  8.2 3.3 %collective-permute-start.1 = (bf16[6,16,768]{2,1,0:T(8,128)(2,1)S(1)}, bf16[6,16,768]{2,1,0:T(8,128)(2,1)S(1)}, u32[]{:S(2)}, u32[]{:S(2)}) collective-permute-start(bf16[6,16,768]{2,1,0:T(8,128)(2,1)S(1)} %pad_maximum_fusion.11), channel_id=1, source_target_pairs={{0,8},{8,0},{16,24},{24,16},{32,40},{40,32},{48,56},{56,48},{64,72... | collective-permute-start | bytes 442376 | tf_op jit(solution)/shard_map/ppermute | solution.py:24
  13.6 4.4 %collective-permute-start.2 = (bf16[6,32,512]{2,1,0:T(8,128)(2,1)S(1)}, bf16[6,32,512]{2,1,0:T(8,128)(2,1)S(1)}, u32[]{:S(2)}, u32[]{:S(2)}) collective-permute-start(bf16[6,32,512]{2,1,0:T(8,128)(2,1)S(1)} %fusion.5), channel_id=1, source_target_pairs={{0,64},{8,200},{16,80},{24,216},{32,96},{40,232},{48,112},{56,248}... | collective-permute-start | bytes 589832 | tf_op jit(solution)/shard_map/ppermute | solution.py:24
  18.0 2.8 %collective-permute-start.3 = (bf16[6,32,256]{2,1,0:T(8,128)(2,1)S(1)}, bf16[6,32,256]{2,1,0:T(8,128)(2,1)S(1)}, u32[]{:S(2)}, u32[]{:S(2)}) collective-permute-start(bf16[6,32,256]{2,1,0:T(8,128)(2,1)S(1)} %pad_maximum_fusion.12), channel_id=1, source_target_pairs={{0,16},{8,56},{16,0},{24,40},{32,48},{40,24},{48,32},{56,8},{64,80... | collective-permute-start | bytes 294920 | tf_op jit(solution)/shard_map/ppermute | solution.py:24
  25.9 2.8 %collective-permute-start = (bf16[256,3072]{0,1:T(8,128)(2,1)S(1)}, bf16[256,3072]{0,1:T(8,128)(2,1)}, u32[]{:S(2)}, u32[]{:S(2)}) collective-permute-start(bf16[256,3072]{0,1:T(8,128)(2,1)S(1)} %copy.7), channel_id=1, source_target_pairs={{0,8},{8,0},{16,24},{24,16},{32,40},{40,32},{48,56},{56,48},{64,72... | collective-permute-start | bytes 4718600 | tf_op jit(solution)/shard_map/ppermute | solution.py:24
  37.8 3.0 %collective-permute-start.7 = (bf16[4,6,32,512]{3,2,1,0:T(8,128)(2,1)S(1)}, bf16[4,6,32,512]{3,2,1,0:T(8,128)(2,1)}, u32[]{:S(2)}, u32[]{:S(2)}) collective-permute-start(bf16[4,6,32,512]{3,2,1,0:T(8,128)(2,1)S(1)} %pad_maximum_fusion.1.refs_5_), channel_id=1, source_target_pairs={{0,16},{8,56},{16,0},{24,40},{32,48},{40,24},{48,32},{56,8},{64,80... | collective-permute-start | bytes 2359304 | tf_op jit(solution)/shard_map/ppermute | solution.py:24
  42.4 2.4 %collective-permute-start.8 = (bf16[4,6,32,256]{3,2,1,0:T(8,128)(2,1)S(1)}, bf16[4,6,32,256]{3,2,1,0:T(8,128)(2,1)}, u32[]{:S(2)}, u32[]{:S(2)}) collective-permute-start(bf16[4,6,32,256]{3,2,1,0:T(8,128)(2,1)S(1)} %pad_maximum_fusion.8.refs_9_), channel_id=1, source_target_pairs={{0,64},{8,200},{16,80},{24,216},{32,96},{40,232},{48,112},{56,248}... | collective-permute-start | bytes 1179656 | tf_op jit(solution)/shard_map/ppermute | solution.py:24
  44.8 11.9 %collective-permute-done.10.refs_11_ = bf16[4,6,32,256]{3,2,1,0:T(8,128)(2,1)S(1)} collective-permute-done((bf16[4,6,32,256]{3,2,1,0:T(8,128)(2,1)S(1)}, bf16[4,6,32,256]{3,2,1,0:T(8,128)(2,1)S(1)}, u32[]{:S(2)}, u32[]{:S(2)}) %collective-permute-start.10) | collective-permute-done | bytes 393248 | tf_op jit(solution)/shard_map/ppermute | solution.py:24
  56.7 3.7 %collective-permute-done.8.refs_10_ = bf16[4,6,32,256]{3,2,1,0:T(8,128)(2,1)} collective-permute-done((bf16[4,6,32,256]{3,2,1,0:T(8,128)(2,1)S(1)}, bf16[4,6,32,256]{3,2,1,0:T(8,128)(2,1)}, u32[]{:S(2)}, u32[]{:S(2)}) %collective-permute-start.8) | collective-permute-done | bytes 393248 | tf_op jit(solution)/shard_map/ppermute | solution.py:24
  63.9 3.9 %fusion.6 = (bf16[3072,512]{1,0:T(8,128)(2,1)}, bf16[512,3072]{0,1:T(8,128)(2,1)S(1)}) fusion(bf16[256,3072]{0,1:T(8,128)(2,1)} %collective-permute-done, bf16[256,3072]{0,1:T(8,128)(2,1)} %copy-done), kind=kLoop, calls=%fused_computation.58 | loop fusion | flops 6291456 | bytes 9437184 | tf_op jit(solution)/shard_map/transpose | solution.py:325
  67.9 3.0 %copy.8.refs_1_ = bf16[512,3072]{1,0:T(8,128)(2,1)} copy(bf16[512,3072]{0,1:T(8,128)(2,1)S(1)} %get-tuple-element.72) | data formatting | bytes 6291456 | tf_op jit(solution)/shard_map/concatenate | solution.py:322
  73.2 19.0 %shard_map.58 = (bf16[256,768]{1,0:T(8,128)(2,1)}, bf16[256,768]{1,0:T(8,128)(2,1)}, bf16[3,512,256]{2,1,0:T(8,128)(2,1)}, bf16[3,512,256]{2,1,0:T(8,128)(2,1)},...) custom-call(s32[3]{0:T(128)} %pad_add_fusion.refs_0_, ...), custom_call_target="tpu_custom_call" | custom-call | flops 7247757312 | bytes 12582912 | tf_op jit(solution)/shard_map/pallas_call | solution.py:199
  92.2 5.3 %collective-permute-start.17 = (bf16[8,256,384]{2,1,0:T(8,128)(2,1)}, bf16[8,256,384]{2,1,0:T(8,128)(2,1)S(1)}, u32[]{:S(2)}, u32[]{:S(2)}) collective-permute-start(bf16[8,256,384]{2,1,0:T(8,128)(2,1)} %get-tuple-element.56), channel_id=1, source_target_pairs={{0,8},{8,0},{16,24},{24,16},{32,40},{40,32},{48,56},{56,48},{64,72... | collective-permute-start | bytes 4718600 | tf_op jit(solution)/shard_map/ppermute | solution.py:24
  101.3 3.0 %add_convert_fusion = bf16[8,256,384]{2,1,0:T(8,128)(2,1)} fusion(bf16[8,256,384]{2,1,0:T(8,128)(2,1)S(1)} %collective-permute-done.17, bf16[8,256,384]{2,1,0:T(8,128)(2,1)} %get-tuple-element.55), kind=kLoop, calls=%fused_computation.1 | loop fusion | flops 3145728 | bytes 4718592 | tf_op jit(solution)/shard_map/convert_element_type | solution.py:305
  104.3 4.7 %collective-permute-done.14 = bf16[3,512,256]{2,1,0:T(8,128)(2,1)} collective-permute-done((bf16[3,512,256]{2,1,0:T(8,128)(2,1)}, bf16[3,512,256]{2,1,0:T(8,128)(2,1)}, u32[]{:S(2)}, u32[]{:S(2)}) %collective-permute-start.14) | collective-permute-done | bytes 786464 | tf_op jit(solution)/shard_map/ppermute | solution.py:24
  109.0 8.3 %collective-permute-done.15 = bf16[3,512,256]{2,1,0:T(8,128)(2,1)S(1)} collective-permute-done((bf16[3,512,256]{2,1,0:T(8,128)(2,1)}, bf16[3,512,256]{2,1,0:T(8,128)(2,1)S(1)}, u32[]{:S(2)}, u32[]{:S(2)}) %collective-permute-start.15) | collective-permute-done | bytes 786464 | tf_op jit(solution)/shard_map/ppermute | solution.py:24
  123.2 4.7 %collective-permute-start.19 = (bf16[2,512,256]{2,1,0:T(8,128)(2,1)S(1)}, bf16[2,512,256]{2,1,0:T(8,128)(2,1)}, u32[]{:S(2)}, u32[]{:S(2)}) collective-permute-start(bf16[2,512,256]{2,1,0:T(8,128)(2,1)S(1)} %add_convert_fusion.2), channel_id=1, source_target_pairs={{0,64},{8,200},{16,80},{24,216},{32,96},{40,232},{48,112},{56,248}... | collective-permute-start | bytes 1572872 | tf_op jit(solution)/shard_map/ppermute | solution.py:24
  127.8 12.3 %collective-permute-done.19 = bf16[2,512,256]{2,1,0:T(8,128)(2,1)} collective-permute-done((bf16[2,512,256]{2,1,0:T(8,128)(2,1)S(1)}, bf16[2,512,256]{2,1,0:T(8,128)(2,1)}, u32[]{:S(2)}, u32[]{:S(2)}) %collective-permute-start.19) | collective-permute-done | bytes 524320 | tf_op jit(solution)/shard_map/ppermute | solution.py:24
  144.2 5.3 %collective-permute-done.22 = bf16[512,256]{1,0:T(8,128)(2,1)S(1)} collective-permute-done((bf16[512,256]{1,0:T(8,128)(2,1)S(1)}, bf16[512,256]{1,0:T(8,128)(2,1)S(1)}, u32[]{:S(2)}, u32[]{:S(2)}) %collective-permute-start.22) | collective-permute-done | bytes 262176 | tf_op jit(solution)/shard_map/ppermute | solution.py:24
  151.3 5.6 %collective-permute-done.20 = bf16[2,512,256]{2,1,0:T(8,128)(2,1)} collective-permute-done((bf16[2,512,256]{2,1,0:T(8,128)(2,1)}, bf16[2,512,256]{2,1,0:T(8,128)(2,1)}, u32[]{:S(2)}, u32[]{:S(2)}) %collective-permute-start.20) | collective-permute-done | bytes 524320 | tf_op jit(solution)/shard_map/ppermute | solution.py:24
  160.7 7.0 %collective-permute-start.13 = (bf16[256,768]{1,0:T(8,128)(2,1)S(1)}, bf16[256,768]{1,0:T(8,128)(2,1)S(1)}, u32[]{:S(2)}, u32[]{:S(2)}) collective-permute-start(bf16[256,768]{1,0:T(8,128)(2,1)S(1)} %copy-done.13), channel_id=1, source_target_pairs={{0,8},{8,0},{16,24},{24,16},{32,40},{40,32},{48,56},{56,48},{64,72... | collective-permute-start | bytes 1179656 | tf_op jit(solution)/shard_map/ppermute | solution.py:24
  169.1 6.9 %collective-permute-start.25 = (bf16[512,256]{1,0:T(8,128)(2,1)S(1)}, bf16[512,256]{1,0:T(8,128)(2,1)S(1)}, u32[]{:S(2)}, u32[]{:S(2)}) collective-permute-start(bf16[512,256]{1,0:T(8,128)(2,1)S(1)} %get-tuple-element.69), channel_id=1, source_target_pairs={{0,8},{8,0},{16,24},{24,16},{32,40},{40,32},{48,56},{56,48},{64,72... | collective-permute-start | bytes 786440 | tf_op jit(solution)/shard_map/ppermute | solution.py:24
  177.2 3.5 %shard_map.59 = bf16[32,16,512]{2,1,0:T(8,128)(2,1)} custom-call(bf16[512,256]{1,0:T(8,128)(2,1)S(1)} %get-tuple-element.90.g0_ref, bf16[512,256]{1,0:T(8,128)(2,1)S(1)} %get-tuple-element.89.g1_ref), custom_call_target="tpu_custom_call" | custom-call | tf_op jit(solution)/shard_map/pallas_call | solution.py:269
  180.8 4.7 %all-to-all-start = ((bf16[32,16,512]{2,1,0:T(8,128)(2,1)}), bf16[32,16,512]{2,1,0:T(8,128)(2,1)S(1)}, u32[]{:S(2)}, u32[]{:S(2)}) async-start(bf16[32,16,512]{2,1,0:T(8,128)(2,1)} %shard_map.59), calls=%async_computation.1 | async-start | bytes 1048576 | tf_op jit(solution)/shard_map/all_to_all | solution.py:414
  189.0 13.3 %all-to-all-done.in_ref = bf16[32,16,512]{2,1,0:T(8,128)(2,1)S(1)} async-done(((bf16[32,16,512]{2,1,0:T(8,128)(2,1)}), bf16[32,16,512]{2,1,0:T(8,128)(2,1)S(1)}, u32[]{:S(2)}, u32[]{:S(2)}) %all-to-all-start) | async-done | bytes 524320 | tf_op jit(solution)/shard_map/all_to_all | solution.py:414
  (103 shorter events, 50.8 us)
Async XLA Ops:
  7.2 151.0 %reduce-scatter.2.cloned.1.call-start = ((), (), s32[]{:S(2)}) async-start(), calls=%async_computation.2 | async-start | bytes 1966080 | tf_op jit(solution)/shard_map/reduce_scatter | solution.py:386
  13.6 9.2 %collective-permute-start.2 = (bf16[6,32,512]{2,1,0:T(8,128)(2,1)S(1)}, bf16[6,32,512]{2,1,0:T(8,128)(2,1)S(1)}, u32[]{:S(2)}, u32[]{:S(2)}) collective-permute-start(bf16[6,32,512]{2,1,0:T(8,128)(2,1)S(1)} %fusion.5), channel_id=1, source_target_pairs={{0,64},{8,200},{16,80},{24,216},{32,96},{40,232},{48,112},{56,248}... | collective-permute-start | bytes 589832 | tf_op jit(solution)/shard_map/ppermute | solution.py:24
  21.6 10.1 %collective-permute-start.6 = (bf16[256,768]{1,0:T(8,128)(2,1)}, bf16[256,768]{1,0:T(8,128)(2,1)}, u32[]{:S(2)}, u32[]{:S(2)}) collective-permute-start(bf16[256,768]{1,0:T(8,128)(2,1)} %pad_maximum_fusion.7), channel_id=1, source_target_pairs={{0,8},{8,0},{16,24},{24,16},{32,40},{40,32},{48,56},{56,48},{64,72... | collective-permute-start | bytes 1179656 | tf_op jit(solution)/shard_map/ppermute | solution.py:24
  23.6 12.0 %collective-permute-start.4 = (bf16[2,6,32,512]{3,2,1,0:T(8,128)(2,1)S(1)}, bf16[2,6,32,512]{3,2,1,0:T(8,128)(2,1)}, u32[]{:S(2)}, u32[]{:S(2)}) collective-permute-start(bf16[2,6,32,512]{3,2,1,0:T(8,128)(2,1)S(1)} %pad_maximum_fusion.5), channel_id=1, source_target_pairs={{0,192},{8,72},{16,208},{24,88},{32,224},{40,104},{48,240},{56,120... | collective-permute-start | bytes 1179656 | tf_op jit(solution)/shard_map/ppermute | solution.py:24
  25.9 38.1 %collective-permute-start = (bf16[256,3072]{0,1:T(8,128)(2,1)S(1)}, bf16[256,3072]{0,1:T(8,128)(2,1)}, u32[]{:S(2)}, u32[]{:S(2)}) collective-permute-start(bf16[256,3072]{0,1:T(8,128)(2,1)S(1)} %copy.7), channel_id=1, source_target_pairs={{0,8},{8,0},{16,24},{24,16},{32,40},{40,32},{48,56},{56,48},{64,72... | collective-permute-start | bytes 4718600 | tf_op jit(solution)/shard_map/ppermute | solution.py:24
  37.8 22.6 %collective-permute-start.7 = (bf16[4,6,32,512]{3,2,1,0:T(8,128)(2,1)S(1)}, bf16[4,6,32,512]{3,2,1,0:T(8,128)(2,1)}, u32[]{:S(2)}, u32[]{:S(2)}) collective-permute-start(bf16[4,6,32,512]{3,2,1,0:T(8,128)(2,1)S(1)} %pad_maximum_fusion.1.refs_5_), channel_id=1, source_target_pairs={{0,16},{8,56},{16,0},{24,40},{32,48},{40,24},{48,32},{56,8},{64,80... | collective-permute-start | bytes 2359304 | tf_op jit(solution)/shard_map/ppermute | solution.py:24
  40.8 19.6 %collective-permute-start.9 = (bf16[4,6,32,512]{3,2,1,0:T(8,128)(2,1)S(1)}, bf16[4,6,32,512]{3,2,1,0:T(8,128)(2,1)S(1)}, u32[]{:S(2)}, u32[]{:S(2)}) collective-permute-start(bf16[4,6,32,512]{3,2,1,0:T(8,128)(2,1)S(1)} %pad_maximum_fusion.1.refs_5_), channel_id=1, source_target_pairs={{0,48},{8,24},{16,32},{24,8},{32,16},{40,56},{48,0},{56,40},{64,11... | collective-permute-start | bytes 2359304 | tf_op jit(solution)/shard_map/ppermute | solution.py:24
  40.8 15.9 %collective-permute-start.10 = (bf16[4,6,32,256]{3,2,1,0:T(8,128)(2,1)S(1)}, bf16[4,6,32,256]{3,2,1,0:T(8,128)(2,1)S(1)}, u32[]{:S(2)}, u32[]{:S(2)}) collective-permute-start(bf16[4,6,32,256]{3,2,1,0:T(8,128)(2,1)S(1)} %pad_maximum_fusion.8.refs_9_), channel_id=1, source_target_pairs={{0,192},{8,72},{16,208},{24,88},{32,224},{40,104},{48,240},{56,120... | collective-permute-start | bytes 1179656 | tf_op jit(solution)/shard_map/ppermute | solution.py:24
  42.4 18.0 %collective-permute-start.8 = (bf16[4,6,32,256]{3,2,1,0:T(8,128)(2,1)S(1)}, bf16[4,6,32,256]{3,2,1,0:T(8,128)(2,1)}, u32[]{:S(2)}, u32[]{:S(2)}) collective-permute-start(bf16[4,6,32,256]{3,2,1,0:T(8,128)(2,1)S(1)} %pad_maximum_fusion.8.refs_9_), channel_id=1, source_target_pairs={{0,64},{8,200},{16,80},{24,216},{32,96},{40,232},{48,112},{56,248}... | collective-permute-start | bytes 1179656 | tf_op jit(solution)/shard_map/ppermute | solution.py:24
  61.2 12.0 %collective-permute-start.11 = (bf16[4,6,32,512]{3,2,1,0:T(8,128)(2,1)}, bf16[4,6,32,512]{3,2,1,0:T(8,128)(2,1)}, u32[]{:S(2)}, u32[]{:S(2)}) collective-permute-start(bf16[4,6,32,512]{3,2,1,0:T(8,128)(2,1)} %collective-permute-done.7.refs_6_), channel_id=1, source_target_pairs={{0,48},{8,24},{16,32},{24,8},{32,16},{40,56},{48,0},{56,40},{64,11... | collective-permute-start | bytes 2359304 | tf_op jit(solution)/shard_map/ppermute | solution.py:24
  63.9 8.9 %collective-permute-start.12 = (bf16[4,6,32,256]{3,2,1,0:T(8,128)(2,1)}, bf16[4,6,32,256]{3,2,1,0:T(8,128)(2,1)}, u32[]{:S(2)}, u32[]{:S(2)}) collective-permute-start(bf16[4,6,32,256]{3,2,1,0:T(8,128)(2,1)} %collective-permute-done.8.refs_10_), channel_id=1, source_target_pairs={{0,192},{8,72},{16,208},{24,88},{32,224},{40,104},{48,240},{56,120... | collective-permute-start | bytes 1179656 | tf_op jit(solution)/shard_map/ppermute | solution.py:24
  92.2 9.1 %collective-permute-start.17 = (bf16[8,256,384]{2,1,0:T(8,128)(2,1)}, bf16[8,256,384]{2,1,0:T(8,128)(2,1)S(1)}, u32[]{:S(2)}, u32[]{:S(2)}) collective-permute-start(bf16[8,256,384]{2,1,0:T(8,128)(2,1)} %get-tuple-element.56), channel_id=1, source_target_pairs={{0,8},{8,0},{16,24},{24,16},{32,40},{40,32},{48,56},{56,48},{64,72... | collective-permute-start | bytes 4718600 | tf_op jit(solution)/shard_map/ppermute | solution.py:24
  97.5 11.5 %collective-permute-start.14 = (bf16[3,512,256]{2,1,0:T(8,128)(2,1)}, bf16[3,512,256]{2,1,0:T(8,128)(2,1)}, u32[]{:S(2)}, u32[]{:S(2)}) collective-permute-start(bf16[3,512,256]{2,1,0:T(8,128)(2,1)} %get-tuple-element.52), channel_id=1, source_target_pairs={{0,48},{8,24},{16,32},{24,8},{32,16},{40,56},{48,0},{56,40},{64,11... | collective-permute-start | bytes 2359304 | tf_op jit(solution)/shard_map/ppermute | solution.py:24
  97.6 19.7 %collective-permute-start.15 = (bf16[3,512,256]{2,1,0:T(8,128)(2,1)}, bf16[3,512,256]{2,1,0:T(8,128)(2,1)S(1)}, u32[]{:S(2)}, u32[]{:S(2)}) collective-permute-start(bf16[3,512,256]{2,1,0:T(8,128)(2,1)} %get-tuple-element.53), channel_id=1, source_target_pairs={{0,48},{8,24},{16,32},{24,8},{32,16},{40,56},{48,0},{56,40},{64,11... | collective-permute-start | bytes 2359304 | tf_op jit(solution)/shard_map/ppermute | solution.py:24
  99.0 20.1 %collective-permute-start.16 = (bf16[3,512,256]{2,1,0:T(8,128)(2,1)}, bf16[3,512,256]{2,1,0:T(8,128)(2,1)S(1)}, u32[]{:S(2)}, u32[]{:S(2)}) collective-permute-start(bf16[3,512,256]{2,1,0:T(8,128)(2,1)} %get-tuple-element.54), channel_id=1, source_target_pairs={{0,192},{8,72},{16,208},{24,88},{32,224},{40,104},{48,240},{56,120... | collective-permute-start | bytes 2359304 | tf_op jit(solution)/shard_map/ppermute | solution.py:24
  121.4 18.8 %collective-permute-start.18 = (bf16[3,512,256]{2,1,0:T(8,128)(2,1)}, bf16[3,512,256]{2,1,0:T(8,128)(2,1)}, u32[]{:S(2)}, u32[]{:S(2)}) collective-permute-start(bf16[3,512,256]{2,1,0:T(8,128)(2,1)} %add_convert_fusion.1), channel_id=1, source_target_pairs={{0,16},{8,56},{16,0},{24,40},{32,48},{40,24},{48,32},{56,8},{64,80... | collective-permute-start | bytes 2359304 | tf_op jit(solution)/shard_map/ppermute | solution.py:24
  123.2 17.0 %collective-permute-start.19 = (bf16[2,512,256]{2,1,0:T(8,128)(2,1)S(1)}, bf16[2,512,256]{2,1,0:T(8,128)(2,1)}, u32[]{:S(2)}, u32[]{:S(2)}) collective-permute-start(bf16[2,512,256]{2,1,0:T(8,128)(2,1)S(1)} %add_convert_fusion.2), channel_id=1, source_target_pairs={{0,64},{8,200},{16,80},{24,216},{32,96},{40,232},{48,112},{56,248}... | collective-permute-start | bytes 1572872 | tf_op jit(solution)/shard_map/ppermute | solution.py:24
  142.4 14.4 %collective-permute-start.20 = (bf16[2,512,256]{2,1,0:T(8,128)(2,1)}, bf16[2,512,256]{2,1,0:T(8,128)(2,1)}, u32[]{:S(2)}, u32[]{:S(2)}) collective-permute-start(bf16[2,512,256]{2,1,0:T(8,128)(2,1)} %pad_maximum_fusion.4), channel_id=1, source_target_pairs={{0,192},{8,72},{16,208},{24,88},{32,224},{40,104},{48,240},{56,120... | collective-permute-start | bytes 1572872 | tf_op jit(solution)/shard_map/ppermute | solution.py:24
  149.6 18.0 %collective-permute-start.23 = (bf16[512,256]{1,0:T(8,128)(2,1)S(1)}, bf16[512,256]{1,0:T(8,128)(2,1)S(1)}, u32[]{:S(2)}, u32[]{:S(2)}) collective-permute-start(bf16[512,256]{1,0:T(8,128)(2,1)S(1)} %fusion.1), channel_id=1, source_target_pairs={{0,16},{8,56},{16,0},{24,40},{32,48},{40,24},{48,32},{56,8},{64,80... | collective-permute-start | bytes 786440 | tf_op jit(solution)/shard_map/ppermute | solution.py:24
  158.1 9.6 %collective-permute-start.21 = (bf16[512,256]{1,0:T(8,128)(2,1)S(1)}, bf16[512,256]{1,0:T(8,128)(2,1)S(1)}, u32[]{:S(2)}, u32[]{:S(2)}) collective-permute-start(bf16[512,256]{1,0:T(8,128)(2,1)S(1)} %fusion.3), channel_id=1, source_target_pairs={{0,64},{8,200},{16,80},{24,216},{32,96},{40,232},{48,112},{56,248}... | collective-permute-start | bytes 786440 | tf_op jit(solution)/shard_map/ppermute | solution.py:24
  159.3 8.4 %collective-permute-start.24 = (bf16[256,384]{1,0:T(8,128)(2,1)S(1)}, bf16[256,384]{1,0:T(8,128)(2,1)S(1)}, u32[]{:S(2)}, u32[]{:S(2)}) collective-permute-start(bf16[256,384]{1,0:T(8,128)(2,1)S(1)} %select_bitcast_fusion), channel_id=1, source_target_pairs={{0,1},{1,0},{2,3},{3,2},{4,5},{5,4},{6,7},{7,6},{8,9},{9,8},{10,11... | collective-permute-start | bytes 589832 | tf_op jit(solution)/shard_map/ppermute | solution.py:390
  160.7 15.2 %collective-permute-start.13 = (bf16[256,768]{1,0:T(8,128)(2,1)S(1)}, bf16[256,768]{1,0:T(8,128)(2,1)S(1)}, u32[]{:S(2)}, u32[]{:S(2)}) collective-permute-start(bf16[256,768]{1,0:T(8,128)(2,1)S(1)} %copy-done.13), channel_id=1, source_target_pairs={{0,8},{8,0},{16,24},{24,16},{32,40},{40,32},{48,56},{56,48},{64,72... | collective-permute-start | bytes 1179656 | tf_op jit(solution)/shard_map/ppermute | solution.py:24
  169.1 8.0 %collective-permute-start.25 = (bf16[512,256]{1,0:T(8,128)(2,1)S(1)}, bf16[512,256]{1,0:T(8,128)(2,1)S(1)}, u32[]{:S(2)}, u32[]{:S(2)}) collective-permute-start(bf16[512,256]{1,0:T(8,128)(2,1)S(1)} %get-tuple-element.69), channel_id=1, source_target_pairs={{0,8},{8,0},{16,24},{24,16},{32,40},{40,32},{48,56},{56,48},{64,72... | collective-permute-start | bytes 786440 | tf_op jit(solution)/shard_map/ppermute | solution.py:24
  180.8 21.6 %all-to-all-start = ((bf16[32,16,512]{2,1,0:T(8,128)(2,1)}), bf16[32,16,512]{2,1,0:T(8,128)(2,1)S(1)}, u32[]{:S(2)}, u32[]{:S(2)}) async-start(bf16[32,16,512]{2,1,0:T(8,128)(2,1)} %shard_map.59), calls=%async_computation.1 | async-start | bytes 1048576 | tf_op jit(solution)/shard_map/all_to_all | solution.py:414
  (19 other events, 216.5 us)
Sparse Core Ops, SparseCore 0:
  119.2 27.7 reduce-scatter.1

commit v3 on v2

--- a/solution.py
+++ b/solution.py
@@ -59,10 +59,10 @@
     return [[zz * NY + yy for yy in ys] for zz in zs]
 
 
-def main_kernel(scale, pos, tok_h, tok_t_h, cot0_h, cot1_h, *refs):
+def main_kernel(scale, pos, tok_h, cot0_h, cot1_h, *refs):
     pieces, refs = refs[:8], refs[8:]
     act0, act1, keep0, keep1, send0, send1, q_keep, q_send, ig_own, ig_other = refs[:10]
-    tok, tok_t, w, cot, v, slope_ref, stage, ig, sem_w, sem_in, sem_out, sem_ig = refs[10:]
+    tok, w, cot, v, slope_ref, stage, ig, sem_w, sem_in, sem_out, sem_ig = refs[10:]
     rows, wide = w.shape[0], w.shape[3]
     tokens = tok.shape[0]
     half, mid = tokens // 2, rows * S // 2
@@ -85,9 +85,6 @@
     ]
     in_copies.append(copy(cot0_h, cot.at[pl.ds(0, half)], sem_in.at[2]))
     in_copies.append(copy(cot1_h, cot.at[pl.ds(half, half)], sem_in.at[3]))
-    for b in range(rows):
-        here = pl.ds(b * S, S)
-        in_copies.append(copy(tok_t_h.at[here], tok_t.at[here], sem_in.at[4 + b]))
     for item in w_copies[:32] + in_copies[:1] + w_copies[32:] + in_copies[1:]:
         item.start()
     for item in w_copies[:32] + in_copies[:1]:
@@ -160,8 +157,12 @@
     sz = 1 - 2 * lax.rem(z + core, 2)
     other = lax.rem(z + sz + NZ, NZ)
     for b in range(rows):
-        in_copies[4 + b].wait()
-        g = jnp.dot(tok_t[b * S : (b + 1) * S], slope_ref[...], preferred_element_type=jnp.float32)
+        g = lax.dot_general(
+            tok[:, b * S : (b + 1) * S],
+            slope_ref[...],
+            (((0,), (0,)), ((), ())),
+            preferred_element_type=jnp.float32,
+        )
         g = (g * scale).astype(jnp.bfloat16)
         for j in range(wide // HALF):
             block = j * rows + b
@@ -184,7 +185,7 @@
         item.wait()
 
 
-def main_part(parts, scale, pos, tok, tok_t, cot0, cot1, pieces):
+def main_part(parts, scale, pos, tok, cot0, cot1, pieces):
     tokens = tok.shape[0]
     rows, wide = pieces[0].shape[1], cot0.shape[1]
     blocks = rows * wide // HALF
@@ -199,11 +200,10 @@
     return pl.pallas_call(
         lambda *refs: main_kernel(scale, *refs),
         out_shape=outs,
-        in_specs=[pl.BlockSpec(memory_space=pltpu.SMEM)] + [hbm] * 12,
+        in_specs=[pl.BlockSpec(memory_space=pltpu.SMEM)] + [hbm] * 11,
         out_specs=[vmem] * 2 + [hbm] * (len(sums) + 2),
         scratch_shapes=[
             held(tok.shape),
-            held(tok_t.shape),
             held(share),
             held((tokens, wide)),
             held((tokens, wide), jnp.float32),
@@ -211,7 +211,7 @@
             held((blocks, S, HALF)),
             held((2, *cut)),
             pltpu.SemaphoreType.DMA((64,)),
-            pltpu.SemaphoreType.DMA((4 + rows,)),
+            pltpu.SemaphoreType.DMA((4,)),
             pltpu.SemaphoreType.DMA((blocks,)),
             pltpu.SemaphoreType.DMA((4,)),
         ],
@@ -221,7 +221,7 @@
             bytes_accessed=8 * tokens * rows * S,
             transcendentals=tokens * wide,
         ),
-    )(pos, tok, tok_t, cot0, cot1, *pieces)
+    )(pos, tok, cot0, cot1, *pieces)
 
 
 def owners():
@@ -322,7 +322,6 @@
     tok = jnp.concatenate([tokens, swap_cores(tokens)], axis=0)
     c_mine, c_theirs = split(cotangent)
     c_recv = swap_cores(c_theirs)
-    tok_t = tok.T
 
     plan = [("z", "y", 0, (cols - 1) * HALF), ("y", "z", (cols - 1) * HALF, cols * HALF)]
 
@@ -348,7 +347,7 @@
         pieces += [fours[n], got1[n], got1[2 + n], exchange(got1[n], large, 2)]
 
     act0, act1, *grads, ig_own, ig_other = main_part(
-        parts, scale, pos, tok, tok_t, c_mine, c_recv, pieces
+        parts, scale, pos, tok, c_mine, c_recv, pieces
     )
     keep0, keep1, send0, send1, q_keep, q_send = grads
     y, z = pos[0], pos[1]

time: 211 us -> 214 us (1.014)
  other arithmetic: 29.5 us -> 19.6 us
  waiting for transfers between devices: 75.5 us -> 84.3 us
  starting transfers between devices: 62.7 us -> 71.1 us
  local copies, waits for them, and re-layouts: 4.69 us -> 1.95 us
    ppermute x25, waiting for transfers between devices: 62.1 us -> 67.4 us  [moved(): return lax.ppermute(array, 'dp', pairs)]
    ppermute x25, starting transfers between devices: 56.5 us -> 61.2 us  [moved(): return lax.ppermute(array, 'dp', pairs)]
    all_to_all x1, starting transfers between devices: 4.73 us -> 9.29 us  [local(): arrived = lax.all_to_all(result, 'dp', 0, 0, tiled=True)]
    transpose x1 -> x0, other arithmetic: 3.93 us -> none  [local(): tok_t = tok.T]
    all_to_all x1, waiting for transfers between devices: 13.3 us -> 16.9 us  [local(): arrived = lax.all_to_all(result, 'dp', 0, 0, tiled=True)]
    concatenate x1 -> x0, local copies, waits for them, and re-layouts: 3.03 us -> none  [local(): tok = jnp.concatenate([tokens, swap_cores(tokens)], axis=0)]
  transfers between devices with their start and end apart: 28 -> 28, of which waited for: 15 -> 14; matrix products, arithmetic and copies ran while one was open for 15% -> 9% of each run, Pallas kernels for 0% -> 0%
where the time goes in v3:
time: 214 us
  waiting for transfers between devices  84.3 us (39%)
  starting transfers between devices  71.1 us (33%)
  Pallas kernels  22.1 us (10%)
  other arithmetic  19.6 us (9%)
  between operations  14.4 us (7%)
    ppermute x25, waiting for transfers between devices, moved(): return lax.ppermute(array, 'dp', pairs)  67.4 us
    ppermute x25, starting transfers between devices, moved(): return lax.ppermute(array, 'dp', pairs)  61.2 us
    pallas_call x1, Pallas kernels, main_part(): pl.pallas_call(lambda *refs: main_kernel(scale, *refs), out_shape=outs, i...  17.7 us
    all_to_all x1, waiting for transfers between devices, local(): arrived = lax.all_to_all(result, 'dp', 0, 0, tiled=True)  16.9 us
    all_to_all x1, starting transfers between devices, local(): arrived = lax.all_to_all(result, 'dp', 0, 0, tiled=True)  9.29 us
    convert_element_type x7, other arithmetic, local(): cast = lambda array: array.astype(jnp.bfloat16)  7.79 us
  transfers between devices with their start and end apart: 28, of which 14 were waited for; matrix products, arithmetic and copies ran while one was open for 9% of the time, Pallas kernels for 0%

profile of v3, /device:TPU:1, one launch (start us, length us, event | category | flops | bytes accessed | tf_op | source)
XLA Modules:
  0.0 213.5 jit_solution(15813365640959701197)
XLA Ops:
  8.2 3.3 %collective-permute-start.1 = (bf16[6,16,768]{2,1,0:T(8,128)(2,1)S(1)}, bf16[6,16,768]{2,1,0:T(8,128)(2,1)S(1)}, u32[]{:S(2)}, u32[]{:S(2)}) collective-permute-start(bf16[6,16,768]{2,1,0:T(8,128)(2,1)S(1)} %pad_maximum_fusion.11), channel_id=1, source_target_pairs={{0,8},{8,0},{16,24},{24,16},{32,40},{40,32},{48,56},{56,48},{64,72... | collective-permute-start | bytes 442376 | tf_op jit(solution)/shard_map/ppermute | solution.py:24
  12.9 4.4 %collective-permute-start.2 = (bf16[6,32,512]{2,1,0:T(8,128)(2,1)S(1)}, bf16[6,32,512]{2,1,0:T(8,128)(2,1)S(1)}, u32[]{:S(2)}, u32[]{:S(2)}) collective-permute-start(bf16[6,32,512]{2,1,0:T(8,128)(2,1)S(1)} %fusion.5), channel_id=1, source_target_pairs={{0,64},{8,200},{16,80},{24,216},{32,96},{40,232},{48,112},{56,248}... | collective-permute-start | bytes 589832 | tf_op jit(solution)/shard_map/ppermute | solution.py:24
  17.3 2.8 %collective-permute-start.3 = (bf16[6,32,256]{2,1,0:T(8,128)(2,1)S(1)}, bf16[6,32,256]{2,1,0:T(8,128)(2,1)S(1)}, u32[]{:S(2)}, u32[]{:S(2)}) collective-permute-start(bf16[6,32,256]{2,1,0:T(8,128)(2,1)S(1)} %pad_maximum_fusion.12), channel_id=1, source_target_pairs={{0,16},{8,56},{16,0},{24,40},{32,48},{40,24},{48,32},{56,8},{64,80... | collective-permute-start | bytes 294920 | tf_op jit(solution)/shard_map/ppermute | solution.py:24
  25.1 4.5 %collective-permute-start = (bf16[256,3072]{1,0:T(8,128)(2,1)S(1)}, bf16[256,3072]{1,0:T(8,128)(2,1)S(1)}, u32[]{:S(2)}, u32[]{:S(2)}) collective-permute-start(bf16[256,3072]{1,0:T(8,128)(2,1)S(1)} %copy-done.2), channel_id=1, source_target_pairs={{0,8},{8,0},{16,24},{24,16},{32,40},{40,32},{48,56},{56,48},{64,72... | collective-permute-start | bytes 4718600 | tf_op jit(solution)/shard_map/ppermute | solution.py:24
  30.3 3.8 %collective-permute-done.4 = bf16[2,6,32,512]{3,2,1,0:T(8,128)(2,1)S(1)} collective-permute-done((bf16[2,6,32,512]{3,2,1,0:T(8,128)(2,1)S(1)}, bf16[2,6,32,512]{3,2,1,0:T(8,128)(2,1)S(1)}, u32[]{:S(2)}, u32[]{:S(2)}) %collective-permute-start.4) | collective-permute-done | bytes 393248 | tf_op jit(solution)/shard_map/ppermute | solution.py:24
  34.3 3.0 %collective-permute-start.7 = (bf16[4,6,32,512]{3,2,1,0:T(8,128)(2,1)S(1)}, bf16[4,6,32,512]{3,2,1,0:T(8,128)(2,1)}, u32[]{:S(2)}, u32[]{:S(2)}) collective-permute-start(bf16[4,6,32,512]{3,2,1,0:T(8,128)(2,1)S(1)} %pad_maximum_fusion.1.refs_4_), channel_id=1, source_target_pairs={{0,16},{8,56},{16,0},{24,40},{32,48},{40,24},{48,32},{56,8},{64,80... | collective-permute-start | bytes 2359304 | tf_op jit(solution)/shard_map/ppermute | solution.py:24
  38.8 2.5 %collective-permute-start.8 = (bf16[4,6,32,256]{3,2,1,0:T(8,128)(2,1)S(1)}, bf16[4,6,32,256]{3,2,1,0:T(8,128)(2,1)S(1)}, u32[]{:S(2)}, u32[]{:S(2)}) collective-permute-start(bf16[4,6,32,256]{3,2,1,0:T(8,128)(2,1)S(1)} %pad_maximum_fusion.8.refs_8_), channel_id=1, source_target_pairs={{0,64},{8,200},{16,80},{24,216},{32,96},{40,232},{48,112},{56,248}... | collective-permute-start | bytes 1179656 | tf_op jit(solution)/shard_map/ppermute | solution.py:24
  41.3 12.4 %collective-permute-done.10.refs_10_ = bf16[4,6,32,256]{3,2,1,0:T(8,128)(2,1)S(1)} collective-permute-done((bf16[4,6,32,256]{3,2,1,0:T(8,128)(2,1)S(1)}, bf16[4,6,32,256]{3,2,1,0:T(8,128)(2,1)S(1)}, u32[]{:S(2)}, u32[]{:S(2)}) %collective-permute-start.10) | collective-permute-done | bytes 393248 | tf_op jit(solution)/shard_map/ppermute | solution.py:24
  53.7 4.2 %collective-permute-done.8.refs_9_ = bf16[4,6,32,256]{3,2,1,0:T(8,128)(2,1)S(1)} collective-permute-done((bf16[4,6,32,256]{3,2,1,0:T(8,128)(2,1)S(1)}, bf16[4,6,32,256]{3,2,1,0:T(8,128)(2,1)S(1)}, u32[]{:S(2)}, u32[]{:S(2)}) %collective-permute-start.8) | collective-permute-done | bytes 393248 | tf_op jit(solution)/shard_map/ppermute | solution.py:24
  63.8 6.9 %collective-permute-done.12.refs_11_ = bf16[4,6,32,256]{3,2,1,0:T(8,128)(2,1)S(1)} collective-permute-done((bf16[4,6,32,256]{3,2,1,0:T(8,128)(2,1)}, bf16[4,6,32,256]{3,2,1,0:T(8,128)(2,1)S(1)}, u32[]{:S(2)}, u32[]{:S(2)}) %collective-permute-start.12) | collective-permute-done | bytes 393248 | tf_op jit(solution)/shard_map/ppermute | solution.py:24
  71.4 17.7 %shard_map.58 = (bf16[256,768]{1,0:T(8,128)(2,1)}, bf16[256,768]{1,0:T(8,128)(2,1)}, bf16[3,512,256]{2,1,0:T(8,128)(2,1)}, bf16[3,512,256]{2,1,0:T(8,128)(2,1)},...) custom-call(s32[3]{0:T(128)} %pad_add_fusion.refs_0_, ...), custom_call_target="tpu_custom_call" | custom-call | flops 7247757312 | bytes 12582912 | tf_op jit(solution)/shard_map/pallas_call | solution.py:200
  89.2 5.2 %collective-permute-start.17 = (bf16[8,256,384]{2,1,0:T(8,128)(2,1)}, bf16[8,256,384]{2,1,0:T(8,128)(2,1)S(1)}, u32[]{:S(2)}, u32[]{:S(2)}) collective-permute-start(bf16[8,256,384]{2,1,0:T(8,128)(2,1)} %get-tuple-element.56), channel_id=1, source_target_pairs={{0,8},{8,0},{16,24},{24,16},{32,40},{40,32},{48,56},{56,48},{64,72... | collective-permute-start | bytes 4718600 | tf_op jit(solution)/shard_map/ppermute | solution.py:24
  98.0 3.0 %add_convert_fusion = bf16[8,256,384]{2,1,0:T(8,128)(2,1)} fusion(bf16[8,256,384]{2,1,0:T(8,128)(2,1)S(1)} %collective-permute-done.17, bf16[8,256,384]{2,1,0:T(8,128)(2,1)} %get-tuple-element.55), kind=kLoop, calls=%fused_computation.1 | loop fusion | flops 3145728 | bytes 4718592 | tf_op jit(solution)/shard_map/convert_element_type | solution.py:305
  100.9 4.9 %collective-permute-done.14 = bf16[3,512,256]{2,1,0:T(8,128)(2,1)} collective-permute-done((bf16[3,512,256]{2,1,0:T(8,128)(2,1)}, bf16[3,512,256]{2,1,0:T(8,128)(2,1)}, u32[]{:S(2)}, u32[]{:S(2)}) %collective-permute-start.14) | collective-permute-done | bytes 786464 | tf_op jit(solution)/shard_map/ppermute | solution.py:24
  105.8 8.3 %collective-permute-done.15 = bf16[3,512,256]{2,1,0:T(8,128)(2,1)S(1)} collective-permute-done((bf16[3,512,256]{2,1,0:T(8,128)(2,1)}, bf16[3,512,256]{2,1,0:T(8,128)(2,1)S(1)}, u32[]{:S(2)}, u32[]{:S(2)}) %collective-permute-start.15) | collective-permute-done | bytes 786464 | tf_op jit(solution)/shard_map/ppermute | solution.py:24
  119.0 5.5 %collective-permute-start.19 = (bf16[2,512,256]{2,1,0:T(8,128)(2,1)S(1)}, bf16[2,512,256]{2,1,0:T(8,128)(2,1)}, u32[]{:S(2)}, u32[]{:S(2)}) collective-permute-start(bf16[2,512,256]{2,1,0:T(8,128)(2,1)S(1)} %add_convert_fusion.2), channel_id=1, source_target_pairs={{0,64},{8,200},{16,80},{24,216},{32,96},{40,232},{48,112},{56,248}... | collective-permute-start | bytes 1572872 | tf_op jit(solution)/shard_map/ppermute | solution.py:24
  124.4 12.3 %collective-permute-done.19 = bf16[2,512,256]{2,1,0:T(8,128)(2,1)} collective-permute-done((bf16[2,512,256]{2,1,0:T(8,128)(2,1)S(1)}, bf16[2,512,256]{2,1,0:T(8,128)(2,1)}, u32[]{:S(2)}, u32[]{:S(2)}) %collective-permute-start.19) | collective-permute-done | bytes 524320 | tf_op jit(solution)/shard_map/ppermute | solution.py:24
  141.0 5.1 %collective-permute-done.22 = bf16[512,256]{1,0:T(8,128)(2,1)S(1)} collective-permute-done((bf16[512,256]{1,0:T(8,128)(2,1)S(1)}, bf16[512,256]{1,0:T(8,128)(2,1)S(1)}, u32[]{:S(2)}, u32[]{:S(2)}) %collective-permute-start.22) | collective-permute-done | bytes 262176 | tf_op jit(solution)/shard_map/ppermute | solution.py:24
  148.3 4.4 %collective-permute-done.20 = bf16[2,512,256]{2,1,0:T(8,128)(2,1)} collective-permute-done((bf16[2,512,256]{2,1,0:T(8,128)(2,1)}, bf16[2,512,256]{2,1,0:T(8,128)(2,1)}, u32[]{:S(2)}, u32[]{:S(2)}) %collective-permute-start.20) | collective-permute-done | bytes 524320 | tf_op jit(solution)/shard_map/ppermute | solution.py:24
  155.8 10.6 %collective-permute-start.13 = (bf16[256,768]{1,0:T(8,128)(2,1)S(1)}, bf16[256,768]{1,0:T(8,128)(2,1)S(1)}, u32[]{:S(2)}, u32[]{:S(2)}) collective-permute-start(bf16[256,768]{1,0:T(8,128)(2,1)S(1)} %copy-done.12), channel_id=1, source_target_pairs={{0,8},{8,0},{16,24},{24,16},{32,40},{40,32},{48,56},{56,48},{64,72... | collective-permute-start | bytes 1179656 | tf_op jit(solution)/shard_map/ppermute | solution.py:24
  167.8 6.0 %collective-permute-start.25 = (bf16[512,256]{1,0:T(8,128)(2,1)S(1)}, bf16[512,256]{1,0:T(8,128)(2,1)S(1)}, u32[]{:S(2)}, u32[]{:S(2)}) collective-permute-start(bf16[512,256]{1,0:T(8,128)(2,1)S(1)} %get-tuple-element.69), channel_id=1, source_target_pairs={{0,8},{8,0},{16,24},{24,16},{32,40},{40,32},{48,56},{56,48},{64,72... | collective-permute-start | bytes 786440 | tf_op jit(solution)/shard_map/ppermute | solution.py:24
  175.0 3.5 %shard_map.59 = bf16[32,16,512]{2,1,0:T(8,128)(2,1)} custom-call(bf16[512,256]{1,0:T(8,128)(2,1)S(1)} %get-tuple-element.88.g0_ref, bf16[512,256]{1,0:T(8,128)(2,1)S(1)} %get-tuple-element.87.g1_ref), custom_call_target="tpu_custom_call" | custom-call | tf_op jit(solution)/shard_map/pallas_call | solution.py:269
  178.6 9.3 %all-to-all-start = ((bf16[32,16,512]{2,1,0:T(8,128)(2,1)}), bf16[32,16,512]{2,1,0:T(8,128)(2,1)S(1)}, u32[]{:S(2)}, u32[]{:S(2)}) async-start(bf16[32,16,512]{2,1,0:T(8,128)(2,1)} %shard_map.59), calls=%async_computation.1 | async-start | bytes 1048576 | tf_op jit(solution)/shard_map/all_to_all | solution.py:413
  189.0 16.9 %all-to-all-done.in_ref = bf16[32,16,512]{2,1,0:T(8,128)(2,1)S(1)} async-done(((bf16[32,16,512]{2,1,0:T(8,128)(2,1)}), bf16[32,16,512]{2,1,0:T(8,128)(2,1)S(1)}, u32[]{:S(2)}, u32[]{:S(2)}) %all-to-all-start) | async-done | bytes 524320 | tf_op jit(solution)/shard_map/all_to_all | solution.py:413
  (105 shorter events, 38.6 us)
Async XLA Ops:
  7.2 147.0 %reduce-scatter.2.cloned.1.call-start = ((), (), s32[]{:S(2)}) async-start(), calls=%async_computation.2 | async-start | bytes 1966080 | tf_op jit(solution)/shard_map/reduce_scatter | solution.py:385
  12.9 9.2 %collective-permute-start.2 = (bf16[6,32,512]{2,1,0:T(8,128)(2,1)S(1)}, bf16[6,32,512]{2,1,0:T(8,128)(2,1)S(1)}, u32[]{:S(2)}, u32[]{:S(2)}) collective-permute-start(bf16[6,32,512]{2,1,0:T(8,128)(2,1)S(1)} %fusion.5), channel_id=1, source_target_pairs={{0,64},{8,200},{16,80},{24,216},{32,96},{40,232},{48,112},{56,248}... | collective-permute-start | bytes 589832 | tf_op jit(solution)/shard_map/ppermute | solution.py:24
  20.1 10.2 %collective-permute-start.6 = (bf16[256,768]{1,0:T(8,128)(2,1)S(1)}, bf16[256,768]{1,0:T(8,128)(2,1)S(1)}, u32[]{:S(2)}, u32[]{:S(2)}) collective-permute-start(bf16[256,768]{1,0:T(8,128)(2,1)S(1)} %pad_maximum_fusion.7), channel_id=1, source_target_pairs={{0,8},{8,0},{16,24},{24,16},{32,40},{40,32},{48,56},{56,48},{64,72... | collective-permute-start | bytes 1179656 | tf_op jit(solution)/shard_map/ppermute | solution.py:24
  22.2 11.9 %collective-permute-start.4 = (bf16[2,6,32,512]{3,2,1,0:T(8,128)(2,1)S(1)}, bf16[2,6,32,512]{3,2,1,0:T(8,128)(2,1)S(1)}, u32[]{:S(2)}, u32[]{:S(2)}) collective-permute-start(bf16[2,6,32,512]{3,2,1,0:T(8,128)(2,1)S(1)} %pad_maximum_fusion.5), channel_id=1, source_target_pairs={{0,192},{8,72},{16,208},{24,88},{32,224},{40,104},{48,240},{56,120... | collective-permute-start | bytes 1179656 | tf_op jit(solution)/shard_map/ppermute | solution.py:24
  25.1 36.9 %collective-permute-start = (bf16[256,3072]{1,0:T(8,128)(2,1)S(1)}, bf16[256,3072]{1,0:T(8,128)(2,1)S(1)}, u32[]{:S(2)}, u32[]{:S(2)}) collective-permute-start(bf16[256,3072]{1,0:T(8,128)(2,1)S(1)} %copy-done.2), channel_id=1, source_target_pairs={{0,8},{8,0},{16,24},{24,16},{32,40},{40,32},{48,56},{56,48},{64,72... | collective-permute-start | bytes 4718600 | tf_op jit(solution)/shard_map/ppermute | solution.py:24
  34.3 23.7 %collective-permute-start.7 = (bf16[4,6,32,512]{3,2,1,0:T(8,128)(2,1)S(1)}, bf16[4,6,32,512]{3,2,1,0:T(8,128)(2,1)}, u32[]{:S(2)}, u32[]{:S(2)}) collective-permute-start(bf16[4,6,32,512]{3,2,1,0:T(8,128)(2,1)S(1)} %pad_maximum_fusion.1.refs_4_), channel_id=1, source_target_pairs={{0,16},{8,56},{16,0},{24,40},{32,48},{40,24},{48,32},{56,8},{64,80... | collective-permute-start | bytes 2359304 | tf_op jit(solution)/shard_map/ppermute | solution.py:24
  37.3 20.7 %collective-permute-start.9 = (bf16[4,6,32,512]{3,2,1,0:T(8,128)(2,1)S(1)}, bf16[4,6,32,512]{3,2,1,0:T(8,128)(2,1)S(1)}, u32[]{:S(2)}, u32[]{:S(2)}) collective-permute-start(bf16[4,6,32,512]{3,2,1,0:T(8,128)(2,1)S(1)} %pad_maximum_fusion.1.refs_4_), channel_id=1, source_target_pairs={{0,48},{8,24},{16,32},{24,8},{32,16},{40,56},{48,0},{56,40},{64,11... | collective-permute-start | bytes 2359304 | tf_op jit(solution)/shard_map/ppermute | solution.py:24
  37.3 16.4 %collective-permute-start.10 = (bf16[4,6,32,256]{3,2,1,0:T(8,128)(2,1)S(1)}, bf16[4,6,32,256]{3,2,1,0:T(8,128)(2,1)S(1)}, u32[]{:S(2)}, u32[]{:S(2)}) collective-permute-start(bf16[4,6,32,256]{3,2,1,0:T(8,128)(2,1)S(1)} %pad_maximum_fusion.8.refs_8_), channel_id=1, source_target_pairs={{0,192},{8,72},{16,208},{24,88},{32,224},{40,104},{48,240},{56,120... | collective-permute-start | bytes 1179656 | tf_op jit(solution)/shard_map/ppermute | solution.py:24
  38.8 19.1 %collective-permute-start.8 = (bf16[4,6,32,256]{3,2,1,0:T(8,128)(2,1)S(1)}, bf16[4,6,32,256]{3,2,1,0:T(8,128)(2,1)S(1)}, u32[]{:S(2)}, u32[]{:S(2)}) collective-permute-start(bf16[4,6,32,256]{3,2,1,0:T(8,128)(2,1)S(1)} %pad_maximum_fusion.8.refs_8_), channel_id=1, source_target_pairs={{0,64},{8,200},{16,80},{24,216},{32,96},{40,232},{48,112},{56,248}... | collective-permute-start | bytes 1179656 | tf_op jit(solution)/shard_map/ppermute | solution.py:24
  59.6 11.6 %collective-permute-start.11 = (bf16[4,6,32,512]{3,2,1,0:T(8,128)(2,1)}, bf16[4,6,32,512]{3,2,1,0:T(8,128)(2,1)}, u32[]{:S(2)}, u32[]{:S(2)}) collective-permute-start(bf16[4,6,32,512]{3,2,1,0:T(8,128)(2,1)} %collective-permute-done.7.refs_5_), channel_id=1, source_target_pairs={{0,48},{8,24},{16,32},{24,8},{32,16},{40,56},{48,0},{56,40},{64,11... | collective-permute-start | bytes 2359304 | tf_op jit(solution)/shard_map/ppermute | solution.py:24
  61.8 8.9 %collective-permute-start.12 = (bf16[4,6,32,256]{3,2,1,0:T(8,128)(2,1)}, bf16[4,6,32,256]{3,2,1,0:T(8,128)(2,1)S(1)}, u32[]{:S(2)}, u32[]{:S(2)}) collective-permute-start(bf16[4,6,32,256]{3,2,1,0:T(8,128)(2,1)} %copy-done.15), channel_id=1, source_target_pairs={{0,192},{8,72},{16,208},{24,88},{32,224},{40,104},{48,240},{56,120... | collective-permute-start | bytes 1179656 | tf_op jit(solution)/shard_map/ppermute | solution.py:24
  89.2 8.8 %collective-permute-start.17 = (bf16[8,256,384]{2,1,0:T(8,128)(2,1)}, bf16[8,256,384]{2,1,0:T(8,128)(2,1)S(1)}, u32[]{:S(2)}, u32[]{:S(2)}) collective-permute-start(bf16[8,256,384]{2,1,0:T(8,128)(2,1)} %get-tuple-element.56), channel_id=1, source_target_pairs={{0,8},{8,0},{16,24},{24,16},{32,40},{40,32},{48,56},{56,48},{64,72... | collective-permute-start | bytes 4718600 | tf_op jit(solution)/shard_map/ppermute | solution.py:24
  94.4 11.5 %collective-permute-start.14 = (bf16[3,512,256]{2,1,0:T(8,128)(2,1)}, bf16[3,512,256]{2,1,0:T(8,128)(2,1)}, u32[]{:S(2)}, u32[]{:S(2)}) collective-permute-start(bf16[3,512,256]{2,1,0:T(8,128)(2,1)} %get-tuple-element.52), channel_id=1, source_target_pairs={{0,48},{8,24},{16,32},{24,8},{32,16},{40,56},{48,0},{56,40},{64,11... | collective-permute-start | bytes 2359304 | tf_op jit(solution)/shard_map/ppermute | solution.py:24
  94.4 19.8 %collective-permute-start.15 = (bf16[3,512,256]{2,1,0:T(8,128)(2,1)}, bf16[3,512,256]{2,1,0:T(8,128)(2,1)S(1)}, u32[]{:S(2)}, u32[]{:S(2)}) collective-permute-start(bf16[3,512,256]{2,1,0:T(8,128)(2,1)} %get-tuple-element.53), channel_id=1, source_target_pairs={{0,48},{8,24},{16,32},{24,8},{32,16},{40,56},{48,0},{56,40},{64,11... | collective-permute-start | bytes 2359304 | tf_op jit(solution)/shard_map/ppermute | solution.py:24
  95.8 19.8 %collective-permute-start.16 = (bf16[3,512,256]{2,1,0:T(8,128)(2,1)}, bf16[3,512,256]{2,1,0:T(8,128)(2,1)S(1)}, u32[]{:S(2)}, u32[]{:S(2)}) collective-permute-start(bf16[3,512,256]{2,1,0:T(8,128)(2,1)} %get-tuple-element.54), channel_id=1, source_target_pairs={{0,192},{8,72},{16,208},{24,88},{32,224},{40,104},{48,240},{56,120... | collective-permute-start | bytes 2359304 | tf_op jit(solution)/shard_map/ppermute | solution.py:24
  118.0 18.8 %collective-permute-start.18 = (bf16[3,512,256]{2,1,0:T(8,128)(2,1)}, bf16[3,512,256]{2,1,0:T(8,128)(2,1)}, u32[]{:S(2)}, u32[]{:S(2)}) collective-permute-start(bf16[3,512,256]{2,1,0:T(8,128)(2,1)} %add_convert_fusion.1), channel_id=1, source_target_pairs={{0,16},{8,56},{16,0},{24,40},{32,48},{40,24},{48,32},{56,8},{64,80... | collective-permute-start | bytes 2359304 | tf_op jit(solution)/shard_map/ppermute | solution.py:24
  119.0 17.8 %collective-permute-start.19 = (bf16[2,512,256]{2,1,0:T(8,128)(2,1)S(1)}, bf16[2,512,256]{2,1,0:T(8,128)(2,1)}, u32[]{:S(2)}, u32[]{:S(2)}) collective-permute-start(bf16[2,512,256]{2,1,0:T(8,128)(2,1)S(1)} %add_convert_fusion.2), channel_id=1, source_target_pairs={{0,64},{8,200},{16,80},{24,216},{32,96},{40,232},{48,112},{56,248}... | collective-permute-start | bytes 1572872 | tf_op jit(solution)/shard_map/ppermute | solution.py:24
  139.0 13.7 %collective-permute-start.20 = (bf16[2,512,256]{2,1,0:T(8,128)(2,1)}, bf16[2,512,256]{2,1,0:T(8,128)(2,1)}, u32[]{:S(2)}, u32[]{:S(2)}) collective-permute-start(bf16[2,512,256]{2,1,0:T(8,128)(2,1)} %pad_maximum_fusion.4), channel_id=1, source_target_pairs={{0,192},{8,72},{16,208},{24,88},{32,224},{40,104},{48,240},{56,120... | collective-permute-start | bytes 1572872 | tf_op jit(solution)/shard_map/ppermute | solution.py:24
  146.3 20.1 %collective-permute-start.23 = (bf16[512,256]{1,0:T(8,128)(2,1)S(1)}, bf16[512,256]{1,0:T(8,128)(2,1)S(1)}, u32[]{:S(2)}, u32[]{:S(2)}) collective-permute-start(bf16[512,256]{1,0:T(8,128)(2,1)S(1)} %fusion.1), channel_id=1, source_target_pairs={{0,16},{8,56},{16,0},{24,40},{32,48},{40,24},{48,32},{56,8},{64,80... | collective-permute-start | bytes 786440 | tf_op jit(solution)/shard_map/ppermute | solution.py:24
  154.0 12.4 %collective-permute-start.21 = (bf16[512,256]{1,0:T(8,128)(2,1)S(1)}, bf16[512,256]{1,0:T(8,128)(2,1)S(1)}, u32[]{:S(2)}, u32[]{:S(2)}) collective-permute-start(bf16[512,256]{1,0:T(8,128)(2,1)S(1)} %fusion.3), channel_id=1, source_target_pairs={{0,64},{8,200},{16,80},{24,216},{32,96},{40,232},{48,112},{56,248}... | collective-permute-start | bytes 786440 | tf_op jit(solution)/shard_map/ppermute | solution.py:24
  155.2 11.2 %collective-permute-start.24 = (bf16[256,384]{1,0:T(8,128)(2,1)S(1)}, bf16[256,384]{1,0:T(8,128)(2,1)S(1)}, u32[]{:S(2)}, u32[]{:S(2)}) collective-permute-start(bf16[256,384]{1,0:T(8,128)(2,1)S(1)} %select_bitcast_fusion), channel_id=1, source_target_pairs={{0,1},{1,0},{2,3},{3,2},{4,5},{5,4},{6,7},{7,6},{8,9},{9,8},{10,11... | collective-permute-start | bytes 589832 | tf_op jit(solution)/shard_map/ppermute | solution.py:389
  155.8 17.9 %collective-permute-start.13 = (bf16[256,768]{1,0:T(8,128)(2,1)S(1)}, bf16[256,768]{1,0:T(8,128)(2,1)S(1)}, u32[]{:S(2)}, u32[]{:S(2)}) collective-permute-start(bf16[256,768]{1,0:T(8,128)(2,1)S(1)} %copy-done.12), channel_id=1, source_target_pairs={{0,8},{8,0},{16,24},{24,16},{32,40},{40,32},{48,56},{56,48},{64,72... | collective-permute-start | bytes 1179656 | tf_op jit(solution)/shard_map/ppermute | solution.py:24
  167.8 7.1 %collective-permute-start.25 = (bf16[512,256]{1,0:T(8,128)(2,1)S(1)}, bf16[512,256]{1,0:T(8,128)(2,1)S(1)}, u32[]{:S(2)}, u32[]{:S(2)}) collective-permute-start(bf16[512,256]{1,0:T(8,128)(2,1)S(1)} %get-tuple-element.69), channel_id=1, source_target_pairs={{0,8},{8,0},{16,24},{24,16},{32,40},{40,32},{48,56},{56,48},{64,72... | collective-permute-start | bytes 786440 | tf_op jit(solution)/shard_map/ppermute | solution.py:24
  178.6 27.3 %all-to-all-start = ((bf16[32,16,512]{2,1,0:T(8,128)(2,1)}), bf16[32,16,512]{2,1,0:T(8,128)(2,1)S(1)}, u32[]{:S(2)}, u32[]{:S(2)}) async-start(bf16[32,16,512]{2,1,0:T(8,128)(2,1)} %shard_map.59), calls=%async_computation.1 | async-start | bytes 1048576 | tf_op jit(solution)/shard_map/all_to_all | solution.py:413
  (21 other events, 201.9 us)
Sparse Core Ops, SparseCore 0:
  115.8 28.0 reduce-scatter.1

commit v4 on v2

--- a/solution.py
+++ b/solution.py
@@ -390,12 +390,8 @@
     ig_there = lax.ppermute(
         jnp.where(odd, ig_x[0], ig_x[1]), "tensor", [(t, t + 1 - 2 * (t % 2)) for t in range(parts)]
     )
-    got4, q_got4, ig_there = together(
-        (
-            exchange(cast(p_slot(sz) + wide32(got3[1])), "z", 1),
-            exchange(q_half, "y", 1),
-            ig_there,
-        )
+    got4, q_got4 = together(
+        (exchange(cast(p_slot(sz) + wide32(got3[1])), "z", 1), exchange(q_half, "y", 1))
     )
     p_block = cast(p_slot(0) + wide32(got3[0]) + wide32(got4))
     q_block = cast(wide32(q_half) + wide32(q_got4))
@@ -412,6 +408,7 @@
     recv = swap_cores(jnp.where(first, q_block, p_block))
     result = newton(jnp.where(first, p_block, recv), jnp.where(first, recv, q_block))
     arrived = lax.all_to_all(result, "dp", 0, 0, tiled=True)
+    arrived, input_grad = together((arrived, input_grad))
     update = place(rows, cols, arrived)
     return (activated, input_grad, update)
 

time: 211 us -> 211 us (level)
    ppermute x1, waiting for transfers between devices: 0.01 us -> 15.2 us  [local(): lax.ppermute(jnp.where(odd, ig_x[0], ig_x[1]), 'tensor', [(t, t + 1 - 2 *...]
    all_to_all x1, waiting for transfers between devices: 13.3 us -> 0.01 us  [local(): arrived = lax.all_to_all(result, 'dp', 0, 0, tiled=True)]
  transfers between devices with their start and end apart: 28 -> 28, of which waited for: 15 -> 15; matrix products, arithmetic and copies ran while one was open for 15% -> 14% of each run, Pallas kernels for 0% -> 2%
where the time goes in v4:
time: 211 us; the launch traced here: 210 us
  waiting for transfers between devices  76.8 us (36%)
  starting transfers between devices  60.7 us (29%)
  other arithmetic  28.5 us (14%)
  Pallas kernels  23.4 us (11%)
  between operations  14.4 us (7%)
  local copies, waits for them, and re-layouts  6.56 us (3%)
    ppermute x25, waiting for transfers between devices, moved(): return lax.ppermute(array, 'dp', pairs)  61.6 us
    ppermute x25, starting transfers between devices, moved(): return lax.ppermute(array, 'dp', pairs)  55.8 us
    pallas_call x1, Pallas kernels, main_part(): pl.pallas_call(lambda *refs: main_kernel(scale, *refs), out_shape=outs, i...  19 us
    ppermute x1, waiting for transfers between devices, local(): lax.ppermute(jnp.where(odd, ig_x[0], ig_x[1]), 'tensor', [(t, t + 1 - 2 *...  15.2 us
    convert_element_type x7, other arithmetic, local(): cast = lambda array: array.astype(jnp.bfloat16)  9.21 us
    all_to_all x1, starting transfers between devices, local(): arrived = lax.all_to_all(result, 'dp', 0, 0, tiled=True)  4.73 us
  transfers between devices with their start and end apart: 28, of which 15 were waited for; matrix products, arithmetic and copies ran while one was open for 14% of the time, Pallas kernels for 2%

profile of v4, /device:TPU:1, one launch (start us, length us, event | category | flops | bytes accessed | tf_op | source)
XLA Modules:
  0.0 210.4 jit_solution(2264734768468929393)
XLA Ops:
  8.2 3.3 %collective-permute-start.1 = (bf16[6,16,768]{2,1,0:T(8,128)(2,1)S(1)}, bf16[6,16,768]{2,1,0:T(8,128)(2,1)S(1)}, u32[]{:S(2)}, u32[]{:S(2)}) collective-permute-start(bf16[6,16,768]{2,1,0:T(8,128)(2,1)S(1)} %pad_maximum_fusion.11), channel_id=1, source_target_pairs={{0,8},{8,0},{16,24},{24,16},{32,40},{40,32},{48,56},{56,48},{64,72... | collective-permute-start | bytes 442376 | tf_op jit(solution)/shard_map/ppermute | solution.py:24
  13.6 4.4 %collective-permute-start.2 = (bf16[6,32,512]{2,1,0:T(8,128)(2,1)S(1)}, bf16[6,32,512]{2,1,0:T(8,128)(2,1)S(1)}, u32[]{:S(2)}, u32[]{:S(2)}) collective-permute-start(bf16[6,32,512]{2,1,0:T(8,128)(2,1)S(1)} %fusion.5), channel_id=1, source_target_pairs={{0,64},{8,200},{16,80},{24,216},{32,96},{40,232},{48,112},{56,248}... | collective-permute-start | bytes 589832 | tf_op jit(solution)/shard_map/ppermute | solution.py:24
  18.0 2.8 %collective-permute-start.3 = (bf16[6,32,256]{2,1,0:T(8,128)(2,1)S(1)}, bf16[6,32,256]{2,1,0:T(8,128)(2,1)S(1)}, u32[]{:S(2)}, u32[]{:S(2)}) collective-permute-start(bf16[6,32,256]{2,1,0:T(8,128)(2,1)S(1)} %pad_maximum_fusion.12), channel_id=1, source_target_pairs={{0,16},{8,56},{16,0},{24,40},{32,48},{40,24},{48,32},{56,8},{64,80... | collective-permute-start | bytes 294920 | tf_op jit(solution)/shard_map/ppermute | solution.py:24
  25.9 2.8 %collective-permute-start = (bf16[256,3072]{0,1:T(8,128)(2,1)S(1)}, bf16[256,3072]{0,1:T(8,128)(2,1)}, u32[]{:S(2)}, u32[]{:S(2)}) collective-permute-start(bf16[256,3072]{0,1:T(8,128)(2,1)S(1)} %copy.7), channel_id=1, source_target_pairs={{0,8},{8,0},{16,24},{24,16},{32,40},{40,32},{48,56},{56,48},{64,72... | collective-permute-start | bytes 4718600 | tf_op jit(solution)/shard_map/ppermute | solution.py:24
  37.8 3.0 %collective-permute-start.7 = (bf16[4,6,32,512]{3,2,1,0:T(8,128)(2,1)S(1)}, bf16[4,6,32,512]{3,2,1,0:T(8,128)(2,1)}, u32[]{:S(2)}, u32[]{:S(2)}) collective-permute-start(bf16[4,6,32,512]{3,2,1,0:T(8,128)(2,1)S(1)} %pad_maximum_fusion.1.refs_5_), channel_id=1, source_target_pairs={{0,16},{8,56},{16,0},{24,40},{32,48},{40,24},{48,32},{56,8},{64,80... | collective-permute-start | bytes 2359304 | tf_op jit(solution)/shard_map/ppermute | solution.py:24
  42.4 2.4 %collective-permute-start.8 = (bf16[4,6,32,256]{3,2,1,0:T(8,128)(2,1)S(1)}, bf16[4,6,32,256]{3,2,1,0:T(8,128)(2,1)}, u32[]{:S(2)}, u32[]{:S(2)}) collective-permute-start(bf16[4,6,32,256]{3,2,1,0:T(8,128)(2,1)S(1)} %pad_maximum_fusion.8.refs_9_), channel_id=1, source_target_pairs={{0,64},{8,200},{16,80},{24,216},{32,96},{40,232},{48,112},{56,248}... | collective-permute-start | bytes 1179656 | tf_op jit(solution)/shard_map/ppermute | solution.py:24
  44.8 11.9 %collective-permute-done.10.refs_11_ = bf16[4,6,32,256]{3,2,1,0:T(8,128)(2,1)S(1)} collective-permute-done((bf16[4,6,32,256]{3,2,1,0:T(8,128)(2,1)S(1)}, bf16[4,6,32,256]{3,2,1,0:T(8,128)(2,1)S(1)}, u32[]{:S(2)}, u32[]{:S(2)}) %collective-permute-start.10) | collective-permute-done | bytes 393248 | tf_op jit(solution)/shard_map/ppermute | solution.py:24
  56.7 3.7 %collective-permute-done.8.refs_10_ = bf16[4,6,32,256]{3,2,1,0:T(8,128)(2,1)} collective-permute-done((bf16[4,6,32,256]{3,2,1,0:T(8,128)(2,1)S(1)}, bf16[4,6,32,256]{3,2,1,0:T(8,128)(2,1)}, u32[]{:S(2)}, u32[]{:S(2)}) %collective-permute-start.8) | collective-permute-done | bytes 393248 | tf_op jit(solution)/shard_map/ppermute | solution.py:24
  64.0 3.9 %fusion.6 = (bf16[3072,512]{1,0:T(8,128)(2,1)}, bf16[512,3072]{0,1:T(8,128)(2,1)S(1)}) fusion(bf16[256,3072]{0,1:T(8,128)(2,1)} %collective-permute-done, bf16[256,3072]{0,1:T(8,128)(2,1)} %copy-done), kind=kLoop, calls=%fused_computation.58 | loop fusion | flops 6291456 | bytes 9437184 | tf_op jit(solution)/shard_map/transpose | solution.py:325
  67.9 3.0 %copy.8.refs_1_ = bf16[512,3072]{1,0:T(8,128)(2,1)} copy(bf16[512,3072]{0,1:T(8,128)(2,1)S(1)} %get-tuple-element.74) | data formatting | bytes 6291456 | tf_op jit(solution)/shard_map/concatenate | solution.py:322
  73.3 19.0 %shard_map.58 = (bf16[256,768]{1,0:T(8,128)(2,1)}, bf16[256,768]{1,0:T(8,128)(2,1)}, bf16[3,512,256]{2,1,0:T(8,128)(2,1)}, bf16[3,512,256]{2,1,0:T(8,128)(2,1)},...) custom-call(s32[3]{0:T(128)} %pad_add_fusion.refs_0_, ...), custom_call_target="tpu_custom_call" | custom-call | flops 7247757312 | bytes 12582912 | tf_op jit(solution)/shard_map/pallas_call | solution.py:199
  92.3 5.3 %collective-permute-start.17 = (bf16[8,256,384]{2,1,0:T(8,128)(2,1)}, bf16[8,256,384]{2,1,0:T(8,128)(2,1)}, u32[]{:S(2)}, u32[]{:S(2)}) collective-permute-start(bf16[8,256,384]{2,1,0:T(8,128)(2,1)} %get-tuple-element.58), channel_id=1, source_target_pairs={{0,8},{8,0},{16,24},{24,16},{32,40},{40,32},{48,56},{56,48},{64,72... | collective-permute-start | bytes 4718600 | tf_op jit(solution)/shard_map/ppermute | solution.py:24
  102.3 3.5 %add_convert_fusion = bf16[8,256,384]{2,1,0:T(8,128)(2,1)} fusion(bf16[8,256,384]{2,1,0:T(8,128)(2,1)} %collective-permute-done.17, bf16[8,256,384]{2,1,0:T(8,128)(2,1)} %get-tuple-element.57), kind=kLoop, calls=%fused_computation.1 | loop fusion | flops 3145728 | bytes 4718592 | tf_op jit(solution)/shard_map/convert_element_type | solution.py:305
  105.8 3.2 %collective-permute-done.14 = bf16[3,512,256]{2,1,0:T(8,128)(2,1)} collective-permute-done((bf16[3,512,256]{2,1,0:T(8,128)(2,1)}, bf16[3,512,256]{2,1,0:T(8,128)(2,1)}, u32[]{:S(2)}, u32[]{:S(2)}) %collective-permute-start.14) | collective-permute-done | bytes 786464 | tf_op jit(solution)/shard_map/ppermute | solution.py:24
  109.0 8.3 %collective-permute-done.15 = bf16[3,512,256]{2,1,0:T(8,128)(2,1)S(1)} collective-permute-done((bf16[3,512,256]{2,1,0:T(8,128)(2,1)}, bf16[3,512,256]{2,1,0:T(8,128)(2,1)S(1)}, u32[]{:S(2)}, u32[]{:S(2)}) %collective-permute-start.15) | collective-permute-done | bytes 786464 | tf_op jit(solution)/shard_map/ppermute | solution.py:24
  123.1 4.6 %collective-permute-start.19 = (bf16[2,512,256]{2,1,0:T(8,128)(2,1)S(1)}, bf16[2,512,256]{2,1,0:T(8,128)(2,1)}, u32[]{:S(2)}, u32[]{:S(2)}) collective-permute-start(bf16[2,512,256]{2,1,0:T(8,128)(2,1)S(1)} %add_convert_fusion.2), channel_id=1, source_target_pairs={{0,64},{8,200},{16,80},{24,216},{32,96},{40,232},{48,112},{56,248}... | collective-permute-start | bytes 1572872 | tf_op jit(solution)/shard_map/ppermute | solution.py:24
  127.8 12.3 %collective-permute-done.19 = bf16[2,512,256]{2,1,0:T(8,128)(2,1)} collective-permute-done((bf16[2,512,256]{2,1,0:T(8,128)(2,1)S(1)}, bf16[2,512,256]{2,1,0:T(8,128)(2,1)}, u32[]{:S(2)}, u32[]{:S(2)}) %collective-permute-start.19) | collective-permute-done | bytes 524320 | tf_op jit(solution)/shard_map/ppermute | solution.py:24
  144.3 6.4 %collective-permute-start.13 = (bf16[256,768]{1,0:T(8,128)(2,1)S(1)}, bf16[256,768]{1,0:T(8,128)(2,1)S(1)}, u32[]{:S(2)}, u32[]{:S(2)}) collective-permute-start(bf16[256,768]{1,0:T(8,128)(2,1)S(1)} %copy-done.12), channel_id=1, source_target_pairs={{0,8},{8,0},{16,24},{24,16},{32,40},{40,32},{48,56},{56,48},{64,72... | collective-permute-start | bytes 1179656 | tf_op jit(solution)/shard_map/ppermute | solution.py:24
  151.3 5.5 %collective-permute-done.20 = bf16[2,512,256]{2,1,0:T(8,128)(2,1)} collective-permute-done((bf16[2,512,256]{2,1,0:T(8,128)(2,1)}, bf16[2,512,256]{2,1,0:T(8,128)(2,1)}, u32[]{:S(2)}, u32[]{:S(2)}) %collective-permute-start.20) | collective-permute-done | bytes 524320 | tf_op jit(solution)/shard_map/ppermute | solution.py:24
  158.2 7.3 %collective-permute-done.21 = bf16[512,256]{1,0:T(8,128)(2,1)S(1)} collective-permute-done((bf16[512,256]{1,0:T(8,128)(2,1)S(1)}, bf16[512,256]{1,0:T(8,128)(2,1)S(1)}, u32[]{:S(2)}, u32[]{:S(2)}) %collective-permute-start.21) | collective-permute-done | bytes 262176 | tf_op jit(solution)/shard_map/ppermute | solution.py:24
  166.9 7.8 %collective-permute-start.24 = (bf16[512,256]{1,0:T(8,128)(2,1)S(1)}, bf16[512,256]{1,0:T(8,128)(2,1)S(1)}, u32[]{:S(2)}, u32[]{:S(2)}) collective-permute-start(bf16[512,256]{1,0:T(8,128)(2,1)S(1)} %get-tuple-element.71), channel_id=1, source_target_pairs={{0,8},{8,0},{16,24},{24,16},{32,40},{40,32},{48,56},{56,48},{64,72... | collective-permute-start | bytes 786440 | tf_op jit(solution)/shard_map/ppermute | solution.py:24
  176.0 3.5 %shard_map.59 = bf16[32,16,512]{2,1,0:T(8,128)(2,1)} custom-call(bf16[512,256]{1,0:T(8,128)(2,1)S(1)} %get-tuple-element.92.g0_ref, bf16[512,256]{1,0:T(8,128)(2,1)S(1)} %get-tuple-element.91.g1_ref), custom_call_target="tpu_custom_call" | custom-call | tf_op jit(solution)/shard_map/pallas_call | solution.py:269
  179.5 4.7 %all-to-all-start = ((bf16[32,16,512]{2,1,0:T(8,128)(2,1)}), bf16[32,16,512]{2,1,0:T(8,128)(2,1)S(1)}, u32[]{:S(2)}, u32[]{:S(2)}) async-start(bf16[32,16,512]{2,1,0:T(8,128)(2,1)} %shard_map.59), calls=%async_computation | async-start | bytes 1048576 | tf_op jit(solution)/shard_map/all_to_all | solution.py:410
  185.6 15.2 %collective-permute-done.25 = bf16[256,384]{1,0:T(8,128)(2,1)S(1)} collective-permute-done((bf16[256,384]{1,0:T(8,128)(2,1)S(1)}, bf16[256,384]{1,0:T(8,128)(2,1)S(1)}, u32[]{:S(2)}, u32[]{:S(2)}) %collective-permute-start.25) | collective-permute-done | bytes 196640 | tf_op jit(solution)/shard_map/ppermute | solution.py:390
  (101 shorter events, 48.0 us)
Async XLA Ops:
  7.2 177.2 %reduce-scatter.2.cloned.1.call-start = ((), (), s32[]{:S(2)}) async-start(), calls=%async_computation.2 | async-start | bytes 1966080 | tf_op jit(solution)/shard_map/reduce_scatter | solution.py:386
  13.6 9.2 %collective-permute-start.2 = (bf16[6,32,512]{2,1,0:T(8,128)(2,1)S(1)}, bf16[6,32,512]{2,1,0:T(8,128)(2,1)S(1)}, u32[]{:S(2)}, u32[]{:S(2)}) collective-permute-start(bf16[6,32,512]{2,1,0:T(8,128)(2,1)S(1)} %fusion.5), channel_id=1, source_target_pairs={{0,64},{8,200},{16,80},{24,216},{32,96},{40,232},{48,112},{56,248}... | collective-permute-start | bytes 589832 | tf_op jit(solution)/shard_map/ppermute | solution.py:24
  21.6 10.1 %collective-permute-start.6 = (bf16[256,768]{1,0:T(8,128)(2,1)}, bf16[256,768]{1,0:T(8,128)(2,1)}, u32[]{:S(2)}, u32[]{:S(2)}) collective-permute-start(bf16[256,768]{1,0:T(8,128)(2,1)} %pad_maximum_fusion.7), channel_id=1, source_target_pairs={{0,8},{8,0},{16,24},{24,16},{32,40},{40,32},{48,56},{56,48},{64,72... | collective-permute-start | bytes 1179656 | tf_op jit(solution)/shard_map/ppermute | solution.py:24
  23.5 12.0 %collective-permute-start.4 = (bf16[2,6,32,512]{3,2,1,0:T(8,128)(2,1)S(1)}, bf16[2,6,32,512]{3,2,1,0:T(8,128)(2,1)}, u32[]{:S(2)}, u32[]{:S(2)}) collective-permute-start(bf16[2,6,32,512]{3,2,1,0:T(8,128)(2,1)S(1)} %pad_maximum_fusion.5), channel_id=1, source_target_pairs={{0,192},{8,72},{16,208},{24,88},{32,224},{40,104},{48,240},{56,120... | collective-permute-start | bytes 1179656 | tf_op jit(solution)/shard_map/ppermute | solution.py:24
  25.9 38.1 %collective-permute-start = (bf16[256,3072]{0,1:T(8,128)(2,1)S(1)}, bf16[256,3072]{0,1:T(8,128)(2,1)}, u32[]{:S(2)}, u32[]{:S(2)}) collective-permute-start(bf16[256,3072]{0,1:T(8,128)(2,1)S(1)} %copy.7), channel_id=1, source_target_pairs={{0,8},{8,0},{16,24},{24,16},{32,40},{40,32},{48,56},{56,48},{64,72... | collective-permute-start | bytes 4718600 | tf_op jit(solution)/shard_map/ppermute | solution.py:24
  37.8 22.6 %collective-permute-start.7 = (bf16[4,6,32,512]{3,2,1,0:T(8,128)(2,1)S(1)}, bf16[4,6,32,512]{3,2,1,0:T(8,128)(2,1)}, u32[]{:S(2)}, u32[]{:S(2)}) collective-permute-start(bf16[4,6,32,512]{3,2,1,0:T(8,128)(2,1)S(1)} %pad_maximum_fusion.1.refs_5_), channel_id=1, source_target_pairs={{0,16},{8,56},{16,0},{24,40},{32,48},{40,24},{48,32},{56,8},{64,80... | collective-permute-start | bytes 2359304 | tf_op jit(solution)/shard_map/ppermute | solution.py:24
  40.8 19.6 %collective-permute-start.9 = (bf16[4,6,32,512]{3,2,1,0:T(8,128)(2,1)S(1)}, bf16[4,6,32,512]{3,2,1,0:T(8,128)(2,1)S(1)}, u32[]{:S(2)}, u32[]{:S(2)}) collective-permute-start(bf16[4,6,32,512]{3,2,1,0:T(8,128)(2,1)S(1)} %pad_maximum_fusion.1.refs_5_), channel_id=1, source_target_pairs={{0,48},{8,24},{16,32},{24,8},{32,16},{40,56},{48,0},{56,40},{64,11... | collective-permute-start | bytes 2359304 | tf_op jit(solution)/shard_map/ppermute | solution.py:24
  40.8 15.9 %collective-permute-start.10 = (bf16[4,6,32,256]{3,2,1,0:T(8,128)(2,1)S(1)}, bf16[4,6,32,256]{3,2,1,0:T(8,128)(2,1)S(1)}, u32[]{:S(2)}, u32[]{:S(2)}) collective-permute-start(bf16[4,6,32,256]{3,2,1,0:T(8,128)(2,1)S(1)} %pad_maximum_fusion.8.refs_9_), channel_id=1, source_target_pairs={{0,192},{8,72},{16,208},{24,88},{32,224},{40,104},{48,240},{56,120... | collective-permute-start | bytes 1179656 | tf_op jit(solution)/shard_map/ppermute | solution.py:24
  42.4 18.0 %collective-permute-start.8 = (bf16[4,6,32,256]{3,2,1,0:T(8,128)(2,1)S(1)}, bf16[4,6,32,256]{3,2,1,0:T(8,128)(2,1)}, u32[]{:S(2)}, u32[]{:S(2)}) collective-permute-start(bf16[4,6,32,256]{3,2,1,0:T(8,128)(2,1)S(1)} %pad_maximum_fusion.8.refs_9_), channel_id=1, source_target_pairs={{0,64},{8,200},{16,80},{24,216},{32,96},{40,232},{48,112},{56,248}... | collective-permute-start | bytes 1179656 | tf_op jit(solution)/shard_map/ppermute | solution.py:24
  61.3 12.0 %collective-permute-start.11 = (bf16[4,6,32,512]{3,2,1,0:T(8,128)(2,1)}, bf16[4,6,32,512]{3,2,1,0:T(8,128)(2,1)}, u32[]{:S(2)}, u32[]{:S(2)}) collective-permute-start(bf16[4,6,32,512]{3,2,1,0:T(8,128)(2,1)} %collective-permute-done.7.refs_6_), channel_id=1, source_target_pairs={{0,48},{8,24},{16,32},{24,8},{32,16},{40,56},{48,0},{56,40},{64,11... | collective-permute-start | bytes 2359304 | tf_op jit(solution)/shard_map/ppermute | solution.py:24
  63.9 8.9 %collective-permute-start.12 = (bf16[4,6,32,256]{3,2,1,0:T(8,128)(2,1)}, bf16[4,6,32,256]{3,2,1,0:T(8,128)(2,1)}, u32[]{:S(2)}, u32[]{:S(2)}) collective-permute-start(bf16[4,6,32,256]{3,2,1,0:T(8,128)(2,1)} %collective-permute-done.8.refs_10_), channel_id=1, source_target_pairs={{0,192},{8,72},{16,208},{24,88},{32,224},{40,104},{48,240},{56,120... | collective-permute-start | bytes 1179656 | tf_op jit(solution)/shard_map/ppermute | solution.py:24
  92.3 10.1 %collective-permute-start.17 = (bf16[8,256,384]{2,1,0:T(8,128)(2,1)}, bf16[8,256,384]{2,1,0:T(8,128)(2,1)}, u32[]{:S(2)}, u32[]{:S(2)}) collective-permute-start(bf16[8,256,384]{2,1,0:T(8,128)(2,1)} %get-tuple-element.58), channel_id=1, source_target_pairs={{0,8},{8,0},{16,24},{24,16},{32,40},{40,32},{48,56},{56,48},{64,72... | collective-permute-start | bytes 4718600 | tf_op jit(solution)/shard_map/ppermute | solution.py:24
  97.6 11.5 %collective-permute-start.14 = (bf16[3,512,256]{2,1,0:T(8,128)(2,1)}, bf16[3,512,256]{2,1,0:T(8,128)(2,1)}, u32[]{:S(2)}, u32[]{:S(2)}) collective-permute-start(bf16[3,512,256]{2,1,0:T(8,128)(2,1)} %get-tuple-element.54), channel_id=1, source_target_pairs={{0,48},{8,24},{16,32},{24,8},{32,16},{40,56},{48,0},{56,40},{64,11... | collective-permute-start | bytes 2359304 | tf_op jit(solution)/shard_map/ppermute | solution.py:24
  97.7 19.7 %collective-permute-start.15 = (bf16[3,512,256]{2,1,0:T(8,128)(2,1)}, bf16[3,512,256]{2,1,0:T(8,128)(2,1)S(1)}, u32[]{:S(2)}, u32[]{:S(2)}) collective-permute-start(bf16[3,512,256]{2,1,0:T(8,128)(2,1)} %get-tuple-element.55), channel_id=1, source_target_pairs={{0,48},{8,24},{16,32},{24,8},{32,16},{40,56},{48,0},{56,40},{64,11... | collective-permute-start | bytes 2359304 | tf_op jit(solution)/shard_map/ppermute | solution.py:24
  99.0 20.1 %collective-permute-start.16 = (bf16[3,512,256]{2,1,0:T(8,128)(2,1)}, bf16[3,512,256]{2,1,0:T(8,128)(2,1)S(1)}, u32[]{:S(2)}, u32[]{:S(2)}) collective-permute-start(bf16[3,512,256]{2,1,0:T(8,128)(2,1)} %get-tuple-element.56), channel_id=1, source_target_pairs={{0,192},{8,72},{16,208},{24,88},{32,224},{40,104},{48,240},{56,120... | collective-permute-start | bytes 2359304 | tf_op jit(solution)/shard_map/ppermute | solution.py:24
  121.3 18.8 %collective-permute-start.18 = (bf16[3,512,256]{2,1,0:T(8,128)(2,1)}, bf16[3,512,256]{2,1,0:T(8,128)(2,1)}, u32[]{:S(2)}, u32[]{:S(2)}) collective-permute-start(bf16[3,512,256]{2,1,0:T(8,128)(2,1)} %add_convert_fusion.1), channel_id=1, source_target_pairs={{0,16},{8,56},{16,0},{24,40},{32,48},{40,24},{48,32},{56,8},{64,80... | collective-permute-start | bytes 2359304 | tf_op jit(solution)/shard_map/ppermute | solution.py:24
  123.1 17.0 %collective-permute-start.19 = (bf16[2,512,256]{2,1,0:T(8,128)(2,1)S(1)}, bf16[2,512,256]{2,1,0:T(8,128)(2,1)}, u32[]{:S(2)}, u32[]{:S(2)}) collective-permute-start(bf16[2,512,256]{2,1,0:T(8,128)(2,1)S(1)} %add_convert_fusion.2), channel_id=1, source_target_pairs={{0,64},{8,200},{16,80},{24,216},{32,96},{40,232},{48,112},{56,248}... | collective-permute-start | bytes 1572872 | tf_op jit(solution)/shard_map/ppermute | solution.py:24
  142.4 14.4 %collective-permute-start.20 = (bf16[2,512,256]{2,1,0:T(8,128)(2,1)}, bf16[2,512,256]{2,1,0:T(8,128)(2,1)}, u32[]{:S(2)}, u32[]{:S(2)}) collective-permute-start(bf16[2,512,256]{2,1,0:T(8,128)(2,1)} %pad_maximum_fusion.4), channel_id=1, source_target_pairs={{0,192},{8,72},{16,208},{24,88},{32,224},{40,104},{48,240},{56,120... | collective-permute-start | bytes 1572872 | tf_op jit(solution)/shard_map/ppermute | solution.py:24
  144.3 13.9 %collective-permute-start.13 = (bf16[256,768]{1,0:T(8,128)(2,1)S(1)}, bf16[256,768]{1,0:T(8,128)(2,1)S(1)}, u32[]{:S(2)}, u32[]{:S(2)}) collective-permute-start(bf16[256,768]{1,0:T(8,128)(2,1)S(1)} %copy-done.12), channel_id=1, source_target_pairs={{0,8},{8,0},{16,24},{24,16},{32,40},{40,32},{48,56},{56,48},{64,72... | collective-permute-start | bytes 1179656 | tf_op jit(solution)/shard_map/ppermute | solution.py:24
  150.7 7.5 %collective-permute-start.23 = (bf16[512,256]{1,0:T(8,128)(2,1)S(1)}, bf16[512,256]{1,0:T(8,128)(2,1)S(1)}, u32[]{:S(2)}, u32[]{:S(2)}) collective-permute-start(bf16[512,256]{1,0:T(8,128)(2,1)S(1)} %fusion), channel_id=1, source_target_pairs={{0,16},{8,56},{16,0},{24,40},{32,48},{40,24},{48,32},{56,8},{64,80... | collective-permute-start | bytes 786440 | tf_op jit(solution)/shard_map/ppermute | solution.py:24
  158.0 7.5 %collective-permute-start.21 = (bf16[512,256]{1,0:T(8,128)(2,1)S(1)}, bf16[512,256]{1,0:T(8,128)(2,1)S(1)}, u32[]{:S(2)}, u32[]{:S(2)}) collective-permute-start(bf16[512,256]{1,0:T(8,128)(2,1)S(1)} %fusion.3), channel_id=1, source_target_pairs={{0,64},{8,200},{16,80},{24,216},{32,96},{40,232},{48,112},{56,248}... | collective-permute-start | bytes 786440 | tf_op jit(solution)/shard_map/ppermute | solution.py:24
  166.9 8.9 %collective-permute-start.24 = (bf16[512,256]{1,0:T(8,128)(2,1)S(1)}, bf16[512,256]{1,0:T(8,128)(2,1)S(1)}, u32[]{:S(2)}, u32[]{:S(2)}) collective-permute-start(bf16[512,256]{1,0:T(8,128)(2,1)S(1)} %get-tuple-element.71), channel_id=1, source_target_pairs={{0,8},{8,0},{16,24},{24,16},{32,40},{40,32},{48,56},{56,48},{64,72... | collective-permute-start | bytes 786440 | tf_op jit(solution)/shard_map/ppermute | solution.py:24
  179.5 23.1 %all-to-all-start = ((bf16[32,16,512]{2,1,0:T(8,128)(2,1)}), bf16[32,16,512]{2,1,0:T(8,128)(2,1)S(1)}, u32[]{:S(2)}, u32[]{:S(2)}) async-start(bf16[32,16,512]{2,1,0:T(8,128)(2,1)} %shard_map.59), calls=%async_computation | async-start | bytes 1048576 | tf_op jit(solution)/shard_map/all_to_all | solution.py:410
  185.4 15.5 %collective-permute-start.25 = (bf16[256,384]{1,0:T(8,128)(2,1)S(1)}, bf16[256,384]{1,0:T(8,128)(2,1)S(1)}, u32[]{:S(2)}, u32[]{:S(2)}) collective-permute-start(bf16[256,384]{1,0:T(8,128)(2,1)S(1)} %select_bitcast_fusion), channel_id=1, source_target_pairs={{0,1},{1,0},{2,3},{3,2},{4,5},{5,4},{6,7},{7,6},{8,9},{9,8},{10,11... | collective-permute-start | bytes 589832 | tf_op jit(solution)/shard_map/ppermute | solution.py:390
  (18 other events, 212.0 us)
Sparse Core Ops, SparseCore 0:
  127.9 24.8 reduce-scatter.1
